TPU v7x, 256 devices: a whole 4x4x8 slice. The times are simulated.
256 devices in a mesh: island: 4 (over z_hi), fsdp: 64 (over y, z_lo, x, core).
Axes of the slice: x: 4, y: 4, z: 8 (z_hi: 4, z_lo: 2; z = z_hi * 2 + z_lo), core: 2. Of those that a mesh axis runs over, the one named last changes fastest.
Arguments:
- params: float32 [18432, 7168], P(('island', 'fsdp')), as said below
- momentum: float32 [18432, 7168], P(('island', 'fsdp')), as said below
- payload: bfloat16 [18432, 7168], P(('island', 'fsdp')), may hold values from -1 to 1, as said below
- scales: float32 [18432, 56], P(('island', 'fsdp')), may hold values from 0 to 1, as said below
- bounds: int32 [4, 65], replicated, may hold values from 0 to 3072, as said below
Outputs:
- params_out: float32 [18432, 7168], P(('island', 'fsdp'))
- momentum_out: float32 [18432, 7168], P(('island', 'fsdp'))
- mean_payload: bfloat16 [18432, 7168], P(('island', 'fsdp'))
- mean_scales: float32 [18432, 56], P(('island', 'fsdp'))
Inputs may be any that keep to these rules, and one draw needn't show every extreme that they name: `bounds`: row i lists the first global row of each of island i's shards and then the end; entry j lies within 12 of j * 48, entry 0 is 0 and the last is 3072; every island has a shard of exactly 72 rows. `payload`: slots outside a device's shard hold zeros. `scales`: slots outside a device's shard hold zeros. `params`: every island holds the same global rows; slots outside a device's shard hold zeros. `momentum`: every island holds the same global rows; slots outside a device's shard hold zeros.
All inputs are finite; a program needn't handle non-finite values. Where the computation divides by a largest or mean magnitude, that divisor is 1e-20 or more.
Results may differ from a plain program's by a relative error of at most 0.017.
Values may be sent and summed in bfloat16 or wider, within the bound.
No kernel may reach another device: no remote copies, remote signals or barrier semaphores. Data moves between devices by JAX's collectives and lax.ppermute only.
A program may use at most 64 MiB of HBM per device.

v0:
```python
import jax
import jax.numpy as jnp
from jax import lax
from jax.sharding import PartitionSpec as P

ROWS_DEV = 48
HALF = 12


momentum_keep = 0.9
outer_rate = 0.7
block_eps = 1e-06


def with_halo(shard, sides, width):
    for axis, dim in sides:
        count, length = (lax.axis_size(axis), shard.shape[dim])
        up = [(i, (i + 1) % count) for i in range(count - 1)]
        down = [(j, i) for i, j in up]
        last = lax.slice_in_dim(shard, length - width, length, axis=dim)
        initial = lax.slice_in_dim(shard, 0, width, axis=dim)
        before = lax.ppermute(last, axis, up)
        after = lax.ppermute(initial, axis, down)
        shard = jnp.concatenate([before, shard, after], axis=dim)
    return shard


def shortened(shard):
    return jax.tree.map(lambda a: a.astype(jnp.bfloat16) if a.dtype == jnp.float32 else a, shard)


def passed_along(value, axis, steps):
    count = lax.axis_size(axis)
    pairs = [(source, (source + steps) % count) for source in range(count)]
    return lax.ppermute(value, axis, pairs)


def dequantize(coded, block_scale):
    rows, width = coded.shape
    count = block_scale.shape[1]
    blocks = coded.astype(jnp.float32).reshape(rows, count, width // count)
    return (blocks * block_scale[:, :, None]).reshape(rows, width)


def requantize(summed, count):
    rows, width = summed.shape
    blocks = summed.reshape(rows, count, width // count)
    block_scale = jnp.max(jnp.abs(blocks), axis=2) + block_eps
    coded = (blocks / block_scale[:, :, None]).astype(jnp.bfloat16).reshape(rows, width)
    return (coded, block_scale)


def add_rims(centre, left_rim, right_rim):
    spare = centre.shape[0] - left_rim.shape[0]
    return (
        centre + jnp.pad(left_rim, ((0, spare), (0, 0))) + jnp.pad(right_rim, ((spare, 0), (0, 0)))
    )


def realign_pair(pair, live_col, rim_rows):
    codes_in, scales_in = pair
    slots = codes_in.shape[0]
    padded_codes, padded_scales = (
        with_halo(codes_in, (("fsdp", 0),), rim_rows),
        with_halo(shortened(scales_in), (("fsdp", 0),), rim_rows).astype(scales_in.dtype),
    )
    codes_out = add_rims(
        padded_codes[rim_rows : rim_rows + slots],
        padded_codes[:rim_rows],
        padded_codes[rim_rows + slots :],
    )
    scales_out = add_rims(
        padded_scales[rim_rows : rim_rows + slots],
        padded_scales[:rim_rows],
        padded_scales[rim_rows + slots :],
    )
    return (codes_out * live_col.astype(jnp.bfloat16), scales_out * live_col)


def shards(params, momentum, payload, scales, bounds):
    slots, width = payload.shape
    count = scales.shape[1]
    island_count = lax.axis_size("island")
    island_pos = lax.axis_index("island")
    shard_pos = lax.axis_index("fsdp")
    shard_start = bounds[island_pos, shard_pos]
    shard_stop = bounds[island_pos, shard_pos + 1]
    global_row = shard_pos * ROWS_DEV - HALF + jnp.arange(slots, dtype=jnp.int32)
    live_col = ((global_row >= shard_start) & (global_row < shard_stop)).astype(jnp.float32)[
        :, None
    ]
    live_codes = payload * live_col.astype(jnp.bfloat16)
    live_scales = scales * live_col
    summed = dequantize(live_codes, live_scales)
    moving = (live_codes, live_scales)
    for hop_number in range(island_count - 1):
        arrived = passed_along((moving[0], shortened(moving[1])), "island", 1)
        moving = realign_pair(arrived, live_col, 2 * HALF)
        summed = summed + dequantize(moving[0], moving[1])
    coded, block_scale = requantize(summed, count)
    new_scales = block_scale * live_col
    delta = dequantize(coded, new_scales) / island_count
    momentum_out = momentum_keep * momentum + delta
    params_out = params - outer_rate * (delta + momentum_keep * momentum_out)
    return (params_out, momentum_out, coded, new_scales)


def solution(mesh):
    in_specs = (
        P(("island", "fsdp"), None),
        P(("island", "fsdp"), None),
        P(("island", "fsdp"), None),
        P(("island", "fsdp"), None),
        P(),
    )
    out_specs = (
        P(("island", "fsdp"), None),
        P(("island", "fsdp"), None),
        P(("island", "fsdp"), None),
        P(("island", "fsdp"), None),
    )
    return jax.shard_map(shards, mesh=mesh, in_specs=in_specs, out_specs=out_specs, check_vma=False)
```

profile of v0, /device:TPU:8, one launch (start us, length us, event | category | flops | bytes accessed | tf_op | source)
XLA Modules:
  0.0 234.5 jit_solution(8312513944749763881)
XLA Ops:
  0.6 1.4 fusion.17
  2.0 1.3 fusion.9
  3.3 1.4 broadcast_multiply_fusion
  4.7 3.3 %collective-permute-start = (bf16[72,7168]{1,0:T(8,128)(2,1)S(1)}, bf16[72,7168]{1,0:T(8,128)(2,1)S(1)}, u32[]{:S(2)}, u32[]{:S(2)}) collective-permute-start(bf16[72,7168]{1,0:T(8,128)(2,1)S(1)} %broadcast_multiply_fusion), channel_id=1, source_target_pairs={{0,64},{64,128},{128,192},{192,0},{1,65},{65,129},{129,193},{193,1... | collective-permute-start | bytes 3096584 | tf_op jit(solution)/shard_map/ppermute | solution.py:35
  8.0 34.5 %collective-permute-done = bf16[72,7168]{1,0:T(8,128)(2,1)S(1)} collective-permute-done((bf16[72,7168]{1,0:T(8,128)(2,1)S(1)}, bf16[72,7168]{1,0:T(8,128)(2,1)S(1)}, u32[]{:S(2)}, u32[]{:S(2)}) %collective-permute-start) | collective-permute-done | bytes 1032224 | tf_op jit(solution)/shard_map/ppermute | solution.py:35
  42.5 1.9 collective-permute-start.1
  44.4 0.0 copy-start.3
  44.4 17.7 %collective-permute-start.2 = (bf16[24,7168]{1,0:T(8,128)(2,1)S(1)}, bf16[24,7168]{1,0:T(8,128)(2,1)S(1)}, u32[]{:S(2)}, u32[]{:S(2)}) collective-permute-start(bf16[24,7168]{1,0:T(8,128)(2,1)S(1)} %get-tuple-element.22), channel_id=1, source_target_pairs={{1,0},{2,1},{3,2},{4,3},{5,4},{6,5},{7,6},{8,7},{9,8},{10,9},{11,1... | collective-permute-start | bytes 1032200 | tf_op jit(solution)/shard_map/ppermute | solution.py:23
  62.2 3.0 %collective-permute-done.1 = bf16[24,7168]{1,0:T(8,128)(2,1)S(1)} collective-permute-done((bf16[24,7168]{1,0:T(8,128)(2,1)S(1)}, bf16[24,7168]{1,0:T(8,128)(2,1)S(1)}, u32[]{:S(2)}, u32[]{:S(2)}) %collective-permute-start.1) | collective-permute-done | bytes 344096 | tf_op jit(solution)/shard_map/ppermute | solution.py:22
  65.1 1.8 collective-permute-done.2
  66.9 0.3 add_multiply_fusion.1
  67.2 3.1 %collective-permute-start.6 = (bf16[72,7168]{1,0:T(8,128)(2,1)S(1)}, bf16[72,7168]{1,0:T(8,128)(2,1)S(1)}, u32[]{:S(2)}, u32[]{:S(2)}) collective-permute-start(bf16[72,7168]{1,0:T(8,128)(2,1)S(1)} %add_multiply_fusion.1), channel_id=1, source_target_pairs={{0,64},{64,128},{128,192},{192,0},{1,65},{65,129},{129,193},{193,1... | collective-permute-start | bytes 3096584 | tf_op jit(solution)/shard_map/ppermute | solution.py:35
  70.3 46.4 %collective-permute-done.6 = bf16[72,7168]{1,0:T(8,128)(2,1)S(1)} collective-permute-done((bf16[72,7168]{1,0:T(8,128)(2,1)S(1)}, bf16[72,7168]{1,0:T(8,128)(2,1)S(1)}, u32[]{:S(2)}, u32[]{:S(2)}) %collective-permute-start.6) | collective-permute-done | bytes 1032224 | tf_op jit(solution)/shard_map/ppermute | solution.py:35
  116.8 1.9 collective-permute-start.7
  118.7 6.7 %collective-permute-start.8 = (bf16[24,7168]{1,0:T(8,128)(2,1)S(1)}, bf16[24,7168]{1,0:T(8,128)(2,1)S(1)}, u32[]{:S(2)}, u32[]{:S(2)}) collective-permute-start(bf16[24,7168]{1,0:T(8,128)(2,1)S(1)} %get-tuple-element.20), channel_id=1, source_target_pairs={{1,0},{2,1},{3,2},{4,3},{5,4},{6,5},{7,6},{8,7},{9,8},{10,9},{11,1... | collective-permute-start | bytes 1032200 | tf_op jit(solution)/shard_map/ppermute | solution.py:23
  125.4 0.0 copy-done.3
  125.4 0.1 copy.15
  125.5 2.9 %collective-permute-done.7 = bf16[24,7168]{1,0:T(8,128)(2,1)S(1)} collective-permute-done((bf16[24,7168]{1,0:T(8,128)(2,1)S(1)}, bf16[24,7168]{1,0:T(8,128)(2,1)S(1)}, u32[]{:S(2)}, u32[]{:S(2)}) %collective-permute-start.7) | collective-permute-done | bytes 344096 | tf_op jit(solution)/shard_map/ppermute | solution.py:22
  128.4 25.0 %collective-permute-done.8 = bf16[24,7168]{1,0:T(8,128)(2,1)S(1)} collective-permute-done((bf16[24,7168]{1,0:T(8,128)(2,1)S(1)}, bf16[24,7168]{1,0:T(8,128)(2,1)S(1)}, u32[]{:S(2)}, u32[]{:S(2)}) %collective-permute-start.8) | collective-permute-done | bytes 344096 | tf_op jit(solution)/shard_map/ppermute | solution.py:23
  153.4 0.3 add_multiply_fusion
  153.7 0.1 collective-permute-start.12
  153.8 0.1 fusion.10
  153.8 2.4 %collective-permute-start.3 = (bf16[72,56]{1,0:T(8,128)(2,1)S(1)}, bf16[72,56]{1,0:T(8,128)(2,1)S(1)}, u32[]{:S(2)}, u32[]{:S(2)}) collective-permute-start(bf16[72,56]{1,0:T(8,128)(2,1)S(1)} %get-tuple-element.15), channel_id=1, source_target_pairs={{0,64},{64,128},{128,192},{192,0},{1,65},{65,129},{129,193},{193,1... | collective-permute-start | bytes 24200 | tf_op jit(solution)/shard_map/ppermute | solution.py:35
  156.3 16.0 %collective-permute-done.3 = bf16[72,56]{1,0:T(8,128)(2,1)S(1)} collective-permute-done((bf16[72,56]{1,0:T(8,128)(2,1)S(1)}, bf16[72,56]{1,0:T(8,128)(2,1)S(1)}, u32[]{:S(2)}, u32[]{:S(2)}) %collective-permute-start.3) | collective-permute-done | bytes 8096 | tf_op jit(solution)/shard_map/ppermute | solution.py:35
  172.3 1.9 collective-permute-start.4
  174.2 7.9 %collective-permute-start.5 = (bf16[24,56]{1,0:T(8,128)(2,1)S(1)}, bf16[24,56]{1,0:T(8,128)(2,1)S(1)}, u32[]{:S(2)}, u32[]{:S(2)}) collective-permute-start(bf16[24,56]{1,0:T(8,128)(2,1)S(1)} %get-tuple-element.34), channel_id=1, source_target_pairs={{1,0},{2,1},{3,2},{4,3},{5,4},{6,5},{7,6},{8,7},{9,8},{10,9},{11,1... | collective-permute-start | bytes 8072 | tf_op jit(solution)/shard_map/ppermute | solution.py:23
  182.2 0.0 collective-permute-done.4
  182.2 1.3 collective-permute-done.5
  183.5 0.1 convert_multiply_fusion.2
  183.6 2.2 collective-permute-start.9
  185.7 3.7 %collective-permute-done.9 = bf16[72,56]{1,0:T(8,128)(2,1)S(1)} collective-permute-done((bf16[72,56]{1,0:T(8,128)(2,1)S(1)}, bf16[72,56]{1,0:T(8,128)(2,1)S(1)}, u32[]{:S(2)}, u32[]{:S(2)}) %collective-permute-start.9) | collective-permute-done | bytes 8096 | tf_op jit(solution)/shard_map/ppermute | solution.py:35
  189.5 1.9 collective-permute-start.10
  191.4 6.7 %collective-permute-start.11 = (bf16[24,56]{1,0:T(8,128)(2,1)S(1)}, bf16[24,56]{1,0:T(8,128)(2,1)S(1)}, u32[]{:S(2)}, u32[]{:S(2)}) collective-permute-start(bf16[24,56]{1,0:T(8,128)(2,1)S(1)} %get-tuple-element.32), channel_id=1, source_target_pairs={{1,0},{2,1},{3,2},{4,3},{5,4},{6,5},{7,6},{8,7},{9,8},{10,9},{11,1... | collective-permute-start | bytes 8072 | tf_op jit(solution)/shard_map/ppermute | solution.py:23
  198.1 0.0 collective-permute-done.10
  198.1 1.3 collective-permute-done.11
  199.4 0.1 convert_multiply_fusion.1
  199.5 1.0 collective-permute-start.15
  200.4 0.0 collective-permute-done.12
  200.5 1.9 collective-permute-start.13
  202.4 6.7 %collective-permute-start.14 = (bf16[24,7168]{1,0:T(8,128)(2,1)S(1)}, bf16[24,7168]{1,0:T(8,128)(2,1)S(1)}, u32[]{:S(2)}, u32[]{:S(2)}) collective-permute-start(bf16[24,7168]{1,0:T(8,128)(2,1)S(1)} %get-tuple-element.18), channel_id=1, source_target_pairs={{1,0},{2,1},{3,2},{4,3},{5,4},{6,5},{7,6},{8,7},{9,8},{10,9},{11,1... | collective-permute-start | bytes 1032200 | tf_op jit(solution)/shard_map/ppermute | solution.py:23
  209.1 0.0 collective-permute-done.15
  209.1 1.9 collective-permute-start.16
  211.0 6.8 %collective-permute-start.17 = (bf16[24,56]{1,0:T(8,128)(2,1)S(1)}, bf16[24,56]{1,0:T(8,128)(2,1)S(1)}, u32[]{:S(2)}, u32[]{:S(2)}) collective-permute-start(bf16[24,56]{1,0:T(8,128)(2,1)S(1)} %get-tuple-element.30), channel_id=1, source_target_pairs={{1,0},{2,1},{3,2},{4,3},{5,4},{6,5},{7,6},{8,7},{9,8},{10,9},{11,1... | collective-permute-start | bytes 8072 | tf_op jit(solution)/shard_map/ppermute | solution.py:23
  217.8 0.0 collective-permute-done.16
  217.9 1.1 collective-permute-done.17
  219.0 0.1 convert_multiply_fusion
  219.1 0.0 collective-permute-done.13
  219.1 0.0 collective-permute-done.14
  219.1 0.6 mul.152
  219.7 0.6 mul.147
  220.3 0.0 copy-start
  220.3 0.6 mul.142
  220.9 0.6 mul.137
  221.5 0.0 copy-done
  221.5 2.5 %abs_bitcast_fusion = (f32[9,8,56,128]{3,1,2,0:T(8,128)S(1)}, f32[72,7168]{1,0:T(8,128)S(1)}) fusion(f32[9,8,56,128]{3,2,1,0:T(8,128)S(1)} %bitcast.49, bf16[24,7168]{1,0:T(8,128)(2,1)S(1)} %collective-permute-done.14, bf16[72,7168]{1,0:T(8,128)(2,1)S(1)} %collective-permute-done.12, bf16[24,7168]{1,0:T(8,128)(2,1)S(1)} %collective-permute-done.13, ...), kind=kLoop, calls=%fused_computation.13 | loop fusion | flops 10838016 | bytes 17203344
  224.0 1.7 copy.21
  225.7 2.2 reduce_max.9
  227.8 0.1 broadcast_add_fusion
  227.9 0.7 copy.16
  228.6 0.6 mul.156
  229.2 0.6 div.17
  229.8 0.4 copy-done.1
  230.2 0.6 copy-done.2
  230.8 3.7 %multiply_subtract_fusion = (f32[72,7168]{1,0:T(8,128)}, f32[72,7168]{1,0:T(8,128)}, bf16[72,7168]{1,0:T(8,128)(2,1)}) fusion(f32[72,7168]{1,0:T(8,128)S(1)} %copy-done.1, f32[9,8,56,128]{3,2,1,0:T(8,128)S(1)} %bitcast.53, f32[72,7168]{1,0:T(8,128)S(1)} %copy-done.2, f32[72,7168]{1,0:T(8,128)S(1)} %get-tuple-element.12, f32[9,8,56,128]{3,2,1,0:T(8,128)S(1)} %bitcast.54), kind=kLoop, calls=%fused_computation.11 | loop fusion | flops 5677056 | bytes 15482880 | tf_op jit(solution)/shard_map/sub | solution.py:104
  (8 shorter events, 0.1 us)
Async XLA Ops:
  4.7 37.8 %collective-permute-start = (bf16[72,7168]{1,0:T(8,128)(2,1)S(1)}, bf16[72,7168]{1,0:T(8,128)(2,1)S(1)}, u32[]{:S(2)}, u32[]{:S(2)}) collective-permute-start(bf16[72,7168]{1,0:T(8,128)(2,1)S(1)} %broadcast_multiply_fusion), channel_id=1, source_target_pairs={{0,64},{64,128},{128,192},{192,0},{1,65},{65,129},{129,193},{193,1... | collective-permute-start | bytes 3096584 | tf_op jit(solution)/shard_map/ppermute | solution.py:35
  42.5 22.6 %collective-permute-start.1 = (bf16[24,7168]{1,0:T(8,128)(2,1)S(1)}, bf16[24,7168]{1,0:T(8,128)(2,1)S(1)}, u32[]{:S(2)}, u32[]{:S(2)}) collective-permute-start(bf16[24,7168]{1,0:T(8,128)(2,1)S(1)} %get-tuple-element.21), channel_id=1, source_target_pairs={{0,1},{1,2},{2,3},{3,4},{4,5},{5,6},{6,7},{7,8},{8,9},{9,10},{10,1... | collective-permute-start | bytes 1032200 | tf_op jit(solution)/shard_map/ppermute | solution.py:22
  44.4 80.9 %copy-start.3 = (f32[72,56]{0,1:T(8,128)S(1)}, f32[72,56]{0,1:T(8,128)}, u32[]{:S(2)}) copy-start(f32[72,56]{0,1:T(8,128)} %param.8) | copy-start | bytes 48388
  44.4 22.5 %collective-permute-start.2 = (bf16[24,7168]{1,0:T(8,128)(2,1)S(1)}, bf16[24,7168]{1,0:T(8,128)(2,1)S(1)}, u32[]{:S(2)}, u32[]{:S(2)}) collective-permute-start(bf16[24,7168]{1,0:T(8,128)(2,1)S(1)} %get-tuple-element.22), channel_id=1, source_target_pairs={{1,0},{2,1},{3,2},{4,3},{5,4},{6,5},{7,6},{8,7},{9,8},{10,9},{11,1... | collective-permute-start | bytes 1032200 | tf_op jit(solution)/shard_map/ppermute | solution.py:23
  67.2 49.5 %collective-permute-start.6 = (bf16[72,7168]{1,0:T(8,128)(2,1)S(1)}, bf16[72,7168]{1,0:T(8,128)(2,1)S(1)}, u32[]{:S(2)}, u32[]{:S(2)}) collective-permute-start(bf16[72,7168]{1,0:T(8,128)(2,1)S(1)} %add_multiply_fusion.1), channel_id=1, source_target_pairs={{0,64},{64,128},{128,192},{192,0},{1,65},{65,129},{129,193},{193,1... | collective-permute-start | bytes 3096584 | tf_op jit(solution)/shard_map/ppermute | solution.py:35
  116.8 11.6 %collective-permute-start.7 = (bf16[24,7168]{1,0:T(8,128)(2,1)S(1)}, bf16[24,7168]{1,0:T(8,128)(2,1)S(1)}, u32[]{:S(2)}, u32[]{:S(2)}) collective-permute-start(bf16[24,7168]{1,0:T(8,128)(2,1)S(1)} %get-tuple-element.19), channel_id=1, source_target_pairs={{0,1},{1,2},{2,3},{3,4},{4,5},{5,6},{6,7},{7,8},{8,9},{9,10},{10,1... | collective-permute-start | bytes 1032200 | tf_op jit(solution)/shard_map/ppermute | solution.py:22
  118.7 34.7 %collective-permute-start.8 = (bf16[24,7168]{1,0:T(8,128)(2,1)S(1)}, bf16[24,7168]{1,0:T(8,128)(2,1)S(1)}, u32[]{:S(2)}, u32[]{:S(2)}) collective-permute-start(bf16[24,7168]{1,0:T(8,128)(2,1)S(1)} %get-tuple-element.20), channel_id=1, source_target_pairs={{1,0},{2,1},{3,2},{4,3},{5,4},{6,5},{7,6},{8,7},{9,8},{10,9},{11,1... | collective-permute-start | bytes 1032200 | tf_op jit(solution)/shard_map/ppermute | solution.py:23
  153.7 46.7 %collective-permute-start.12 = (bf16[72,7168]{1,0:T(8,128)(2,1)S(1)}, bf16[72,7168]{1,0:T(8,128)(2,1)S(1)}, u32[]{:S(2)}, u32[]{:S(2)}) collective-permute-start(bf16[72,7168]{1,0:T(8,128)(2,1)S(1)} %add_multiply_fusion), channel_id=1, source_target_pairs={{0,64},{64,128},{128,192},{192,0},{1,65},{65,129},{129,193},{193,1... | collective-permute-start | bytes 3096584 | tf_op jit(solution)/shard_map/ppermute | solution.py:35
  153.8 18.5 %collective-permute-start.3 = (bf16[72,56]{1,0:T(8,128)(2,1)S(1)}, bf16[72,56]{1,0:T(8,128)(2,1)S(1)}, u32[]{:S(2)}, u32[]{:S(2)}) collective-permute-start(bf16[72,56]{1,0:T(8,128)(2,1)S(1)} %get-tuple-element.15), channel_id=1, source_target_pairs={{0,64},{64,128},{128,192},{192,0},{1,65},{65,129},{129,193},{193,1... | collective-permute-start | bytes 24200 | tf_op jit(solution)/shard_map/ppermute | solution.py:35
  172.3 9.8 %collective-permute-start.4 = (bf16[24,56]{1,0:T(8,128)(2,1)S(1)}, bf16[24,56]{1,0:T(8,128)(2,1)S(1)}, u32[]{:S(2)}, u32[]{:S(2)}) collective-permute-start(bf16[24,56]{1,0:T(8,128)(2,1)S(1)} %get-tuple-element.33), channel_id=1, source_target_pairs={{0,1},{1,2},{2,3},{3,4},{4,5},{5,6},{6,7},{7,8},{8,9},{9,10},{10,1... | collective-permute-start | bytes 8072 | tf_op jit(solution)/shard_map/ppermute | solution.py:22
  174.2 9.2 %collective-permute-start.5 = (bf16[24,56]{1,0:T(8,128)(2,1)S(1)}, bf16[24,56]{1,0:T(8,128)(2,1)S(1)}, u32[]{:S(2)}, u32[]{:S(2)}) collective-permute-start(bf16[24,56]{1,0:T(8,128)(2,1)S(1)} %get-tuple-element.34), channel_id=1, source_target_pairs={{1,0},{2,1},{3,2},{4,3},{5,4},{6,5},{7,6},{8,7},{9,8},{10,9},{11,1... | collective-permute-start | bytes 8072 | tf_op jit(solution)/shard_map/ppermute | solution.py:23
  183.6 5.9 %collective-permute-start.9 = (bf16[72,56]{1,0:T(8,128)(2,1)S(1)}, bf16[72,56]{1,0:T(8,128)(2,1)S(1)}, u32[]{:S(2)}, u32[]{:S(2)}) collective-permute-start(bf16[72,56]{1,0:T(8,128)(2,1)S(1)} %get-tuple-element.26), channel_id=1, source_target_pairs={{0,64},{64,128},{128,192},{192,0},{1,65},{65,129},{129,193},{193,1... | collective-permute-start | bytes 24200 | tf_op jit(solution)/shard_map/ppermute | solution.py:35
  189.5 8.6 %collective-permute-start.10 = (bf16[24,56]{1,0:T(8,128)(2,1)S(1)}, bf16[24,56]{1,0:T(8,128)(2,1)S(1)}, u32[]{:S(2)}, u32[]{:S(2)}) collective-permute-start(bf16[24,56]{1,0:T(8,128)(2,1)S(1)} %get-tuple-element.31), channel_id=1, source_target_pairs={{0,1},{1,2},{2,3},{3,4},{4,5},{5,6},{6,7},{7,8},{8,9},{9,10},{10,1... | collective-permute-start | bytes 8072 | tf_op jit(solution)/shard_map/ppermute | solution.py:22
  191.4 8.0 %collective-permute-start.11 = (bf16[24,56]{1,0:T(8,128)(2,1)S(1)}, bf16[24,56]{1,0:T(8,128)(2,1)S(1)}, u32[]{:S(2)}, u32[]{:S(2)}) collective-permute-start(bf16[24,56]{1,0:T(8,128)(2,1)S(1)} %get-tuple-element.32), channel_id=1, source_target_pairs={{1,0},{2,1},{3,2},{4,3},{5,4},{6,5},{7,6},{8,7},{9,8},{10,9},{11,1... | collective-permute-start | bytes 8072 | tf_op jit(solution)/shard_map/ppermute | solution.py:23
  199.5 9.6 %collective-permute-start.15 = (bf16[72,56]{1,0:T(8,128)(2,1)S(1)}, bf16[72,56]{1,0:T(8,128)(2,1)S(1)}, u32[]{:S(2)}, u32[]{:S(2)}) collective-permute-start(bf16[72,56]{1,0:T(8,128)(2,1)S(1)} %get-tuple-element.28), channel_id=1, source_target_pairs={{0,64},{64,128},{128,192},{192,0},{1,65},{65,129},{129,193},{193,1... | collective-permute-start | bytes 24200 | tf_op jit(solution)/shard_map/ppermute | solution.py:35
  200.5 18.6 %collective-permute-start.13 = (bf16[24,7168]{1,0:T(8,128)(2,1)S(1)}, bf16[24,7168]{1,0:T(8,128)(2,1)S(1)}, u32[]{:S(2)}, u32[]{:S(2)}) collective-permute-start(bf16[24,7168]{1,0:T(8,128)(2,1)S(1)} %get-tuple-element.17), channel_id=1, source_target_pairs={{0,1},{1,2},{2,3},{3,4},{4,5},{5,6},{6,7},{7,8},{8,9},{9,10},{10,1... | collective-permute-start | bytes 1032200 | tf_op jit(solution)/shard_map/ppermute | solution.py:22
  202.4 16.7 %collective-permute-start.14 = (bf16[24,7168]{1,0:T(8,128)(2,1)S(1)}, bf16[24,7168]{1,0:T(8,128)(2,1)S(1)}, u32[]{:S(2)}, u32[]{:S(2)}) collective-permute-start(bf16[24,7168]{1,0:T(8,128)(2,1)S(1)} %get-tuple-element.18), channel_id=1, source_target_pairs={{1,0},{2,1},{3,2},{4,3},{5,4},{6,5},{7,6},{8,7},{9,8},{10,9},{11,1... | collective-permute-start | bytes 1032200 | tf_op jit(solution)/shard_map/ppermute | solution.py:23
  209.1 8.8 %collective-permute-start.16 = (bf16[24,56]{1,0:T(8,128)(2,1)S(1)}, bf16[24,56]{1,0:T(8,128)(2,1)S(1)}, u32[]{:S(2)}, u32[]{:S(2)}) collective-permute-start(bf16[24,56]{1,0:T(8,128)(2,1)S(1)} %get-tuple-element.29), channel_id=1, source_target_pairs={{0,1},{1,2},{2,3},{3,4},{4,5},{5,6},{6,7},{7,8},{8,9},{9,10},{10,1... | collective-permute-start | bytes 8072 | tf_op jit(solution)/shard_map/ppermute | solution.py:22
  211.0 8.0 %collective-permute-start.17 = (bf16[24,56]{1,0:T(8,128)(2,1)S(1)}, bf16[24,56]{1,0:T(8,128)(2,1)S(1)}, u32[]{:S(2)}, u32[]{:S(2)}) collective-permute-start(bf16[24,56]{1,0:T(8,128)(2,1)S(1)} %get-tuple-element.30), channel_id=1, source_target_pairs={{1,0},{2,1},{3,2},{4,3},{5,4},{6,5},{7,6},{8,7},{9,8},{10,9},{11,1... | collective-permute-start | bytes 8072 | tf_op jit(solution)/shard_map/ppermute | solution.py:23
  220.3 1.2 copy-start
  228.6 1.6 copy-start.1
  228.6 2.2 copy-start.2
where the time goes:
time: 237 us; the launch traced here: 235 us
  waiting for transfers between devices  137 us (58%)
  starting transfers between devices  76 us (32%)
  other arithmetic  12 us (5%)
  local copies, waits for them, and re-layouts  8.54 us (4%)
    ppermute x6, waiting for transfers between devices, passed_along(): return lax.ppermute(value, axis, pairs)  101 us
    ppermute x6, starting transfers between devices, with_halo(): after = lax.ppermute(initial, axis, down)  52.4 us
    ppermute x6, waiting for transfers between devices, with_halo(): after = lax.ppermute(initial, axis, down)  30.6 us
    ppermute x6, starting transfers between devices, passed_along(): return lax.ppermute(value, axis, pairs)  12.1 us
    ppermute x6, starting transfers between devices, with_halo(): before = lax.ppermute(last, axis, up)  11.5 us
    ppermute x6, waiting for transfers between devices, with_halo(): before = lax.ppermute(last, axis, up)  5.89 us
  transfers between devices with their start and end apart: 18, of which 11 were waited for; matrix products, arithmetic and copies ran while one was open for 0% of the time, Pallas kernels for 0%

commit v1 on v0

v1 whole, which is shorter than its diff:
```python
import functools

import jax
import jax.numpy as jnp
from jax import lax
from jax.experimental import pallas as pl
from jax.experimental.pallas import tpu as pltpu
from jax.sharding import PartitionSpec as P

ROWS_DEV = 48
HALF = 12
BAND = 24
QB = 128

momentum_keep = 0.9
outer_rate = 0.7
block_eps = 1e-06

F32 = jnp.float32
BF16 = jnp.bfloat16
AXES = ("island", "fsdp")
PAIRINGS = ({0: 1, 1: 0, 2: 3, 3: 2}, {0: 3, 3: 0, 1: 2, 2: 1})


def island_swap(value, step):
    shards = lax.axis_size("fsdp")
    pairs = [
        (i * shards + j, PAIRINGS[(j + step) % 2][i] * shards + j)
        for i in range(4)
        for j in range(shards)
    ]
    return lax.ppermute(value, AXES, pairs)


def inner_swap(value):
    return lax.ppermute(value, "fsdp", [(j, j ^ 1) for j in range(lax.axis_size("fsdp"))])


def outer_swap(value):
    count = lax.axis_size("fsdp")
    pairs = [(j, (j + 1) % count if j & 1 else (j - 1) % count) for j in range(count)]
    return lax.ppermute(value, "fsdp", pairs)


def local_call(body, out_shapes, info, *arrays, cost=1 << 20, **kwargs):
    vmem = pl.BlockSpec(memory_space=pltpu.VMEM)
    return pl.pallas_call(
        body,
        out_shape=out_shapes,
        in_specs=[pl.BlockSpec(memory_space=pltpu.SMEM)] + [vmem] * len(arrays),
        out_specs=jax.tree.map(lambda _: vmem, out_shapes),
        cost_estimate=pl.CostEstimate(flops=cost, bytes_accessed=cost, transcendentals=0),
        **kwargs,
    )(info, *arrays)


def live_rows(info_ref, first, rows, width):
    row = lax.broadcasted_iota(jnp.int32, (rows, width), 0) + first
    return ((row >= info_ref[0]) & (row < info_ref[1])).astype(F32)


def terms_body(info, payload, scales, mid_send, mid_keep, in_send, in_keep, out_send, out_keep):
    half = payload.shape[1] // 2
    blocks = half // QB

    def fill(band, part, target):
        rows = slice(band * BAND, (band + 1) * BAND)
        live_scales = scales[rows, :] * live_rows(info, band * BAND, BAND, scales.shape[1])
        for k in range(blocks):
            g = part * blocks + k
            scale = live_scales[:, g : g + 1]
            block = payload[rows, g * QB : (g + 1) * QB].astype(F32) * scale
            target[:, k * QB : (k + 1) * QB] = block.astype(target.dtype)

    for a in range(2):

        @pl.when(info[2] == a)
        def _(a=a):
            fill(1, 1 - a, mid_send)
            fill(1, a, mid_keep)

    for c in range(2):

        @pl.when(info[4] == c)
        def _(c=c):
            inner, outer = (2, 0) if c == 0 else (0, 2)
            fill(outer, c, out_send)
            fill(outer, 1 - c, out_keep)
            fill(inner, 1 - c, in_send)
            fill(inner, c, in_keep)


def fold_body(info, mid_send, mid_keep, in_keep, in_recv, send, keep):
    wide, narrow = mid_send.shape[1], in_keep.shape[1] // 2
    send[:, :wide] = mid_send[...]
    keep[:, :wide] = mid_keep[...]
    for a in range(2):

        @pl.when(info[2] == a)
        def _(a=a):
            for part, target in ((1 - a, send), (a, keep)):
                cols = slice(part * narrow, (part + 1) * narrow)
                total = in_keep[:, cols] + in_recv[:, cols].astype(F32)
                target[:, wide:] = total.astype(target.dtype)


def fold_outer_body(info, out_keep, out_recv, send, keep):
    width = out_keep.shape[1] // 2
    for a in range(2):

        @pl.when(info[2] == a)
        def _(a=a):
            for part, target in ((1 - a, send), (a, keep)):
                cols = slice(part * width, (part + 1) * width)
                total = out_keep[:, cols] + out_recv[:, cols].astype(F32)
                target[...] = total.astype(target.dtype)


def split_body(pieces, info, keep, recv, send, keep_next):
    for b in range(2):

        @pl.when(info[3] == b)
        def _(b=b):
            at = 0
            for width in pieces:
                half = width // 2
                for part, target in ((1 - b, send), (b, keep_next)):
                    cols = slice(at + part * half, at + (part + 1) * half)
                    total = keep[:, cols] + recv[:, cols].astype(F32)
                    target[:, at // 2 : at // 2 + half] = total.astype(target.dtype)
                at += width


def join_body(pieces, which, info, own, recv, out):
    for b in range(2):

        @pl.when(info[which] == b)
        def _(b=b):
            at = 0
            for width in pieces:
                half = width // 2
                src = slice(at // 2, at // 2 + half)
                for part, source in ((b, own), (1 - b, recv)):
                    out[:, at + part * half : at + (part + 1) * half] = source[:, src]
                at += width


def reduce_band(info, send, keep, pieces):
    rows, width = send.shape
    recv = island_swap(send, 0)
    send, keep = local_call(
        functools.partial(split_body, pieces),
        [
            jax.ShapeDtypeStruct((rows, width // 2), BF16),
            jax.ShapeDtypeStruct((rows, width // 2), F32),
        ],
        info,
        keep,
        recv,
    )
    recv = island_swap(send, 1)
    quarter = (keep + recv.astype(F32)).astype(BF16)
    other = island_swap(quarter, 1)
    return local_call(
        functools.partial(join_body, pieces, 3),
        jax.ShapeDtypeStruct((rows, width), BF16),
        info,
        quarter,
        other,
    )


def step_body(info, own1, recv1, in_mine, in_other, out_mine, out_other, params, momentum,
              params_out, momentum_out, payload_out, scales_out):
    width = params.shape[1]
    half = width // 2
    blocks = half // QB
    a, c = info[2], info[4]
    lane = lax.broadcasted_iota(jnp.int32, (BAND, QB), 1)

    def band(first, source):
        rows = pl.ds(first, BAND)
        live = live_rows(info, first, BAND, QB)
        scale_row = jnp.zeros((BAND, QB), F32)
        for g in range(2 * blocks):
            cols = slice(g * QB, (g + 1) * QB)
            summed = source(g // blocks, slice((g % blocks) * QB, (g % blocks + 1) * QB)).astype(F32)
            block_scale = jnp.max(jnp.abs(summed), axis=1, keepdims=True) + block_eps
            coded = (summed * (1.0 / block_scale)).astype(BF16).astype(F32) * live
            block_live = block_scale * live
            delta = coded * (block_live * 0.25)
            moved = momentum_keep * momentum[rows, cols] + delta
            momentum_out[rows, cols] = moved
            params_out[rows, cols] = params[rows, cols] - outer_rate * (
                delta + momentum_keep * moved
            )
            payload_out[rows, cols] = coded.astype(BF16)
            scale_row = jnp.where(lane == g, block_live, scale_row)
        scales_out[rows, :] = scale_row[:, : 2 * blocks]

    def pick(flag, one, two):
        return lambda part, cols: jnp.where(flag == part, one[:, cols], two[:, cols])

    inner_first = pl.multiple_of((1 - c) * (2 * BAND), 16)
    outer_first = pl.multiple_of(c * (2 * BAND), 16)
    band(BAND, pick(a, own1, recv1))
    band(inner_first, pick(c, in_mine, in_other))
    band(outer_first, pick(1 - c, out_mine, out_other))


def shards(params, momentum, payload, scales, bounds):
    slots, width = payload.shape
    half = width // 2
    island_pos = lax.axis_index("island")
    shard_pos = lax.axis_index("fsdp")
    origin = shard_pos * ROWS_DEV - HALF
    odd = shard_pos & 1
    low, high = island_pos & 1, island_pos >> 1
    bit_a = jnp.where(odd == 0, low ^ high, high)
    bit_b = jnp.where(odd == 0, high, low ^ high)
    info = jnp.stack(
        [
            bounds[island_pos, shard_pos] - origin,
            bounds[island_pos, shard_pos + 1] - origin,
            bit_a,
            bit_b,
            odd,
        ]
    ).astype(jnp.int32)

    def shape(columns, dtype):
        return jax.ShapeDtypeStruct((BAND, columns), dtype)

    mid_send, mid_keep, in_send, in_keep, out_send, out_keep = local_call(
        terms_body, [shape(half, BF16), shape(half, F32)] * 3, info, payload, scales
    )
    out_recv = outer_swap(out_send)
    in_recv = inner_swap(in_send)
    wide = half + half // 2
    send1, keep1 = local_call(
        fold_body, [shape(wide, BF16), shape(wide, F32)], info, mid_send, mid_keep, in_keep, in_recv
    )
    own1 = reduce_band(info, send1, keep1, (half, half // 2))
    send2, keep2 = local_call(
        fold_outer_body, [shape(half // 2, BF16), shape(half // 2, F32)], info, out_keep, out_recv
    )
    own2 = reduce_band(info, send2, keep2, (half // 2,))
    recv2 = island_swap(own2, 0)
    recv1 = island_swap(own1, 0)
    join = functools.partial(join_body, (half,), 2)
    out_mine = local_call(join, shape(half, BF16), info, own2, recv2)
    out_other = outer_swap(out_mine)
    in_mine = local_call(join, shape(half, BF16), info, own1[:, half:], recv1[:, half:])
    in_other = inner_swap(in_mine)
    return local_call(
        step_body,
        [
            jax.ShapeDtypeStruct((slots, width), F32),
            jax.ShapeDtypeStruct((slots, width), F32),
            jax.ShapeDtypeStruct((slots, width), BF16),
            jax.ShapeDtypeStruct((slots, width // QB), F32),
        ],
        info,
        own1[:, :half],
        recv1[:, :half],
        in_mine,
        in_other,
        out_mine,
        out_other,
        params,
        momentum,
        compiler_params=pltpu.CompilerParams(vmem_limit_bytes=40 << 20),
    )


def solution(mesh):
    spec = P(("island", "fsdp"), None)
    return jax.shard_map(
        shards, mesh=mesh, in_specs=(spec,) * 4 + (P(),), out_specs=(spec,) * 4, check_vma=False
    )
```

time: 237 us -> 87.4 us (0.37)
  waiting for transfers between devices: 137 us -> 20.2 us
  starting transfers between devices: 76 us -> 25.2 us
  Pallas kernels: 0 us -> 21.6 us
  other arithmetic: 12 us -> 1.88 us
  local copies, waits for them, and re-layouts: 8.54 us -> 15.2 us
    ppermute x18 -> x12, waiting for transfers between devices: 137 us -> 20.2 us  [the longest x8 17.4 us: island_swap(): return lax.ppermute(value, AXES, pairs)]
    ppermute x18 -> x12, starting transfers between devices: 76 us -> 25.2 us  [the longest x8 17.5 us: island_swap(): return lax.ppermute(value, AXES, pairs)]
    pallas_call x0 -> x10, Pallas kernels: none -> 21.6 us  [local_call(): pl.pallas_call(body, out_shape=out_shapes, in_specs=[pl.BlockSpec(memory_...]
    unnamed x11 -> x29, local copies, waits for them, and re-layouts: 3.47 us -> 9.43 us
    sub x1 -> x0, other arithmetic: 3.71 us -> none  [shards(): params_out = params - outer_rate * (delta + momentum_keep * momentum_out)]
    mul x5 -> x0, local copies, waits for them, and re-layouts: 2.98 us -> none  [dequantize(): return (blocks * block_scale[:, :, None]).reshape(rows, width)]
    slice x6 -> x4, local copies, waits for them, and re-layouts: 0.14 us -> 3.11 us  [the longest x1 1.53 us: shards(): own1[:, half:]]
    unnamed x1 -> x0, other arithmetic: 2.49 us -> none
  transfers between devices with their start and end apart: 18 -> 12, of which waited for: 11 -> 9; matrix products, arithmetic and copies ran while one was open for 0% -> 6% of each run, Pallas kernels for 0% -> 14%
where the time goes in v1:
time: 87.4 us; the launch traced here: 86.2 us
  starting transfers between devices  25.2 us (29%)
  Pallas kernels  21.6 us (25%)
  waiting for transfers between devices  20.2 us (23%)
  local copies, waits for them, and re-layouts  15.2 us (17%)
  between operations  2.03 us (2%)
  other arithmetic  1.88 us (2%)
    pallas_call x10, Pallas kernels, local_call(): pl.pallas_call(body, out_shape=out_shapes, in_specs=[pl.BlockSpec(memory_...  21.6 us
    ppermute x8, starting transfers between devices, island_swap(): return lax.ppermute(value, AXES, pairs)  17.5 us
    ppermute x8, waiting for transfers between devices, island_swap(): return lax.ppermute(value, AXES, pairs)  17.4 us
    unnamed x29, local copies, waits for them, and re-layouts  9.43 us
    ppermute x2, starting transfers between devices, outer_swap(): return lax.ppermute(value, 'fsdp', pairs)  5.59 us
    ppermute x2, starting transfers between devices, inner_swap(): lax.ppermute(value, 'fsdp', [(j, j ^ 1) for j in range(lax.axis_size('fsd...  2.16 us
    convert_element_type x2, other arithmetic, reduce_band(): quarter = (keep + recv.astype(F32)).astype(BF16)  1.88 us
  transfers between devices with their start and end apart: 12, of which 9 were waited for; matrix products, arithmetic and copies ran while one was open for 6% of the time, Pallas kernels for 14%

profile of v1, /device:TPU:8, one launch (start us, length us, event | category | flops | bytes accessed | tf_op | source)
XLA Modules:
  0.0 86.2 jit_solution(6559251791155627657)
XLA Ops:
  0.7 1.4 %fusion = (s32[1,1]{1,0:T(1,128)}, s32[1,1]{1,0:T(1,128)}) fusion(s32[4,65]{1,0:T(4,128)} %param.9, s32[]{:T(128)S(6)} %select_n.17, s32[]{:T(128)S(6)} %select_n.19, s32[]{:T(128)S(6)} %select_n.18), kind=kLoop, calls=%fused_computation.2 | loop fusion | bytes 28 | tf_op jit(solution)/shard_map/dynamic_slice | solution.py:224
  3.3 1.4 %copy.9.scales = f32[72,56]{1,0:T(8,128)} copy(f32[72,56]{0,1:T(8,128)} %param.8) | data formatting | bytes 32256 | tf_op args[3]
  4.8 0.7 stack.23.info
  5.4 3.3 %shard_map.84 = (bf16[24,3584]{1,0:T(8,128)(2,1)}, f32[24,3584]{1,0:T(8,128)}, bf16[24,3584]{1,0:T(8,128)(2,1)}, f32[24,3584]{1,0:T(8,128)}, bf16[24,3584]{1,0:T(8,128)(2,1)}, /*index=5*/f32[24,3584]{1,0:T(8,128)}) custom-call(s32[5]{0:T(128)} %stack.23.info, bf16[72,7168]{1,0:T(8,128)(2,1)} %payload.1, f32[72,56]{1,0:T(8,128)} %copy.9.scales), custom_call_target="tpu_custom_call" | custom-call | flops 1048576 | bytes 1048576 | tf_op jit(solution)/shard_map/pallas_call | solution.py:47
  8.7 0.0 collective-permute-start
  8.7 1.6 %collective-permute-done.in_recv = bf16[24,3584]{1,0:T(8,128)(2,1)S(1)} collective-permute-done((bf16[24,3584]{1,0:T(8,128)(2,1)}, bf16[24,3584]{1,0:T(8,128)(2,1)S(1)}, u32[]{:S(2)}, u32[]{:S(2)}) %collective-permute-start) | collective-permute-done | bytes 172064 | tf_op jit(solution)/shard_map/ppermute | solution.py:36
  10.3 0.0 copy-start.7
  10.3 0.7 copy-done.7
  11.0 2.2 %shard_map.85 = (bf16[24,5376]{1,0:T(8,128)(2,1)}, f32[24,5376]{1,0:T(8,128)}) custom-call(s32[5]{0:T(128)} %stack.23.info, bf16[24,3584]{1,0:T(8,128)(2,1)} %get-tuple-element.18.mid_send, f32[24,3584]{1,0:T(8,128)} %get-tuple-element.19.mid_keep, f32[24,3584]{1,0:T(8,128)} %get-tuple-element.20.in_keep, bf16[24,3584]{1,0:T(8,128)(2,1)} %copy-done.7), custom_call_target="tpu_custom_call" | custom-call | flops 1048576 | bytes 1048576 | tf_op jit(solution)/shard_map/pallas_call | solution.py:47
  13.1 3.3 %collective-permute-start.1 = (bf16[24,5376]{1,0:T(8,128)(2,1)}, bf16[24,5376]{1,0:T(8,128)(2,1)S(1)}, u32[]{:S(2)}, u32[]{:S(2)}) collective-permute-start(bf16[24,5376]{1,0:T(8,128)(2,1)} %get-tuple-element.23), channel_id=1, source_target_pairs={{0,64},{1,193},{2,66},{3,195},{4,68},{5,197},{6,70},{7,199},{8,72}... | collective-permute-start | bytes 774152 | tf_op jit(solution)/shard_map/ppermute | solution.py:32
  16.4 5.6 %collective-permute-start.6 = (bf16[24,3584]{1,0:T(8,128)(2,1)}, bf16[24,3584]{1,0:T(8,128)(2,1)S(1)}, u32[]{:S(2)}, u32[]{:S(2)}) collective-permute-start(bf16[24,3584]{1,0:T(8,128)(2,1)} %get-tuple-element.27), channel_id=1, source_target_pairs={{0,63},{1,2},{2,1},{3,4},{4,3},{5,6},{6,5},{7,8},{8,7},{9,10},{10,... | collective-permute-start | bytes 516104 | tf_op jit(solution)/shard_map/ppermute | solution.py:42
  22.0 1.8 %collective-permute-done.1.recv = bf16[24,5376]{1,0:T(8,128)(2,1)S(1)} collective-permute-done((bf16[24,5376]{1,0:T(8,128)(2,1)}, bf16[24,5376]{1,0:T(8,128)(2,1)S(1)}, u32[]{:S(2)}, u32[]{:S(2)}) %collective-permute-start.1) | collective-permute-done | bytes 258080 | tf_op jit(solution)/shard_map/ppermute | solution.py:32
  23.8 0.0 copy-start.6
  23.8 0.7 copy-done.6
  24.5 1.9 %shard_map.86 = (bf16[24,2688]{1,0:T(8,128)(2,1)}, f32[24,2688]{1,0:T(8,128)}) custom-call(s32[5]{0:T(128)} %stack.23.info, f32[24,5376]{1,0:T(8,128)} %get-tuple-element.22.keep, bf16[24,5376]{1,0:T(8,128)(2,1)} %copy-done.6), custom_call_target="tpu_custom_call" | custom-call | flops 1048576 | bytes 1048576 | tf_op jit(solution)/shard_map/pallas_call | solution.py:47
  26.4 0.0 copy-start
  26.4 0.0 copy-start.4
  26.4 5.8 %collective-permute-start.2 = (bf16[24,2688]{1,0:T(8,128)(2,1)}, bf16[24,2688]{1,0:T(8,128)(2,1)S(1)}, u32[]{:S(2)}, u32[]{:S(2)}) collective-permute-start(bf16[24,2688]{1,0:T(8,128)(2,1)} %get-tuple-element.25), channel_id=1, source_target_pairs={{0,192},{1,65},{2,194},{3,67},{4,196},{5,69},{6,198},{7,71},{8,200... | collective-permute-start | bytes 387080 | tf_op jit(solution)/shard_map/ppermute | solution.py:32
  32.3 0.0 collective-permute-done.6.out_recv
  32.3 0.7 copy-done.8
  32.9 1.8 %shard_map.89 = (bf16[24,1792]{1,0:T(8,128)(2,1)}, f32[24,1792]{1,0:T(8,128)}) custom-call(s32[5]{0:T(128)} %stack.23.info, f32[24,3584]{1,0:T(8,128)} %get-tuple-element.26.out_keep, bf16[24,3584]{1,0:T(8,128)(2,1)} %copy-done.8), custom_call_target="tpu_custom_call" | custom-call | flops 1048576 | bytes 1048576 | tf_op jit(solution)/shard_map/pallas_call | solution.py:47
  34.7 1.5 %collective-permute-start.7 = (bf16[24,1792]{1,0:T(8,128)(2,1)}, bf16[24,1792]{1,0:T(8,128)(2,1)S(1)}, u32[]{:S(2)}, u32[]{:S(2)}) collective-permute-start(bf16[24,1792]{1,0:T(8,128)(2,1)} %get-tuple-element.29), channel_id=1, source_target_pairs={{0,64},{1,193},{2,66},{3,195},{4,68},{5,197},{6,70},{7,199},{8,72}... | collective-permute-start | bytes 258056 | tf_op jit(solution)/shard_map/ppermute | solution.py:32
  36.2 1.2 %collective-permute-done.2 = bf16[24,2688]{1,0:T(8,128)(2,1)S(1)} collective-permute-done((bf16[24,2688]{1,0:T(8,128)(2,1)}, bf16[24,2688]{1,0:T(8,128)(2,1)S(1)}, u32[]{:S(2)}, u32[]{:S(2)}) %collective-permute-start.2) | collective-permute-done | bytes 129056 | tf_op jit(solution)/shard_map/ppermute | solution.py:32
  37.4 1.0 %add_convert_fusion.own = bf16[24,2688]{1,0:T(8,128)(2,1)S(1)} fusion(f32[24,2688]{1,0:T(8,128)} %get-tuple-element.24, bf16[24,2688]{1,0:T(8,128)(2,1)S(1)} %collective-permute-done.2), kind=kLoop, calls=%fused_computation | loop fusion | flops 193536 | bytes 516096 | tf_op jit(solution)/shard_map/convert_element_type | solution.py:162
  38.4 0.0 copy-start.5
  38.4 4.6 %collective-permute-start.3 = (bf16[24,2688]{1,0:T(8,128)(2,1)S(1)}, bf16[24,2688]{1,0:T(8,128)(2,1)S(1)}, u32[]{:S(2)}, u32[]{:S(2)}) collective-permute-start(bf16[24,2688]{1,0:T(8,128)(2,1)S(1)} %add_convert_fusion.own), channel_id=1, source_target_pairs={{0,192},{1,65},{2,194},{3,67},{4,196},{5,69},{6,198},{7,71},{8,200... | collective-permute-start | bytes 387080 | tf_op jit(solution)/shard_map/ppermute | solution.py:32
  43.0 0.3 collective-permute-done.7.recv
  43.3 0.6 copy-done.11
  43.9 1.7 %shard_map.90 = (bf16[24,896]{1,0:T(8,128)(2,1)}, f32[24,896]{1,0:T(8,128)}) custom-call(s32[5]{0:T(128)} %stack.23.info, f32[24,1792]{1,0:T(8,128)} %get-tuple-element.28.keep, bf16[24,1792]{1,0:T(8,128)(2,1)} %copy-done.11), custom_call_target="tpu_custom_call" | custom-call | flops 1048576 | bytes 1048576 | tf_op jit(solution)/shard_map/pallas_call | solution.py:47
  45.6 0.0 collective-permute-start.8
  45.6 0.6 collective-permute-done.3.recv
  46.2 0.0 copy-done.5
  46.2 0.6 copy-done.10
  46.9 1.7 %shard_map.87 = bf16[24,5376]{1,0:T(8,128)(2,1)} custom-call(s32[5]{0:T(128)} %stack.23.info, bf16[24,2688]{1,0:T(8,128)(2,1)} %copy-done.5, bf16[24,2688]{1,0:T(8,128)(2,1)} %copy-done.10), custom_call_target="tpu_custom_call" | custom-call | flops 1048576 | bytes 1048576 | tf_op jit(solution)/shard_map/pallas_call | solution.py:47
  48.6 1.5 %collective-permute-start.4 = (bf16[24,5376]{1,0:T(8,128)(2,1)}, bf16[24,5376]{1,0:T(8,128)(2,1)S(1)}, u32[]{:S(2)}, u32[]{:S(2)}) collective-permute-start(bf16[24,5376]{1,0:T(8,128)(2,1)} %shard_map.87), channel_id=1, source_target_pairs={{0,64},{1,193},{2,66},{3,195},{4,68},{5,197},{6,70},{7,199},{8,72}... | collective-permute-start | bytes 774152 | tf_op jit(solution)/shard_map/ppermute | solution.py:32
  50.1 2.4 %collective-permute-done.8 = bf16[24,896]{1,0:T(8,128)(2,1)S(1)} collective-permute-done((bf16[24,896]{1,0:T(8,128)(2,1)}, bf16[24,896]{1,0:T(8,128)(2,1)S(1)}, u32[]{:S(2)}, u32[]{:S(2)}) %collective-permute-start.8) | collective-permute-done | bytes 43040 | tf_op jit(solution)/shard_map/ppermute | solution.py:32
  52.5 0.9 %add_convert_fusion.1.own = bf16[24,896]{1,0:T(8,128)(2,1)S(1)} fusion(f32[24,896]{1,0:T(8,128)} %get-tuple-element.30, bf16[24,896]{1,0:T(8,128)(2,1)S(1)} %collective-permute-done.8), kind=kLoop, calls=%fused_computation.1 | loop fusion | flops 64512 | bytes 172032 | tf_op jit(solution)/shard_map/convert_element_type | solution.py:162
  53.4 0.0 copy-start.9
  53.4 0.8 collective-permute-start.9
  54.1 5.5 %collective-permute-done.9.recv = bf16[24,896]{1,0:T(8,128)(2,1)S(1)} collective-permute-done((bf16[24,896]{1,0:T(8,128)(2,1)S(1)}, bf16[24,896]{1,0:T(8,128)(2,1)S(1)}, u32[]{:S(2)}, u32[]{:S(2)}) %collective-permute-start.9) | collective-permute-done | bytes 43040 | tf_op jit(solution)/shard_map/ppermute | solution.py:32
  59.7 0.0 copy-done.9
  59.7 0.6 copy-done.13
  60.3 1.5 %shard_map.91.own = bf16[24,1792]{1,0:T(8,128)(2,1)} custom-call(s32[5]{0:T(128)} %stack.23.info, bf16[24,896]{1,0:T(8,128)(2,1)} %copy-done.9, bf16[24,896]{1,0:T(8,128)(2,1)} %copy-done.13), custom_call_target="tpu_custom_call" | custom-call | flops 1048576 | bytes 1048576 | tf_op jit(solution)/shard_map/pallas_call | solution.py:47
  61.8 0.0 collective-permute-start.10
  61.8 5.6 %collective-permute-done.10.recv = bf16[24,1792]{1,0:T(8,128)(2,1)S(1)} collective-permute-done((bf16[24,1792]{1,0:T(8,128)(2,1)}, bf16[24,1792]{1,0:T(8,128)(2,1)S(1)}, u32[]{:S(2)}, u32[]{:S(2)}) %collective-permute-start.10) | collective-permute-done | bytes 86048 | tf_op jit(solution)/shard_map/ppermute | solution.py:32
  67.4 0.6 copy-done.12
  68.0 1.6 %shard_map.92.out_mine = bf16[24,3584]{1,0:T(8,128)(2,1)} custom-call(s32[5]{0:T(128)} %stack.23.info, bf16[24,1792]{1,0:T(8,128)(2,1)} %shard_map.91.own, bf16[24,1792]{1,0:T(8,128)(2,1)} %copy-done.12), custom_call_target="tpu_custom_call" | custom-call | flops 1048576 | bytes 1048576 | tf_op jit(solution)/shard_map/pallas_call | solution.py:47
  69.6 0.0 collective-permute-start.11
  69.6 1.5 %slice.18.own = bf16[24,1792]{1,0:T(8,128)(2,1)} slice(bf16[24,5376]{1,0:T(8,128)(2,1)} %shard_map.87), slice={[0:24], [3584:5376]} | slice | bytes 172032 | tf_op jit(solution)/shard_map/slice | solution.py:253
  71.2 0.0 collective-permute-done.4
  71.2 0.6 slice.19.recv
  71.8 1.6 %shard_map.88.in_mine = bf16[24,3584]{1,0:T(8,128)(2,1)} custom-call(s32[5]{0:T(128)} %stack.23.info, bf16[24,1792]{1,0:T(8,128)(2,1)} %slice.18.own, bf16[24,1792]{1,0:T(8,128)(2,1)} %slice.19.recv), custom_call_target="tpu_custom_call" | custom-call | flops 1048576 | bytes 1048576 | tf_op jit(solution)/shard_map/pallas_call | solution.py:47
  73.4 2.2 %collective-permute-start.5 = (bf16[24,3584]{1,0:T(8,128)(2,1)}, bf16[24,3584]{1,0:T(8,128)(2,1)S(1)}, u32[]{:S(2)}, u32[]{:S(2)}) collective-permute-start(bf16[24,3584]{1,0:T(8,128)(2,1)} %shard_map.88.in_mine), channel_id=1, source_target_pairs={{0,1},{1,0},{2,3},{3,2},{4,5},{5,4},{6,7},{7,6},{8,9},{9,8},{10,11... | collective-permute-start | bytes 516104 | tf_op jit(solution)/shard_map/ppermute | solution.py:36
  75.6 0.9 %slice.16.own1 = bf16[24,3584]{1,0:T(8,128)(2,1)S(1)} slice(bf16[24,5376]{1,0:T(8,128)(2,1)} %shard_map.87), slice={[0:24], [0:3584]} | slice | bytes 344064 | tf_op jit(solution)/shard_map/slice | solution.py:264
  76.5 1.1 %collective-permute-done.11.out_other = bf16[24,3584]{1,0:T(8,128)(2,1)S(1)} collective-permute-done((bf16[24,3584]{1,0:T(8,128)(2,1)}, bf16[24,3584]{1,0:T(8,128)(2,1)S(1)}, u32[]{:S(2)}, u32[]{:S(2)}) %collective-permute-start.11) | collective-permute-done | bytes 172064 | tf_op jit(solution)/shard_map/ppermute | solution.py:42
  77.7 0.0 collective-permute-done.5.in_other
  77.7 0.0 copy-done
  77.7 0.0 copy-done.4
  77.7 0.0 copy-start.1
  77.7 1.6 %copy-done.1 = f32[72,7168]{1,0:T(8,128)S(1)} copy-done((f32[72,7168]{1,0:T(8,128)S(1)}, f32[72,7168]{1,0:T(8,128)}, u32[]{:S(2)}) %copy-start.1) | copy-done | bytes 2064408
  79.3 0.9 %copy-done.2 = bf16[24,3584]{1,0:T(8,128)(2,1)S(1)} copy-done((bf16[24,3584]{1,0:T(8,128)(2,1)S(1)}, bf16[24,3584]{1,0:T(8,128)(2,1)}, u32[]{:S(2)}) %copy-start.2) | copy-done | bytes 172056
  80.2 0.9 %copy-done.3 = bf16[24,3584]{1,0:T(8,128)(2,1)S(1)} copy-done((bf16[24,3584]{1,0:T(8,128)(2,1)S(1)}, bf16[24,3584]{1,0:T(8,128)(2,1)}, u32[]{:S(2)}) %copy-start.3) | copy-done | bytes 172056
  81.1 4.4 %shard_map.93 = (f32[72,7168]{1,0:T(8,128)}, f32[72,7168]{1,0:T(8,128)}, bf16[72,7168]{1,0:T(8,128)(2,1)}, f32[72,56]{1,0:T(8,128)S(1)}) custom-call(s32[5]{0:T(128)S(1)} %copy-done.4, bf16[24,3584]{1,0:T(8,128)(2,1)S(1)} %slice.16.own1, bf16[24,3584]{1,0:T(8,128)(2,1)S(1)} %slice.17.recv1, bf16[24,3584]{1,0:T(8,128)(2,1)S(1)} %copy-done.3, ...), custom_call_target="tpu_custom_call" | custom-call | flops 1048576 | bytes 1048576 | tf_op jit(solution)/shard_map/pallas_call | solution.py:47
  85.5 0.7 copy.10
  (8 shorter events, 0.0 us)
Async XLA Ops:
  8.7 1.6 %collective-permute-start = (bf16[24,3584]{1,0:T(8,128)(2,1)}, bf16[24,3584]{1,0:T(8,128)(2,1)S(1)}, u32[]{:S(2)}, u32[]{:S(2)}) collective-permute-start(bf16[24,3584]{1,0:T(8,128)(2,1)} %get-tuple-element.21), channel_id=1, source_target_pairs={{0,1},{1,0},{2,3},{3,2},{4,5},{5,4},{6,7},{7,6},{8,9},{9,8},{10,11... | collective-permute-start | bytes 516104 | tf_op jit(solution)/shard_map/ppermute | solution.py:36
  10.3 0.7 copy-start.7
  13.1 10.7 %collective-permute-start.1 = (bf16[24,5376]{1,0:T(8,128)(2,1)}, bf16[24,5376]{1,0:T(8,128)(2,1)S(1)}, u32[]{:S(2)}, u32[]{:S(2)}) collective-permute-start(bf16[24,5376]{1,0:T(8,128)(2,1)} %get-tuple-element.23), channel_id=1, source_target_pairs={{0,64},{1,193},{2,66},{3,195},{4,68},{5,197},{6,70},{7,199},{8,72}... | collective-permute-start | bytes 774152 | tf_op jit(solution)/shard_map/ppermute | solution.py:32
  16.4 15.8 %collective-permute-start.6 = (bf16[24,3584]{1,0:T(8,128)(2,1)}, bf16[24,3584]{1,0:T(8,128)(2,1)S(1)}, u32[]{:S(2)}, u32[]{:S(2)}) collective-permute-start(bf16[24,3584]{1,0:T(8,128)(2,1)} %get-tuple-element.27), channel_id=1, source_target_pairs={{0,63},{1,2},{2,1},{3,4},{4,3},{5,6},{6,5},{7,8},{8,7},{9,10},{10,... | collective-permute-start | bytes 516104 | tf_op jit(solution)/shard_map/ppermute | solution.py:42
  23.8 0.7 copy-start.6
  26.4 51.3 %copy-start = (f32[72,7168]{1,0:T(8,128)S(1)}, f32[72,7168]{1,0:T(8,128)}, u32[]{:S(2)}) copy-start(f32[72,7168]{1,0:T(8,128)} %params.1) | copy-start | bytes 6193156
  26.4 51.3 %copy-start.4 = (s32[5]{0:T(128)S(1)}, s32[5]{0:T(128)}, u32[]{:S(2)}) copy-start(s32[5]{0:T(128)} %stack.23.info) | copy-start | bytes 64
  26.4 11.0 %collective-permute-start.2 = (bf16[24,2688]{1,0:T(8,128)(2,1)}, bf16[24,2688]{1,0:T(8,128)(2,1)S(1)}, u32[]{:S(2)}, u32[]{:S(2)}) collective-permute-start(bf16[24,2688]{1,0:T(8,128)(2,1)} %get-tuple-element.25), channel_id=1, source_target_pairs={{0,192},{1,65},{2,194},{3,67},{4,196},{5,69},{6,198},{7,71},{8,200... | collective-permute-start | bytes 387080 | tf_op jit(solution)/shard_map/ppermute | solution.py:32
  32.3 0.7 copy-start.8
  34.7 8.6 %collective-permute-start.7 = (bf16[24,1792]{1,0:T(8,128)(2,1)}, bf16[24,1792]{1,0:T(8,128)(2,1)S(1)}, u32[]{:S(2)}, u32[]{:S(2)}) collective-permute-start(bf16[24,1792]{1,0:T(8,128)(2,1)} %get-tuple-element.29), channel_id=1, source_target_pairs={{0,64},{1,193},{2,66},{3,195},{4,68},{5,197},{6,70},{7,199},{8,72}... | collective-permute-start | bytes 258056 | tf_op jit(solution)/shard_map/ppermute | solution.py:32
  38.4 7.9 %copy-start.5 = (bf16[24,2688]{1,0:T(8,128)(2,1)}, bf16[24,2688]{1,0:T(8,128)(2,1)S(1)}, u32[]{:S(2)}) copy-start(bf16[24,2688]{1,0:T(8,128)(2,1)S(1)} %add_convert_fusion.own) | copy-start | bytes 387076
  38.4 7.9 %collective-permute-start.3 = (bf16[24,2688]{1,0:T(8,128)(2,1)S(1)}, bf16[24,2688]{1,0:T(8,128)(2,1)S(1)}, u32[]{:S(2)}, u32[]{:S(2)}) collective-permute-start(bf16[24,2688]{1,0:T(8,128)(2,1)S(1)} %add_convert_fusion.own), channel_id=1, source_target_pairs={{0,192},{1,65},{2,194},{3,67},{4,196},{5,69},{6,198},{7,71},{8,200... | collective-permute-start | bytes 387080 | tf_op jit(solution)/shard_map/ppermute | solution.py:32
  43.3 0.6 copy-start.11
  45.6 6.9 %collective-permute-start.8 = (bf16[24,896]{1,0:T(8,128)(2,1)}, bf16[24,896]{1,0:T(8,128)(2,1)S(1)}, u32[]{:S(2)}, u32[]{:S(2)}) collective-permute-start(bf16[24,896]{1,0:T(8,128)(2,1)} %get-tuple-element.31), channel_id=1, source_target_pairs={{0,192},{1,65},{2,194},{3,67},{4,196},{5,69},{6,198},{7,71},{8,200... | collective-permute-start | bytes 129032 | tf_op jit(solution)/shard_map/ppermute | solution.py:32
  46.2 0.7 copy-start.10
  48.6 22.6 %collective-permute-start.4 = (bf16[24,5376]{1,0:T(8,128)(2,1)}, bf16[24,5376]{1,0:T(8,128)(2,1)S(1)}, u32[]{:S(2)}, u32[]{:S(2)}) collective-permute-start(bf16[24,5376]{1,0:T(8,128)(2,1)} %shard_map.87), channel_id=1, source_target_pairs={{0,64},{1,193},{2,66},{3,195},{4,68},{5,197},{6,70},{7,199},{8,72}... | collective-permute-start | bytes 774152 | tf_op jit(solution)/shard_map/ppermute | solution.py:32
  53.4 6.3 %copy-start.9 = (bf16[24,896]{1,0:T(8,128)(2,1)}, bf16[24,896]{1,0:T(8,128)(2,1)S(1)}, u32[]{:S(2)}) copy-start(bf16[24,896]{1,0:T(8,128)(2,1)S(1)} %add_convert_fusion.1.own) | copy-start | bytes 129028
  53.4 6.3 %collective-permute-start.9 = (bf16[24,896]{1,0:T(8,128)(2,1)S(1)}, bf16[24,896]{1,0:T(8,128)(2,1)S(1)}, u32[]{:S(2)}, u32[]{:S(2)}) collective-permute-start(bf16[24,896]{1,0:T(8,128)(2,1)S(1)} %add_convert_fusion.1.own), channel_id=1, source_target_pairs={{0,192},{1,65},{2,194},{3,67},{4,196},{5,69},{6,198},{7,71},{8,200... | collective-permute-start | bytes 129032 | tf_op jit(solution)/shard_map/ppermute | solution.py:32
  59.7 0.6 copy-start.13
  61.8 5.6 %collective-permute-start.10 = (bf16[24,1792]{1,0:T(8,128)(2,1)}, bf16[24,1792]{1,0:T(8,128)(2,1)S(1)}, u32[]{:S(2)}, u32[]{:S(2)}) collective-permute-start(bf16[24,1792]{1,0:T(8,128)(2,1)} %shard_map.91.own), channel_id=1, source_target_pairs={{0,64},{1,193},{2,66},{3,195},{4,68},{5,197},{6,70},{7,199},{8,72}... | collective-permute-start | bytes 258056 | tf_op jit(solution)/shard_map/ppermute | solution.py:32
  67.4 0.6 copy-start.12
  69.6 8.1 %collective-permute-start.11 = (bf16[24,3584]{1,0:T(8,128)(2,1)}, bf16[24,3584]{1,0:T(8,128)(2,1)S(1)}, u32[]{:S(2)}, u32[]{:S(2)}) collective-permute-start(bf16[24,3584]{1,0:T(8,128)(2,1)} %shard_map.92.out_mine), channel_id=1, source_target_pairs={{0,63},{1,2},{2,1},{3,4},{4,3},{5,6},{6,5},{7,8},{8,7},{9,10},{10,... | collective-permute-start | bytes 516104 | tf_op jit(solution)/shard_map/ppermute | solution.py:42
  73.4 4.2 %collective-permute-start.5 = (bf16[24,3584]{1,0:T(8,128)(2,1)}, bf16[24,3584]{1,0:T(8,128)(2,1)S(1)}, u32[]{:S(2)}, u32[]{:S(2)}) collective-permute-start(bf16[24,3584]{1,0:T(8,128)(2,1)} %shard_map.88.in_mine), channel_id=1, source_target_pairs={{0,1},{1,0},{2,3},{3,2},{4,5},{5,4},{6,7},{7,6},{8,9},{9,8},{10,11... | collective-permute-start | bytes 516104 | tf_op jit(solution)/shard_map/ppermute | solution.py:36
  77.7 1.6 %copy-start.1 = (f32[72,7168]{1,0:T(8,128)S(1)}, f32[72,7168]{1,0:T(8,128)}, u32[]{:S(2)}) copy-start(f32[72,7168]{1,0:T(8,128)} %momentum.1) | copy-start | bytes 6193156
  79.3 0.9 %copy-start.2 = (bf16[24,3584]{1,0:T(8,128)(2,1)S(1)}, bf16[24,3584]{1,0:T(8,128)(2,1)}, u32[]{:S(2)}) copy-start(bf16[24,3584]{1,0:T(8,128)(2,1)} %shard_map.92.out_mine) | copy-start | bytes 516100
  80.2 0.9 %copy-start.3 = (bf16[24,3584]{1,0:T(8,128)(2,1)S(1)}, bf16[24,3584]{1,0:T(8,128)(2,1)}, u32[]{:S(2)}) copy-start(bf16[24,3584]{1,0:T(8,128)(2,1)} %shard_map.88.in_mine) | copy-start | bytes 516100

commit v2 on v0

v2 whole, which is shorter than its diff:
```python
import jax
import jax.numpy as jnp
from jax import lax
from jax.experimental import pallas as pl
from jax.experimental.pallas import tpu as pltpu
from jax.sharding import PartitionSpec as P

ROWS_DEV = 48
HALF = 12
BAND = 24
QB = 128

momentum_keep = 0.9
outer_rate = 0.7
block_eps = 1e-06

F32 = jnp.float32
BF16 = jnp.bfloat16
AXES = ("island", "fsdp")
PAIRINGS = ({0: 1, 1: 0, 2: 3, 3: 2}, {0: 3, 3: 0, 1: 2, 2: 1})


def island_swap(value, step):
    shards = lax.axis_size("fsdp")
    pairs = [
        (i * shards + j, PAIRINGS[(j + step) % 2][i] * shards + j)
        for i in range(4)
        for j in range(shards)
    ]
    return lax.ppermute(value, AXES, pairs)


def inner_swap(value):
    return lax.ppermute(value, "fsdp", [(j, j ^ 1) for j in range(lax.axis_size("fsdp"))])


def outer_swap(value):
    count = lax.axis_size("fsdp")
    pairs = [(j, (j + 1) % count if j & 1 else (j - 1) % count) for j in range(count)]
    return lax.ppermute(value, "fsdp", pairs)


def place(bounds):
    island, shard = lax.axis_index("island"), lax.axis_index("fsdp")
    origin = shard * ROWS_DEV - HALF
    odd = shard & 1
    low, high = island & 1, island >> 1
    bit_a = jnp.where(odd == 0, low ^ high, high)
    bit_b = jnp.where(odd == 0, high, low ^ high)
    return bounds[island, shard] - origin, bounds[island, shard + 1] - origin, bit_a, bit_b, odd


def live_rows(span, first, rows, width):
    row = lax.broadcasted_iota(jnp.int32, (rows, width), 0) + first
    return ((row >= span[0]) & (row < span[1])).astype(F32)


def local_call(body, outs, bounds, *arrays, grant, scratch=()):
    vmem = pl.BlockSpec(memory_space=pltpu.VMEM)
    return pl.pallas_call(
        body,
        out_shape=[jax.ShapeDtypeStruct(s, d) for s, d in outs],
        in_specs=[pl.BlockSpec(memory_space=pltpu.SMEM)] + [vmem] * len(arrays),
        out_specs=[vmem] * len(outs),
        scratch_shapes=scratch,
        cost_estimate=pl.CostEstimate(flops=1 << 20, bytes_accessed=1 << 20, transcendentals=0),
        compiler_params=pltpu.CompilerParams(vmem_limit_bytes=grant << 20),
    )(bounds, *arrays)


def terms_body(bounds, payload, scales, mid_send, mid_keep, in_send, out_send, out_first, out_keep,
               rows_scales):
    lo, hi, a, b, c = place(bounds)
    blocks = payload.shape[1] // QB
    half, eighth = blocks // 2, blocks // 8
    slots = payload.shape[0]
    rows_scales[:, :] = jnp.zeros(rows_scales.shape, F32)
    rows_scales[:, :blocks] = jnp.transpose(scales[...]) * live_rows((lo, hi), 0, slots, blocks)

    def fill(first, start, count, target, at=0):
        rows = pl.ds(first, BAND)
        local = pltpu.roll(rows_scales[rows, :], lax.rem(QB - start, QB), 1)
        for k in range(count):
            cols = pl.ds(pl.multiple_of((start + k) * QB, QB), QB)
            block = payload[rows, cols].astype(F32) * local[:, k : k + 1]
            target[:, (at + k) * QB : (at + k + 1) * QB] = block.astype(target.dtype)

    inner = pl.multiple_of((1 - c) * (2 * BAND), 16)
    outer = pl.multiple_of(c * (2 * BAND), 16)
    for u in range(2):
        for v in range(2):
            mine = (a ^ 1 ^ u) * 2 + (b ^ 1 ^ v)
            theirs = (b ^ 1 ^ u) * 2 + (a ^ 1 ^ v)
            fill(outer, c * half + theirs * eighth, eighth, out_send.at[2 * u + v])
            fill(inner, (1 - c) * half + theirs * eighth, eighth, in_send.at[2 * u + v])
    for u in range(2):
        for v in range(2):
            mine = (a ^ 1 ^ u) * 2 + (b ^ 1 ^ v)
            wide = (mid_send, mid_keep)[u].at[v]
            fill(BAND, mine * 2 * eighth, 2 * eighth, wide)
            fill(inner, c * half + mine * eighth, eighth, wide, 2 * eighth)
            fill(outer, (1 - c) * half + mine * eighth, eighth, (out_first, out_keep)[u].at[v])


def add_to(total, part):
    return (total.astype(F32) + part.astype(F32)).astype(total.dtype)


def reduce_band(send, keep):
    recv = island_swap(send, 0)
    send = (keep[0] + recv[0].astype(F32)).astype(BF16)
    keep = keep[1] + recv[1].astype(F32)
    recv = island_swap(send, 1)
    quarter = (keep + recv.astype(F32)).astype(BF16)
    other = island_swap(quarter, 1)
    return jnp.stack([quarter, other])


def step_body(bounds, own1, recv1, in_other, own2, recv2, out_other, params, momentum,
              params_out, momentum_out, payload_out, scales_out, rows_scales):
    lo, hi, a, b, c = place(bounds)
    blocks = params.shape[1] // QB
    half, fourth, eighth = blocks // 2, blocks // 4, blocks // 8
    lane = lax.broadcasted_iota(jnp.int32, (BAND, QB), 1)

    def band(first, source):
        rows = pl.ds(first, BAND)
        live = live_rows((lo, hi), first, BAND, QB)
        scale_row = jnp.zeros((BAND, QB), F32)
        for g in range(blocks):
            cols = slice(g * QB, (g + 1) * QB)
            summed = source(g).astype(F32)
            block_scale = jnp.max(jnp.abs(summed), axis=1, keepdims=True) + block_eps
            coded = (summed * (1.0 / block_scale)).astype(BF16).astype(F32) * live
            block_live = block_scale * live
            delta = coded * (block_live * 0.25)
            moved = momentum_keep * momentum[rows, cols] + delta
            momentum_out[rows, cols] = moved
            params_out[rows, cols] = params[rows, cols] - outer_rate * (
                delta + momentum_keep * moved
            )
            payload_out[rows, cols] = coded.astype(BF16)
            scale_row = jnp.where(lane == g, block_live, scale_row)
        rows_scales[rows, :] = scale_row

    def mid(g):
        part, quarter, k = g // half, g // fourth % 2, g % fourth
        cols = slice(k * QB, (k + 1) * QB)
        return jnp.where(a == part, own1[quarter ^ b, :, cols], recv1[quarter ^ b, :, cols])

    def side(mine_half, own, recv, at, other):
        def source(g):
            part, quarter, k = g % half // fourth, g // eighth % 2, g % eighth
            near = slice((at + k) * QB, (at + k + 1) * QB)
            far = slice(k * QB, (k + 1) * QB)
            mine = jnp.where(a == part, own[quarter ^ b, :, near], recv[quarter ^ b, :, near])
            theirs = other[2 * (part ^ b) + (quarter ^ a), :, far]
            return jnp.where(mine_half == g // half, mine, theirs)

        return source

    band(BAND, mid)
    band(pl.multiple_of((1 - c) * (2 * BAND), 16), side(c, own1, recv1, fourth, in_other))
    band(pl.multiple_of(c * (2 * BAND), 16), side(1 - c, own2, recv2, 0, out_other))
    scales_out[...] = jnp.transpose(rows_scales[...])[:blocks, :]


def shards(params, momentum, payload, scales, bounds):
    slots, width = payload.shape
    fourth, eighth = width // 4, width // 8
    wide = fourth + eighth
    mid_send, mid_keep, in_send, out_send, out_first, out_keep = local_call(
        terms_body,
        [
            ((2, BAND, wide), BF16),
            ((2, BAND, wide), F32),
            ((4, BAND, eighth), BF16),
            ((4, BAND, eighth), BF16),
            ((2, BAND, eighth), BF16),
            ((2, BAND, eighth), F32),
        ],
        bounds,
        payload,
        scales.T,
        grant=8,
        scratch=[pltpu.VMEM((slots, QB), F32)],
    )
    out_recv = outer_swap(out_send)
    in_recv = inner_swap(in_send)
    send1 = mid_send.at[:, :, fourth:].set(add_to(mid_send[:, :, fourth:], in_recv[:2]))
    keep1 = mid_keep.at[:, :, fourth:].set(add_to(mid_keep[:, :, fourth:], in_recv[2:]))
    own1 = reduce_band(send1, keep1)
    own2 = reduce_band(add_to(out_first, out_recv[:2]), add_to(out_keep, out_recv[2:]))
    recv2 = island_swap(own2, 0)
    out_other = outer_swap(jnp.concatenate([own2, recv2]))
    recv1 = island_swap(own1, 0)
    in_other = inner_swap(jnp.concatenate([own1[:, :, fourth:], recv1[:, :, fourth:]]))
    params_out, momentum_out, payload_out, scales_out = local_call(
        step_body,
        [
            ((slots, width), F32),
            ((slots, width), F32),
            ((slots, width), BF16),
            ((width // QB, slots), F32),
        ],
        bounds,
        own1,
        recv1,
        in_other,
        own2,
        recv2,
        out_other,
        params,
        momentum,
        grant=20,
        scratch=[pltpu.VMEM((slots, QB), F32)],
    )
    return params_out, momentum_out, payload_out, scales_out.T


def solution(mesh):
    spec = P(("island", "fsdp"), None)
    return jax.shard_map(
        shards, mesh=mesh, in_specs=(spec,) * 4 + (P(),), out_specs=(spec,) * 4, check_vma=False
    )
```

time: 237 us -> 66 us (0.28)
  waiting for transfers between devices: 137 us -> 26.9 us
  starting transfers between devices: 76 us -> 27.5 us
  other arithmetic: 12 us -> 0.34 us
  Pallas kernels: 0 us -> 6.96 us
  local copies, waits for them, and re-layouts: 8.54 us -> 2.66 us
    ppermute x18 -> x12, waiting for transfers between devices: 137 us -> 26.9 us  [the longest x8 21.1 us: island_swap(): return lax.ppermute(value, AXES, pairs)]
    ppermute x18 -> x12, starting transfers between devices: 76 us -> 27.5 us  [the longest x8 23.8 us: island_swap(): return lax.ppermute(value, AXES, pairs)]
    pallas_call x0 -> x2, Pallas kernels: none -> 6.96 us  [local_call(): pl.pallas_call(body, out_shape=[jax.ShapeDtypeStruct(s, d) for s, d in ou...]
    sub x1 -> x0, other arithmetic: 3.71 us -> none  [shards(): params_out = params - outer_rate * (delta + momentum_keep * momentum_out)]
    mul x5 -> x0, local copies, waits for them, and re-layouts: 2.98 us -> none  [dequantize(): return (blocks * block_scale[:, :, None]).reshape(rows, width)]
    unnamed x1 -> x0, other arithmetic: 2.49 us -> none
  transfers between devices with their start and end apart: 18 -> 12, of which waited for: 11 -> 8; matrix products, arithmetic and copies ran while one was open for 0% -> 1% of each run, Pallas kernels for 0% -> 0%
where the time goes in v2:
time: 66 us; the launch traced here: 65.1 us
  starting transfers between devices  27.5 us (42%)
  waiting for transfers between devices  26.9 us (41%)
  Pallas kernels  6.96 us (11%)
  local copies, waits for them, and re-layouts  2.66 us (4%)
  between operations  0.73 us (1%)
    ppermute x8, starting transfers between devices, island_swap(): return lax.ppermute(value, AXES, pairs)  23.8 us
    ppermute x8, waiting for transfers between devices, island_swap(): return lax.ppermute(value, AXES, pairs)  21.1 us
    pallas_call x2, Pallas kernels, local_call(): pl.pallas_call(body, out_shape=[jax.ShapeDtypeStruct(s, d) for s, d in ou...  6.96 us
    ppermute x2, waiting for transfers between devices, outer_swap(): return lax.ppermute(value, 'fsdp', pairs)  4.57 us
    ppermute x2, starting transfers between devices, outer_swap(): return lax.ppermute(value, 'fsdp', pairs)  3.62 us
    unnamed x12, local copies, waits for them, and re-layouts  2.65 us
  transfers between devices with their start and end apart: 12, of which 8 were waited for; matrix products, arithmetic and copies ran while one was open for 1% of the time, Pallas kernels for 0%

profile of v2, /device:TPU:8, one launch (start us, length us, event | category | flops | bytes accessed | tf_op | source)
XLA Modules:
  0.0 65.1 jit_solution(13114878433550532089)
XLA Ops:
  0.6 0.0 copy-start.2
  0.6 1.2 %copy-done.2 = bf16[72,7168]{1,0:T(8,128)(2,1)S(1)} copy-done((bf16[72,7168]{1,0:T(8,128)(2,1)S(1)}, bf16[72,7168]{1,0:T(8,128)(2,1)}, u32[]{:S(2)}) %copy-start.2) | copy-done | bytes 1032216
  1.9 0.0 copy-start.3
  1.9 0.7 %copy-done.3 = f32[72,56]{0,1:T(8,128)S(1)} copy-done((f32[72,56]{0,1:T(8,128)S(1)}, f32[72,56]{0,1:T(8,128)}, u32[]{:S(2)}) %copy-start.3) | copy-done | bytes 16152
  2.6 0.0 copy-start.4
  2.6 0.7 %copy-done.4 = s32[4,65]{1,0:T(4,128)S(1)} copy-done((s32[4,65]{1,0:T(4,128)S(1)}, s32[4,65]{1,0:T(4,128)}, u32[]{:S(2)}) %copy-start.4) | copy-done | bytes 1064
  3.3 2.5 %shard_map.84 = (bf16[2,24,2688]{2,1,0:T(8,128)(2,1)S(1)}, f32[2,24,2688]{2,1,0:T(8,128)S(1)}, bf16[4,24,896]{2,1,0:T(8,128)(2,1)S(1)}, bf16[4,24,896]{2,1,0:T(8...) custom-call(s32[4,65]{1,0:T(4,128)S(1)} %copy-done.4, bf16[72,7168]{1,0:T(8,128)(2,1)S(1)} %copy-done.2, ...), custom_call_target="tpu_custom_call" | custom-call | flops 1048576 | bytes 1048576 | tf_op jit(solution)/shard_map/pallas_call | solution.py:60
  5.7 3.5 %collective-permute-start.6 = (bf16[4,24,896]{2,1,0:T(8,128)(2,1)S(1)}, bf16[4,24,896]{2,1,0:T(8,128)(2,1)S(1)}, u32[]{:S(2)}, u32[]{:S(2)}) collective-permute-start(bf16[4,24,896]{2,1,0:T(8,128)(2,1)S(1)} %get-tuple-element.42), channel_id=1, source_target_pairs={{0,63},{1,2},{2,1},{3,4},{4,3},{5,6},{6,5},{7,8},{8,7},{9,10},{10,... | collective-permute-start | bytes 516104 | tf_op jit(solution)/shard_map/ppermute | solution.py:40
  9.3 0.0 collective-permute-start
  9.3 4.4 %collective-permute-done.6 = bf16[4,24,896]{2,1,0:T(8,128)(2,1)S(1)} collective-permute-done((bf16[4,24,896]{2,1,0:T(8,128)(2,1)S(1)}, bf16[4,24,896]{2,1,0:T(8,128)(2,1)S(1)}, u32[]{:S(2)}, u32[]{:S(2)}) %collective-permute-start.6) | collective-permute-done | bytes 172064 | tf_op jit(solution)/shard_map/ppermute | solution.py:40
  13.7 3.4 %collective-permute-start.7 = (bf16[2,24,896]{2,1,0:T(8,128)(2,1)S(1)}, bf16[2,24,896]{2,1,0:T(8,128)(2,1)S(1)}, u32[]{:S(2)}, u32[]{:S(2)}) collective-permute-start(bf16[2,24,896]{2,1,0:T(8,128)(2,1)S(1)} %get-tuple-element.48), channel_id=1, source_target_pairs={{0,64},{1,193},{2,66},{3,195},{4,68},{5,197},{6,70},{7,199},{8,72}... | collective-permute-start | bytes 258056 | tf_op jit(solution)/shard_map/ppermute | solution.py:30
  17.1 0.0 collective-permute-done
  17.1 0.0 copy-start
  17.1 0.0 copy-start.1
  17.1 0.0 copy-start.5
  17.1 0.1 collective-permute-start.1
  17.3 2.3 %collective-permute-done.7 = bf16[2,24,896]{2,1,0:T(8,128)(2,1)S(1)} collective-permute-done((bf16[2,24,896]{2,1,0:T(8,128)(2,1)S(1)}, bf16[2,24,896]{2,1,0:T(8,128)(2,1)S(1)}, u32[]{:S(2)}, u32[]{:S(2)}) %collective-permute-start.7) | collective-permute-done | bytes 86048 | tf_op jit(solution)/shard_map/ppermute | solution.py:30
  19.7 6.3 %collective-permute-start.8 = (bf16[24,896]{1,0:T(8,128)(2,1)S(1)}, bf16[24,896]{1,0:T(8,128)(2,1)S(1)}, u32[]{:S(2)}, u32[]{:S(2)}) collective-permute-start(bf16[24,896]{1,0:T(8,128)(2,1)S(1)} %fusion.11), channel_id=1, source_target_pairs={{0,192},{1,65},{2,194},{3,67},{4,196},{5,69},{6,198},{7,71},{8,200... | collective-permute-start | bytes 129032 | tf_op jit(solution)/shard_map/ppermute | solution.py:30
  25.9 2.1 %collective-permute-done.1 = bf16[2,24,2688]{2,1,0:T(8,128)(2,1)S(1)} collective-permute-done((bf16[2,24,2688]{2,1,0:T(8,128)(2,1)S(1)}, bf16[2,24,2688]{2,1,0:T(8,128)(2,1)S(1)}, u32[]{:S(2)}, u32[]{:S(2)}) %collective-permute-start.1) | collective-permute-done | bytes 258080 | tf_op jit(solution)/shard_map/ppermute | solution.py:30
  28.0 4.6 %collective-permute-start.2 = (bf16[24,2688]{1,0:T(8,128)(2,1)S(1)}, bf16[24,2688]{1,0:T(8,128)(2,1)S(1)}, u32[]{:S(2)}, u32[]{:S(2)}) collective-permute-start(bf16[24,2688]{1,0:T(8,128)(2,1)S(1)} %fusion.4), channel_id=1, source_target_pairs={{0,192},{1,65},{2,194},{3,67},{4,196},{5,69},{6,198},{7,71},{8,200... | collective-permute-start | bytes 387080 | tf_op jit(solution)/shard_map/ppermute | solution.py:30
  32.6 0.0 collective-permute-done.8
  32.7 0.1 collective-permute-start.9
  32.8 4.1 %collective-permute-done.2 = bf16[24,2688]{1,0:T(8,128)(2,1)S(1)} collective-permute-done((bf16[24,2688]{1,0:T(8,128)(2,1)S(1)}, bf16[24,2688]{1,0:T(8,128)(2,1)S(1)}, u32[]{:S(2)}, u32[]{:S(2)}) %collective-permute-start.2) | collective-permute-done | bytes 129056 | tf_op jit(solution)/shard_map/ppermute | solution.py:30
  36.8 0.1 fusion.3
  36.9 4.6 %collective-permute-start.3 = (bf16[24,2688]{1,0:T(8,128)(2,1)S(1)}, bf16[24,2688]{1,0:T(8,128)(2,1)S(1)}, u32[]{:S(2)}, u32[]{:S(2)}) collective-permute-start(bf16[24,2688]{1,0:T(8,128)(2,1)S(1)} %fusion.3), channel_id=1, source_target_pairs={{0,192},{1,65},{2,194},{3,67},{4,196},{5,69},{6,198},{7,71},{8,200... | collective-permute-start | bytes 387080 | tf_op jit(solution)/shard_map/ppermute | solution.py:30
  41.5 0.0 collective-permute-done.9
  41.6 2.2 %collective-permute-start.10 = (bf16[2,24,896]{2,1,0:T(8,128)(2,1)S(1)}, bf16[2,24,896]{2,1,0:T(8,128)(2,1)S(1)}, u32[]{:S(2)}, u32[]{:S(2)}) collective-permute-start(bf16[2,24,896]{2,1,0:T(8,128)(2,1)S(1)} %pad_maximum_fusion.3.own2), channel_id=1, source_target_pairs={{0,64},{1,193},{2,66},{3,195},{4,68},{5,197},{6,70},{7,199},{8,72}... | collective-permute-start | bytes 258056 | tf_op jit(solution)/shard_map/ppermute | solution.py:30
  43.8 5.2 %collective-permute-done.3 = bf16[24,2688]{1,0:T(8,128)(2,1)S(1)} collective-permute-done((bf16[24,2688]{1,0:T(8,128)(2,1)S(1)}, bf16[24,2688]{1,0:T(8,128)(2,1)S(1)}, u32[]{:S(2)}, u32[]{:S(2)}) %collective-permute-start.3) | collective-permute-done | bytes 129056 | tf_op jit(solution)/shard_map/ppermute | solution.py:30
  49.0 2.4 %collective-permute-start.4 = (bf16[2,24,2688]{2,1,0:T(8,128)(2,1)S(1)}, bf16[2,24,2688]{2,1,0:T(8,128)(2,1)S(1)}, u32[]{:S(2)}, u32[]{:S(2)}) collective-permute-start(bf16[2,24,2688]{2,1,0:T(8,128)(2,1)S(1)} %pad_maximum_fusion.own1), channel_id=1, source_target_pairs={{0,64},{1,193},{2,66},{3,195},{4,68},{5,197},{6,70},{7,199},{8,72}... | collective-permute-start | bytes 774152 | tf_op jit(solution)/shard_map/ppermute | solution.py:30
  51.4 0.0 collective-permute-done.10.recv2
  51.5 0.1 collective-permute-start.11
  51.6 7.5 %collective-permute-done.4.recv1 = bf16[2,24,2688]{2,1,0:T(8,128)(2,1)S(1)} collective-permute-done((bf16[2,24,2688]{2,1,0:T(8,128)(2,1)S(1)}, bf16[2,24,2688]{2,1,0:T(8,128)(2,1)S(1)}, u32[]{:S(2)}, u32[]{:S(2)}) %collective-permute-start.4) | collective-permute-done | bytes 258080 | tf_op jit(solution)/shard_map/ppermute | solution.py:30
  59.1 0.1 collective-permute-start.5
  59.2 0.2 collective-permute-done.11.out_other
  59.4 1.2 %collective-permute-done.5.in_other = bf16[4,24,896]{2,1,0:T(8,128)(2,1)S(1)} collective-permute-done((bf16[4,24,896]{2,1,0:T(8,128)(2,1)S(1)}, bf16[4,24,896]{2,1,0:T(8,128)(2,1)S(1)}, u32[]{:S(2)}, u32[]{:S(2)}) %collective-permute-start.5) | collective-permute-done | bytes 172064 | tf_op jit(solution)/shard_map/ppermute | solution.py:34
  60.6 0.0 copy-done
  60.6 0.0 copy-done.1
  60.6 0.0 copy-done.5
  60.6 4.5 %shard_map.85 = (f32[72,7168]{1,0:T(8,128)}, f32[72,7168]{1,0:T(8,128)}, bf16[72,7168]{1,0:T(8,128)(2,1)}, f32[56,72]{1,0:T(8,128)}) custom-call(s32[4,65]{1,0:T(4,128)S(1)} %copy-done.5, bf16[2,24,2688]{2,1,0:T(8,128)(2,1)S(1)} %pad_maximum_fusion.own1, bf16[2,24,2688]{2,1,0:T(8,128)(2,1)S(1)} %collective-permute-done.4.recv1, ...), custom_call_target="tpu_custom_call" | custom-call | flops 1048576 | bytes 1048576 | tf_op jit(solution)/shard_map/pallas_call | solution.py:60
  (12 shorter events, 0.3 us)
Async XLA Ops:
  0.6 1.2 %copy-start.2 = (bf16[72,7168]{1,0:T(8,128)(2,1)S(1)}, bf16[72,7168]{1,0:T(8,128)(2,1)}, u32[]{:S(2)}) copy-start(bf16[72,7168]{1,0:T(8,128)(2,1)} %payload.1) | copy-start | bytes 3096580
  1.9 0.7 %copy-start.3 = (f32[72,56]{0,1:T(8,128)S(1)}, f32[72,56]{0,1:T(8,128)}, u32[]{:S(2)}) copy-start(f32[72,56]{0,1:T(8,128)} %param.12) | copy-start | bytes 48388
  2.6 0.7 %copy-start.4 = (s32[4,65]{1,0:T(4,128)S(1)}, s32[4,65]{1,0:T(4,128)}, u32[]{:S(2)}) copy-start(s32[4,65]{1,0:T(4,128)} %bounds.3) | copy-start | bytes 3124
  5.7 7.9 %collective-permute-start.6 = (bf16[4,24,896]{2,1,0:T(8,128)(2,1)S(1)}, bf16[4,24,896]{2,1,0:T(8,128)(2,1)S(1)}, u32[]{:S(2)}, u32[]{:S(2)}) collective-permute-start(bf16[4,24,896]{2,1,0:T(8,128)(2,1)S(1)} %get-tuple-element.42), channel_id=1, source_target_pairs={{0,63},{1,2},{2,1},{3,4},{4,3},{5,6},{6,5},{7,8},{8,7},{9,10},{10,... | collective-permute-start | bytes 516104 | tf_op jit(solution)/shard_map/ppermute | solution.py:40
  9.3 7.8 %collective-permute-start = (bf16[4,24,896]{2,1,0:T(8,128)(2,1)S(1)}, bf16[4,24,896]{2,1,0:T(8,128)(2,1)S(1)}, u32[]{:S(2)}, u32[]{:S(2)}) collective-permute-start(bf16[4,24,896]{2,1,0:T(8,128)(2,1)S(1)} %get-tuple-element.39), channel_id=1, source_target_pairs={{0,1},{1,0},{2,3},{3,2},{4,5},{5,4},{6,7},{7,6},{8,9},{9,8},{10,11... | collective-permute-start | bytes 516104 | tf_op jit(solution)/shard_map/ppermute | solution.py:34
  13.7 5.9 %collective-permute-start.7 = (bf16[2,24,896]{2,1,0:T(8,128)(2,1)S(1)}, bf16[2,24,896]{2,1,0:T(8,128)(2,1)S(1)}, u32[]{:S(2)}, u32[]{:S(2)}) collective-permute-start(bf16[2,24,896]{2,1,0:T(8,128)(2,1)S(1)} %get-tuple-element.48), channel_id=1, source_target_pairs={{0,64},{1,193},{2,66},{3,195},{4,68},{5,197},{6,70},{7,199},{8,72}... | collective-permute-start | bytes 258056 | tf_op jit(solution)/shard_map/ppermute | solution.py:30
  17.1 43.5 %copy-start = (f32[72,7168]{1,0:T(8,128)S(1)}, f32[72,7168]{1,0:T(8,128)}, u32[]{:S(2)}) copy-start(f32[72,7168]{1,0:T(8,128)} %params.1) | copy-start | bytes 6193156
  17.1 43.5 %copy-start.1 = (f32[72,7168]{1,0:T(8,128)S(1)}, f32[72,7168]{1,0:T(8,128)}, u32[]{:S(2)}) copy-start(f32[72,7168]{1,0:T(8,128)} %momentum.1) | copy-start | bytes 6193156
  17.1 43.5 %copy-start.5 = (s32[4,65]{1,0:T(4,128)S(1)}, s32[4,65]{1,0:T(4,128)}, u32[]{:S(2)}) copy-start(s32[4,65]{1,0:T(4,128)} %bounds.3) | copy-start | bytes 3124
  17.1 10.8 %collective-permute-start.1 = (bf16[2,24,2688]{2,1,0:T(8,128)(2,1)S(1)}, bf16[2,24,2688]{2,1,0:T(8,128)(2,1)S(1)}, u32[]{:S(2)}, u32[]{:S(2)}) collective-permute-start(bf16[2,24,2688]{2,1,0:T(8,128)(2,1)S(1)} %fusion.5), channel_id=1, source_target_pairs={{0,64},{1,193},{2,66},{3,195},{4,68},{5,197},{6,70},{7,199},{8,72}... | collective-permute-start | bytes 774152 | tf_op jit(solution)/shard_map/ppermute | solution.py:30
  19.7 13.0 %collective-permute-start.8 = (bf16[24,896]{1,0:T(8,128)(2,1)S(1)}, bf16[24,896]{1,0:T(8,128)(2,1)S(1)}, u32[]{:S(2)}, u32[]{:S(2)}) collective-permute-start(bf16[24,896]{1,0:T(8,128)(2,1)S(1)} %fusion.11), channel_id=1, source_target_pairs={{0,192},{1,65},{2,194},{3,67},{4,196},{5,69},{6,198},{7,71},{8,200... | collective-permute-start | bytes 129032 | tf_op jit(solution)/shard_map/ppermute | solution.py:30
  28.0 8.8 %collective-permute-start.2 = (bf16[24,2688]{1,0:T(8,128)(2,1)S(1)}, bf16[24,2688]{1,0:T(8,128)(2,1)S(1)}, u32[]{:S(2)}, u32[]{:S(2)}) collective-permute-start(bf16[24,2688]{1,0:T(8,128)(2,1)S(1)} %fusion.4), channel_id=1, source_target_pairs={{0,192},{1,65},{2,194},{3,67},{4,196},{5,69},{6,198},{7,71},{8,200... | collective-permute-start | bytes 387080 | tf_op jit(solution)/shard_map/ppermute | solution.py:30
  32.7 8.9 %collective-permute-start.9 = (bf16[24,896]{1,0:T(8,128)(2,1)S(1)}, bf16[24,896]{1,0:T(8,128)(2,1)S(1)}, u32[]{:S(2)}, u32[]{:S(2)}) collective-permute-start(bf16[24,896]{1,0:T(8,128)(2,1)S(1)} %fusion.10), channel_id=1, source_target_pairs={{0,192},{1,65},{2,194},{3,67},{4,196},{5,69},{6,198},{7,71},{8,200... | collective-permute-start | bytes 129032 | tf_op jit(solution)/shard_map/ppermute | solution.py:30
  36.9 12.1 %collective-permute-start.3 = (bf16[24,2688]{1,0:T(8,128)(2,1)S(1)}, bf16[24,2688]{1,0:T(8,128)(2,1)S(1)}, u32[]{:S(2)}, u32[]{:S(2)}) collective-permute-start(bf16[24,2688]{1,0:T(8,128)(2,1)S(1)} %fusion.3), channel_id=1, source_target_pairs={{0,192},{1,65},{2,194},{3,67},{4,196},{5,69},{6,198},{7,71},{8,200... | collective-permute-start | bytes 387080 | tf_op jit(solution)/shard_map/ppermute | solution.py:30
  41.6 9.9 %collective-permute-start.10 = (bf16[2,24,896]{2,1,0:T(8,128)(2,1)S(1)}, bf16[2,24,896]{2,1,0:T(8,128)(2,1)S(1)}, u32[]{:S(2)}, u32[]{:S(2)}) collective-permute-start(bf16[2,24,896]{2,1,0:T(8,128)(2,1)S(1)} %pad_maximum_fusion.3.own2), channel_id=1, source_target_pairs={{0,64},{1,193},{2,66},{3,195},{4,68},{5,197},{6,70},{7,199},{8,72}... | collective-permute-start | bytes 258056 | tf_op jit(solution)/shard_map/ppermute | solution.py:30
  49.0 10.1 %collective-permute-start.4 = (bf16[2,24,2688]{2,1,0:T(8,128)(2,1)S(1)}, bf16[2,24,2688]{2,1,0:T(8,128)(2,1)S(1)}, u32[]{:S(2)}, u32[]{:S(2)}) collective-permute-start(bf16[2,24,2688]{2,1,0:T(8,128)(2,1)S(1)} %pad_maximum_fusion.own1), channel_id=1, source_target_pairs={{0,64},{1,193},{2,66},{3,195},{4,68},{5,197},{6,70},{7,199},{8,72}... | collective-permute-start | bytes 774152 | tf_op jit(solution)/shard_map/ppermute | solution.py:30
  51.5 7.9 %collective-permute-start.11 = (bf16[4,24,896]{2,1,0:T(8,128)(2,1)S(1)}, bf16[4,24,896]{2,1,0:T(8,128)(2,1)S(1)}, u32[]{:S(2)}, u32[]{:S(2)}) collective-permute-start(bf16[4,24,896]{2,1,0:T(8,128)(2,1)S(1)} %pad_maximum_fusion.2), channel_id=1, source_target_pairs={{0,63},{1,2},{2,1},{3,4},{4,3},{5,6},{6,5},{7,8},{8,7},{9,10},{10,... | collective-permute-start | bytes 516104 | tf_op jit(solution)/shard_map/ppermute | solution.py:40
  59.1 1.5 %collective-permute-start.5 = (bf16[4,24,896]{2,1,0:T(8,128)(2,1)S(1)}, bf16[4,24,896]{2,1,0:T(8,128)(2,1)S(1)}, u32[]{:S(2)}, u32[]{:S(2)}) collective-permute-start(bf16[4,24,896]{2,1,0:T(8,128)(2,1)S(1)} %pad_maximum_fusion.1), channel_id=1, source_target_pairs={{0,1},{1,0},{2,3},{3,2},{4,5},{5,4},{6,7},{7,6},{8,9},{9,8},{10,11... | collective-permute-start | bytes 516104 | tf_op jit(solution)/shard_map/ppermute | solution.py:34

commit v3 on v0

v3 whole, which is shorter than its diff:
```python
import jax
import jax.numpy as jnp
from jax import lax
from jax.experimental import pallas as pl
from jax.experimental.pallas import tpu as pltpu
from jax.sharding import PartitionSpec as P

ROWS_DEV = 48
HALF = 12
BAND = 24
QB = 128

momentum_keep = 0.9
outer_rate = 0.7
block_eps = 1e-06

F32 = jnp.float32
BF16 = jnp.bfloat16
AXES = ("island", "fsdp")
PAIRINGS = ({0: 1, 1: 0, 2: 3, 3: 2}, {0: 3, 3: 0, 1: 2, 2: 1})


def island_swap(value, step):
    shards = lax.axis_size("fsdp")
    pairs = [
        (i * shards + j, PAIRINGS[(j + step) % 2][i] * shards + j)
        for i in range(4)
        for j in range(shards)
    ]
    return lax.ppermute(value, AXES, pairs)


def inner_swap(value):
    return lax.ppermute(value, "fsdp", [(j, j ^ 1) for j in range(lax.axis_size("fsdp"))])


def outer_swap(value):
    count = lax.axis_size("fsdp")
    pairs = [(j, (j + 1) % count if j & 1 else (j - 1) % count) for j in range(count)]
    return lax.ppermute(value, "fsdp", pairs)


def place():
    island, odd = lax.axis_index("island"), lax.axis_index("fsdp") & 1
    low, high = island & 1, island >> 1
    return jnp.where(odd == 0, low ^ high, high), jnp.where(odd == 0, high, low ^ high), odd


VMEM = pl.BlockSpec(memory_space=pltpu.VMEM)
HBM = pl.BlockSpec(memory_space=pltpu.HBM)


def local_call(body, outs, ins, *arrays, grant=2, aliases=None, scratch=(), cost=1):
    return pl.pallas_call(
        body,
        out_shape=[jax.ShapeDtypeStruct(s, d) for s, d, _ in outs],
        in_specs=ins,
        out_specs=[space for _, _, space in outs],
        scratch_shapes=scratch,
        input_output_aliases=aliases or {},
        cost_estimate=pl.CostEstimate(
            flops=cost << 20, bytes_accessed=cost << 20, transcendentals=0
        ),
        compiler_params=pltpu.CompilerParams(vmem_limit_bytes=grant << 20),
    )(*arrays)


def fill(payload, rows_scales, first, start, count, target, at=0):
    rows = pl.ds(first, BAND)
    local = pltpu.roll(rows_scales[rows, :], lax.rem(QB - start, QB), 1)
    for k in range(count):
        cols = pl.ds(pl.multiple_of((start + k) * QB, QB), QB)
        block = payload[rows, cols].astype(F32) * local[:, k : k + 1]
        target[:, (at + k) * QB : (at + k + 1) * QB] = block.astype(target.dtype)


def side_rows(odd):
    return pl.multiple_of((1 - odd) * (2 * BAND), 16), pl.multiple_of(odd * (2 * BAND), 16)


def edge_terms_body(payload_in, scales_in, bounds_in, out_send, in_send, payload, rows_scales, live,
                    scales, bounds, sems):
    _, b, c = place()
    slots, width = payload.shape
    blocks = width // QB
    half, fourth = blocks // 2, blocks // 4
    copies = [pltpu.make_async_copy(bounds_in, bounds, sems.at[0])]
    copies.append(pltpu.make_async_copy(scales_in, scales, sems.at[1]))
    for n, part in enumerate((c, 1 - c)):
        cols = pl.ds(pl.multiple_of(part * (width // 2), QB), width // 2)
        copies.append(
            pltpu.make_async_copy(payload_in.at[:, cols], payload.at[:, cols], sems.at[2 + n])
        )
    for copy in copies:
        copy.start()
    copies[0].wait()
    island, shard = lax.axis_index("island"), lax.axis_index("fsdp")
    origin = shard * ROWS_DEV - HALF
    row = lax.broadcasted_iota(jnp.int32, (slots, QB), 0) + origin
    live[...] = ((row >= bounds[island, shard]) & (row < bounds[island, shard + 1])).astype(F32)
    rows_scales[...] = jnp.zeros(rows_scales.shape, F32)
    copies[1].wait()
    rows_scales[:, :blocks] = jnp.transpose(scales[...]) * live[:, :blocks]
    inner, outer = side_rows(c)
    for copy, first, start, target in (
        (copies[2], outer, c * half, out_send),
        (copies[3], inner, (1 - c) * half, in_send),
    ):
        copy.wait()
        for u in range(2):
            fill(payload, rows_scales, first, start + (b ^ 1 ^ u) * fourth, fourth, target.at[u])


def mid_terms_body(payload, rows_scales, send, keep):
    a = place()[0]
    half = payload.shape[1] // QB // 2
    fill(payload, rows_scales, BAND, (1 - a) * half, half, send)
    fill(payload, rows_scales, BAND, a * half, half, keep)


def side_terms_body(payload, rows_scales, in_first, in_keep, out_first, out_keep):
    a, _, c = place()
    blocks = payload.shape[1] // QB
    half, fourth = blocks // 2, blocks // 4
    inner, outer = side_rows(c)
    for part, near, far in ((1 - a, in_first, out_first), (a, in_keep, out_keep)):
        fill(payload, rows_scales, inner, c * half + part * fourth, fourth, near)
        fill(payload, rows_scales, outer, (1 - c) * half + part * fourth, fourth, far)


def add_to(total, part):
    return (total.astype(F32) + part.astype(F32)).astype(total.dtype)


def reduce_band(send, keep):
    total = add_to(island_swap(send, 0), keep)
    return add_to(total, island_swap(total, 1))


def step_band(first, source, live, params, momentum, params_out, momentum_out, coded_out,
              scale_out, params_new, momentum_new, sems):
    rows = pl.ds(first, BAND)
    blocks = params.shape[1] // QB
    fourth = blocks // 4
    lane = lax.broadcasted_iota(jnp.int32, (BAND, QB), 1)
    alive = live[rows, :]
    scale_row = jnp.zeros((BAND, QB), F32)
    copies = []
    for g in range(blocks):
        cols = slice(g * QB, (g + 1) * QB)
        summed = source(g).astype(F32)
        block_scale = jnp.max(jnp.abs(summed), axis=1, keepdims=True) + block_eps
        coded = (summed * (1.0 / block_scale)).astype(BF16).astype(F32) * alive
        block_live = block_scale * alive
        delta = coded * (block_live * 0.25)
        moved = momentum_keep * momentum[rows, cols] + delta
        momentum_new[:, cols] = moved
        params_new[:, cols] = params[rows, cols] - outer_rate * (delta + momentum_keep * moved)
        coded_out[:, cols] = coded.astype(BF16)
        scale_row = jnp.where(lane == g, block_live, scale_row)
        if g % fourth == fourth - 1:
            part = slice((g + 1 - fourth) * QB, (g + 1) * QB)
            for n, (new, out) in enumerate(
                ((params_new, params_out), (momentum_new, momentum_out))
            ):
                copy = pltpu.make_async_copy(
                    new.at[:, part], out.at[rows, part], sems.at[n, g // fourth]
                )
                copy.start()
                copies.append(copy)
    scale_out[...] = scale_row
    return copies


def side_source(blocks, mine_half, own, recv, other):
    a, b, _ = place()
    half, fourth = blocks // 2, blocks // 4

    def source(g):
        part, k = g % half // fourth, g % fourth
        cols = slice(k * QB, (k + 1) * QB)
        mine = jnp.where(a == part, own[:, cols], recv[:, cols])
        theirs = other[part ^ b, :, cols]
        return jnp.where(mine_half == g // half, mine, theirs)

    return source


def mid_step_body(own, recv, live, params, momentum, params_out, momentum_out, coded, scale,
                  *scratch):
    a = place()[0]
    blocks = params.shape[1] // QB
    half = blocks // 2

    def source(g):
        cols = slice(g % half * QB, (g % half + 1) * QB)
        return jnp.where(a == g // half, own[:, cols], recv[:, cols])

    for copy in step_band(BAND, source, live, params, momentum, params_out, momentum_out, coded,
                          scale, *scratch):
        copy.wait()


def inner_step_body(own, recv, other, live, params, momentum, _p, _m, params_out, momentum_out,
                    coded, scale, *scratch):
    c = place()[2]
    blocks = params.shape[1] // QB
    source = side_source(blocks, c, own, recv, other)
    for copy in step_band(side_rows(c)[0], source, live, params, momentum, params_out,
                          momentum_out, coded, scale, *scratch):
        copy.wait()


def outer_step_body(own, recv, other, coded_mid, scale_mid, coded_in, scale_in, live, params,
                    momentum, _p, _m, params_out, momentum_out, payload_out, scales_out, payload,
                    rows_scales, scales, *scratch):
    c = place()[2]
    blocks = params.shape[1] // QB
    inner, outer = side_rows(c)
    payload[pl.ds(BAND, BAND), :] = coded_mid[...]
    payload[pl.ds(inner, BAND), :] = coded_in[...]
    rows_scales[pl.ds(BAND, BAND), :] = scale_mid[...]
    rows_scales[pl.ds(inner, BAND), :] = scale_in[...]
    source = side_source(blocks, 1 - c, own, recv, other)
    copies = step_band(outer, source, live, params, momentum, params_out, momentum_out,
                       payload.at[pl.ds(outer, BAND)], rows_scales.at[pl.ds(outer, BAND)], *scratch)
    sems = scratch[-1]
    copies.append(pltpu.make_async_copy(payload, payload_out, sems.at[2, 0]))
    copies[-1].start()
    scales[...] = jnp.transpose(rows_scales[...])[:blocks, :]
    copies.append(pltpu.make_async_copy(scales, scales_out, sems.at[2, 1]))
    copies[-1].start()
    for copy in copies:
        copy.wait()


def shards(params, momentum, payload, scales, bounds):
    slots, width = payload.shape
    half, fourth, blocks = width // 2, width // 4, width // QB
    out_send, in_send, payload_near, rows_scales, live = local_call(
        edge_terms_body,
        [
            ((2, BAND, fourth), BF16, VMEM),
            ((2, BAND, fourth), BF16, VMEM),
            ((slots, width), BF16, VMEM),
            ((slots, QB), F32, VMEM),
            ((slots, QB), F32, VMEM),
        ],
        [HBM, HBM, HBM],
        *(pltpu.with_memory_space_constraint(x, pltpu.HBM) for x in (payload, scales.T, bounds)),
        scratch=[
            pltpu.VMEM((blocks, slots), F32),
            pltpu.SMEM(bounds.shape, jnp.int32),
            pltpu.SemaphoreType.DMA((4,)),
        ],
    )
    out_recv = outer_swap(out_send)
    in_recv = inner_swap(in_send)
    near = (payload_near, rows_scales)
    mid_send, mid_keep = local_call(
        mid_terms_body, [((BAND, half), BF16, VMEM), ((BAND, half), F32, VMEM)], [VMEM] * 2, *near
    )
    in_first, in_keep, out_first, out_keep = local_call(
        side_terms_body,
        [((BAND, fourth), BF16, VMEM), ((BAND, fourth), F32, VMEM)] * 2,
        [VMEM] * 2,
        *near,
    )
    own_mid = reduce_band(mid_send, mid_keep)
    own_in = reduce_band(add_to(in_first, in_recv[0]), add_to(in_keep, in_recv[1]))
    own_out = reduce_band(add_to(out_first, out_recv[0]), add_to(out_keep, out_recv[1]))
    recv_mid = island_swap(own_mid, 0)
    recv_out = island_swap(own_out, 0)
    recv_in = island_swap(own_in, 0)
    out_other = outer_swap(jnp.stack([own_out, recv_out]))
    in_other = inner_swap(jnp.stack([own_in, recv_in]))

    whole = ((slots, width), F32, HBM)
    band = [((BAND, width), BF16, VMEM), ((BAND, QB), F32, VMEM)]
    scratch = [
        pltpu.VMEM((BAND, width), F32),
        pltpu.VMEM((BAND, width), F32),
        pltpu.SemaphoreType.DMA((3, 4)),
    ]
    state = (live, params, momentum)
    params_out, momentum_out, coded_mid, scale_mid = local_call(
        mid_step_body, [whole, whole] + band, [VMEM] * 5, own_mid, recv_mid, *state,
        grant=4, scratch=scratch, cost=24,
    )
    params_out, momentum_out, coded_in, scale_in = local_call(
        inner_step_body, [whole, whole] + band, [VMEM] * 6 + [HBM] * 2, own_in, recv_in, in_other,
        *state, params_out, momentum_out,
        grant=4, scratch=scratch, cost=4, aliases={6: 0, 7: 1},
    )
    params_out, momentum_out, payload_out, scales_out = local_call(
        outer_step_body,
        [whole, whole, ((slots, width), BF16, HBM), ((blocks, slots), F32, HBM)],
        [VMEM] * 10 + [HBM] * 2,
        own_out, recv_out, out_other, coded_mid, scale_mid, coded_in, scale_in,
        *state, params_out, momentum_out,
        grant=6, cost=4, aliases={10: 0, 11: 1},
        scratch=[
            pltpu.VMEM((slots, width), BF16),
            pltpu.VMEM((slots, QB), F32),
            pltpu.VMEM((blocks, slots), F32),
        ] + scratch,
    )
    return params_out, momentum_out, payload_out, scales_out.T


def solution(mesh):
    spec = P(("island", "fsdp"), None)
    return jax.shard_map(
        shards, mesh=mesh, in_specs=(spec,) * 4 + (P(),), out_specs=(spec,) * 4, check_vma=False
    )
```

time: 237 us -> 54.4 us (0.23)
  the two profiles are of different devices: /device:TPU:8 before, /device:TPU:0 now
where the time goes in v3:
time: 54.4 us; the launch traced here: 54.3 us
  starting transfers between devices  33.2 us (61%)
  waiting for transfers between devices  12.9 us (24%)
  Pallas kernels  7.22 us (13%)
  between operations  0.76 us (1%)
    ppermute x9, starting transfers between devices, island_swap(): return lax.ppermute(value, AXES, pairs)  26.8 us
    ppermute x9, waiting for transfers between devices, island_swap(): return lax.ppermute(value, AXES, pairs)  8.48 us
    pallas_call x6, Pallas kernels, local_call(): pl.pallas_call(body, out_shape=[jax.ShapeDtypeStruct(s, d) for s, d, _ in...  7.22 us
    ppermute x2, starting transfers between devices, outer_swap(): return lax.ppermute(value, 'fsdp', pairs)  6.19 us
    ppermute x2, waiting for transfers between devices, outer_swap(): return lax.ppermute(value, 'fsdp', pairs)  4.37 us
  transfers between devices with their start and end apart: 13, of which 6 were waited for; matrix products, arithmetic and copies ran while one was open for 1% of the time, Pallas kernels for 7%

profile of v3, /device:TPU:0, one launch (start us, length us, event | category | flops | bytes accessed | tf_op | source)
XLA Modules:
  0.0 54.3 jit_solution(6192815738739137853)
XLA Ops:
  0.6 1.6 %shard_map.84 = (bf16[2,24,1792]{2,1,0:T(8,128)(2,1)S(1)}, bf16[2,24,1792]{2,1,0:T(8,128)(2,1)S(1)}, bf16[72,7168]{1,0:T(8,128)(2,1)S(1)}, f32[72,128]{1,0:T(8,128)S(1)}, f32[72,128]{1,0:T(8,128)S(1)}) custom-call(bf16[72,7168]{1,0:T(8,128)(2,1)} %payload_in.1, f32[56,72]{1,0:T(8,128)} %bitcast.30, s32[4,65]{1,0:T(4,128)} %bounds_in.1), custom_call_target="tpu_custom_call" | custom-call | flops 1048576 | bytes 1048576 | tf_op jit(solution)/shard_map/pallas_call | solution.py:54
  2.3 0.1 collective-permute-start.8
  2.4 4.9 %collective-permute-start = (bf16[2,24,1792]{2,1,0:T(8,128)(2,1)S(1)}, bf16[2,24,1792]{2,1,0:T(8,128)(2,1)S(1)}, u32[]{:S(2)}, u32[]{:S(2)}) collective-permute-start(bf16[2,24,1792]{2,1,0:T(8,128)(2,1)S(1)} %get-tuple-element.30), channel_id=1, source_target_pairs={{0,63},{1,2},{2,1},{3,4},{4,3},{5,6},{6,5},{7,8},{8,7},{9,10},{10,... | collective-permute-start | bytes 516104 | tf_op jit(solution)/shard_map/ppermute | solution.py:40
  7.3 0.5 shard_map.86
  7.8 3.4 %collective-permute-start.5 = (bf16[24,3584]{1,0:T(8,128)(2,1)S(1)}, bf16[24,3584]{1,0:T(8,128)(2,1)S(1)}, u32[]{:S(2)}, u32[]{:S(2)}) collective-permute-start(bf16[24,3584]{1,0:T(8,128)(2,1)S(1)} %get-tuple-element.32), channel_id=1, source_target_pairs={{0,64},{1,193},{2,66},{3,195},{4,68},{5,197},{6,70},{7,199},{8,72}... | collective-permute-start | bytes 516104 | tf_op jit(solution)/shard_map/ppermute | solution.py:30
  11.1 0.0 copy-start.1
  11.1 0.5 shard_map.85
  11.7 0.0 copy-start
  11.7 0.0 collective-permute-done.8
  11.7 0.1 collective-permute-start.9
  11.8 0.0 collective-permute-done
  11.9 6.8 %collective-permute-start.1 = (bf16[24,1792]{1,0:T(8,128)(2,1)S(1)}, bf16[24,1792]{1,0:T(8,128)(2,1)S(1)}, u32[]{:S(2)}, u32[]{:S(2)}) collective-permute-start(bf16[24,1792]{1,0:T(8,128)(2,1)S(1)} %fusion.5), channel_id=1, source_target_pairs={{0,64},{1,193},{2,66},{3,195},{4,68},{5,197},{6,70},{7,199},{8,72}... | collective-permute-start | bytes 258056 | tf_op jit(solution)/shard_map/ppermute | solution.py:30
  18.7 0.0 collective-permute-done.5
  18.7 3.3 %collective-permute-start.6 = (bf16[24,3584]{1,0:T(8,128)(2,1)S(1)}, bf16[24,3584]{1,0:T(8,128)(2,1)S(1)}, u32[]{:S(2)}, u32[]{:S(2)}) collective-permute-start(bf16[24,3584]{1,0:T(8,128)(2,1)S(1)} %add_convert_fusion.1), channel_id=1, source_target_pairs={{0,192},{1,65},{2,194},{3,67},{4,196},{5,69},{6,198},{7,71},{8,200... | collective-permute-start | bytes 516104 | tf_op jit(solution)/shard_map/ppermute | solution.py:30
  22.1 0.0 collective-permute-done.9
  22.1 1.0 %collective-permute-start.10 = (bf16[24,1792]{1,0:T(8,128)(2,1)S(1)}, bf16[24,1792]{1,0:T(8,128)(2,1)S(1)}, u32[]{:S(2)}, u32[]{:S(2)}) collective-permute-start(bf16[24,1792]{1,0:T(8,128)(2,1)S(1)} %fusion.1), channel_id=1, source_target_pairs={{0,192},{1,65},{2,194},{3,67},{4,196},{5,69},{6,198},{7,71},{8,200... | collective-permute-start | bytes 258056 | tf_op jit(solution)/shard_map/ppermute | solution.py:30
  23.1 1.4 %collective-permute-done.1 = bf16[24,1792]{1,0:T(8,128)(2,1)S(1)} collective-permute-done((bf16[24,1792]{1,0:T(8,128)(2,1)S(1)}, bf16[24,1792]{1,0:T(8,128)(2,1)S(1)}, u32[]{:S(2)}, u32[]{:S(2)}) %collective-permute-start.1) | collective-permute-done | bytes 86048 | tf_op jit(solution)/shard_map/ppermute | solution.py:30
  24.6 3.8 %collective-permute-start.2 = (bf16[24,1792]{1,0:T(8,128)(2,1)S(1)}, bf16[24,1792]{1,0:T(8,128)(2,1)S(1)}, u32[]{:S(2)}, u32[]{:S(2)}) collective-permute-start(bf16[24,1792]{1,0:T(8,128)(2,1)S(1)} %fusion.4), channel_id=1, source_target_pairs={{0,192},{1,65},{2,194},{3,67},{4,196},{5,69},{6,198},{7,71},{8,200... | collective-permute-start | bytes 258056 | tf_op jit(solution)/shard_map/ppermute | solution.py:30
  28.4 0.6 %collective-permute-done.10 = bf16[24,1792]{1,0:T(8,128)(2,1)S(1)} collective-permute-done((bf16[24,1792]{1,0:T(8,128)(2,1)S(1)}, bf16[24,1792]{1,0:T(8,128)(2,1)S(1)}, u32[]{:S(2)}, u32[]{:S(2)}) %collective-permute-start.10) | collective-permute-done | bytes 86048 | tf_op jit(solution)/shard_map/ppermute | solution.py:30
  29.1 2.7 %collective-permute-start.11 = (bf16[24,1792]{1,0:T(8,128)(2,1)S(1)}, bf16[24,1792]{1,0:T(8,128)(2,1)S(1)}, u32[]{:S(2)}, u32[]{:S(2)}) collective-permute-start(bf16[24,1792]{1,0:T(8,128)(2,1)S(1)} %add_convert_fusion.2.own), channel_id=1, source_target_pairs={{0,64},{1,193},{2,66},{3,195},{4,68},{5,197},{6,70},{7,199},{8,72}... | collective-permute-start | bytes 258056 | tf_op jit(solution)/shard_map/ppermute | solution.py:30
  31.8 1.4 %collective-permute-done.2 = bf16[24,1792]{1,0:T(8,128)(2,1)S(1)} collective-permute-done((bf16[24,1792]{1,0:T(8,128)(2,1)S(1)}, bf16[24,1792]{1,0:T(8,128)(2,1)S(1)}, u32[]{:S(2)}, u32[]{:S(2)}) %collective-permute-start.2) | collective-permute-done | bytes 86048 | tf_op jit(solution)/shard_map/ppermute | solution.py:30
  33.2 5.5 %collective-permute-start.3 = (bf16[24,1792]{1,0:T(8,128)(2,1)S(1)}, bf16[24,1792]{1,0:T(8,128)(2,1)S(1)}, u32[]{:S(2)}, u32[]{:S(2)}) collective-permute-start(bf16[24,1792]{1,0:T(8,128)(2,1)S(1)} %add_convert_fusion.3.own), channel_id=1, source_target_pairs={{0,64},{1,193},{2,66},{3,195},{4,68},{5,197},{6,70},{7,199},{8,72}... | collective-permute-start | bytes 258056 | tf_op jit(solution)/shard_map/ppermute | solution.py:30
  38.8 0.0 collective-permute-done.6
  38.8 0.1 collective-permute-start.7
  38.9 0.0 collective-permute-done.11.recv
  38.9 0.1 collective-permute-start.12
  39.0 4.3 %collective-permute-done.3.recv = bf16[24,1792]{1,0:T(8,128)(2,1)S(1)} collective-permute-done((bf16[24,1792]{1,0:T(8,128)(2,1)S(1)}, bf16[24,1792]{1,0:T(8,128)(2,1)S(1)}, u32[]{:S(2)}, u32[]{:S(2)}) %collective-permute-start.3) | collective-permute-done | bytes 86048 | tf_op jit(solution)/shard_map/ppermute | solution.py:30
  43.4 1.3 %collective-permute-start.4 = (bf16[2,24,1792]{2,1,0:T(8,128)(2,1)S(1)}, bf16[2,24,1792]{2,1,0:T(8,128)(2,1)S(1)}, u32[]{:S(2)}, u32[]{:S(2)}) collective-permute-start(bf16[2,24,1792]{2,1,0:T(8,128)(2,1)S(1)} %pad_maximum_fusion), channel_id=1, source_target_pairs={{0,63},{1,2},{2,1},{3,4},{4,3},{5,6},{6,5},{7,8},{8,7},{9,10},{10,... | collective-permute-start | bytes 516104 | tf_op jit(solution)/shard_map/ppermute | solution.py:40
  44.6 0.7 %collective-permute-done.7.recv = bf16[24,3584]{1,0:T(8,128)(2,1)S(1)} collective-permute-done((bf16[24,3584]{1,0:T(8,128)(2,1)S(1)}, bf16[24,3584]{1,0:T(8,128)(2,1)S(1)}, u32[]{:S(2)}, u32[]{:S(2)}) %collective-permute-start.7) | collective-permute-done | bytes 172064 | tf_op jit(solution)/shard_map/ppermute | solution.py:30
  45.3 0.0 copy-done.1
  45.3 0.0 copy-done
  45.3 1.4 %shard_map.87 = (f32[72,7168]{1,0:T(8,128)}, f32[72,7168]{1,0:T(8,128)}, bf16[24,7168]{1,0:T(8,128)(2,1)S(1)}, f32[24,128]{1,0:T(8,128)S(1)}) custom-call(bf16[24,3584]{1,0:T(8,128)(2,1)S(1)} %add_convert_fusion.own, bf16[24,3584]{1,0:T(8,128)(2,1)S(1)} %collective-permute-done.7.recv, f32[72,128]{1,0:T(8,128)S(1)} %get-tuple-element.34.live, ...), custom_call_target="tpu_custom_call" | custom-call | flops 25165824 | bytes 25165824 | tf_op jit(solution)/shard_map/pallas_call | solution.py:54
  46.7 0.0 collective-permute-done.12.other
  46.7 1.4 %shard_map.88 = (f32[72,7168]{1,0:T(8,128)}, f32[72,7168]{1,0:T(8,128)}, bf16[24,7168]{1,0:T(8,128)(2,1)S(1)}, f32[24,128]{1,0:T(8,128)S(1)}) custom-call(bf16[24,1792]{1,0:T(8,128)(2,1)S(1)} %add_convert_fusion.2.own, bf16[24,1792]{1,0:T(8,128)(2,1)S(1)} %collective-permute-done.11.recv, ...), custom_call_target="tpu_custom_call", output_to_operand_aliasing={{0}: (6, {}), {1}: (7, {})} | custom-call | flops 4194304 | bytes 4194304 | tf_op jit(solution)/shard_map/pallas_call | solution.py:54
  48.1 4.4 %collective-permute-done.4.other = bf16[2,24,1792]{2,1,0:T(8,128)(2,1)S(1)} collective-permute-done((bf16[2,24,1792]{2,1,0:T(8,128)(2,1)S(1)}, bf16[2,24,1792]{2,1,0:T(8,128)(2,1)S(1)}, u32[]{:S(2)}, u32[]{:S(2)}) %collective-permute-start.4) | collective-permute-done | bytes 172064 | tf_op jit(solution)/shard_map/ppermute | solution.py:40
  52.5 1.8 %shard_map.89 = (f32[72,7168]{1,0:T(8,128)}, f32[72,7168]{1,0:T(8,128)}, bf16[72,7168]{1,0:T(8,128)(2,1)}, f32[56,72]{1,0:T(8,128)}) custom-call(bf16[24,1792]{1,0:T(8,128)(2,1)S(1)} %add_convert_fusion.3.own, bf16[24,1792]{1,0:T(8,128)(2,1)S(1)} %collective-permute-done.3.recv, ...), custom_call_target="tpu_custom_call", output_to_operand_aliasing={{0}: (10, {}), {1}: (11, {})} | custom-call | flops 4194304 | bytes 4194304 | tf_op jit(solution)/shard_map/pallas_call | solution.py:54
  (10 shorter events, 0.3 us)
Async XLA Ops:
  2.3 9.4 %collective-permute-start.8 = (bf16[2,24,1792]{2,1,0:T(8,128)(2,1)S(1)}, bf16[2,24,1792]{2,1,0:T(8,128)(2,1)S(1)}, u32[]{:S(2)}, u32[]{:S(2)}) collective-permute-start(bf16[2,24,1792]{2,1,0:T(8,128)(2,1)S(1)} %get-tuple-element.38), channel_id=1, source_target_pairs={{0,1},{1,0},{2,3},{3,2},{4,5},{5,4},{6,7},{7,6},{8,9},{9,8},{10,11... | collective-permute-start | bytes 516104 | tf_op jit(solution)/shard_map/ppermute | solution.py:34
  2.4 9.5 %collective-permute-start = (bf16[2,24,1792]{2,1,0:T(8,128)(2,1)S(1)}, bf16[2,24,1792]{2,1,0:T(8,128)(2,1)S(1)}, u32[]{:S(2)}, u32[]{:S(2)}) collective-permute-start(bf16[2,24,1792]{2,1,0:T(8,128)(2,1)S(1)} %get-tuple-element.30), channel_id=1, source_target_pairs={{0,63},{1,2},{2,1},{3,4},{4,3},{5,6},{6,5},{7,8},{8,7},{9,10},{10,... | collective-permute-start | bytes 516104 | tf_op jit(solution)/shard_map/ppermute | solution.py:40
  7.8 10.9 %collective-permute-start.5 = (bf16[24,3584]{1,0:T(8,128)(2,1)S(1)}, bf16[24,3584]{1,0:T(8,128)(2,1)S(1)}, u32[]{:S(2)}, u32[]{:S(2)}) collective-permute-start(bf16[24,3584]{1,0:T(8,128)(2,1)S(1)} %get-tuple-element.32), channel_id=1, source_target_pairs={{0,64},{1,193},{2,66},{3,195},{4,68},{5,197},{6,70},{7,199},{8,72}... | collective-permute-start | bytes 516104 | tf_op jit(solution)/shard_map/ppermute | solution.py:30
  11.1 34.2 %copy-start.1 = (f32[72,7168]{1,0:T(8,128)S(1)}, f32[72,7168]{1,0:T(8,128)}, u32[]{:S(2)}) copy-start(f32[72,7168]{1,0:T(8,128)} %momentum.5) | copy-start | bytes 6193156
  11.7 33.6 %copy-start = (f32[72,7168]{1,0:T(8,128)S(1)}, f32[72,7168]{1,0:T(8,128)}, u32[]{:S(2)}) copy-start(f32[72,7168]{1,0:T(8,128)} %params.5) | copy-start | bytes 6193156
  11.7 10.3 %collective-permute-start.9 = (bf16[24,1792]{1,0:T(8,128)(2,1)S(1)}, bf16[24,1792]{1,0:T(8,128)(2,1)S(1)}, u32[]{:S(2)}, u32[]{:S(2)}) collective-permute-start(bf16[24,1792]{1,0:T(8,128)(2,1)S(1)} %fusion.2), channel_id=1, source_target_pairs={{0,64},{1,193},{2,66},{3,195},{4,68},{5,197},{6,70},{7,199},{8,72}... | collective-permute-start | bytes 258056 | tf_op jit(solution)/shard_map/ppermute | solution.py:30
  11.9 12.7 %collective-permute-start.1 = (bf16[24,1792]{1,0:T(8,128)(2,1)S(1)}, bf16[24,1792]{1,0:T(8,128)(2,1)S(1)}, u32[]{:S(2)}, u32[]{:S(2)}) collective-permute-start(bf16[24,1792]{1,0:T(8,128)(2,1)S(1)} %fusion.5), channel_id=1, source_target_pairs={{0,64},{1,193},{2,66},{3,195},{4,68},{5,197},{6,70},{7,199},{8,72}... | collective-permute-start | bytes 258056 | tf_op jit(solution)/shard_map/ppermute | solution.py:30
  18.7 20.0 %collective-permute-start.6 = (bf16[24,3584]{1,0:T(8,128)(2,1)S(1)}, bf16[24,3584]{1,0:T(8,128)(2,1)S(1)}, u32[]{:S(2)}, u32[]{:S(2)}) collective-permute-start(bf16[24,3584]{1,0:T(8,128)(2,1)S(1)} %add_convert_fusion.1), channel_id=1, source_target_pairs={{0,192},{1,65},{2,194},{3,67},{4,196},{5,69},{6,198},{7,71},{8,200... | collective-permute-start | bytes 516104 | tf_op jit(solution)/shard_map/ppermute | solution.py:30
  22.1 6.9 %collective-permute-start.10 = (bf16[24,1792]{1,0:T(8,128)(2,1)S(1)}, bf16[24,1792]{1,0:T(8,128)(2,1)S(1)}, u32[]{:S(2)}, u32[]{:S(2)}) collective-permute-start(bf16[24,1792]{1,0:T(8,128)(2,1)S(1)} %fusion.1), channel_id=1, source_target_pairs={{0,192},{1,65},{2,194},{3,67},{4,196},{5,69},{6,198},{7,71},{8,200... | collective-permute-start | bytes 258056 | tf_op jit(solution)/shard_map/ppermute | solution.py:30
  24.6 8.6 %collective-permute-start.2 = (bf16[24,1792]{1,0:T(8,128)(2,1)S(1)}, bf16[24,1792]{1,0:T(8,128)(2,1)S(1)}, u32[]{:S(2)}, u32[]{:S(2)}) collective-permute-start(bf16[24,1792]{1,0:T(8,128)(2,1)S(1)} %fusion.4), channel_id=1, source_target_pairs={{0,192},{1,65},{2,194},{3,67},{4,196},{5,69},{6,198},{7,71},{8,200... | collective-permute-start | bytes 258056 | tf_op jit(solution)/shard_map/ppermute | solution.py:30
  29.1 9.8 %collective-permute-start.11 = (bf16[24,1792]{1,0:T(8,128)(2,1)S(1)}, bf16[24,1792]{1,0:T(8,128)(2,1)S(1)}, u32[]{:S(2)}, u32[]{:S(2)}) collective-permute-start(bf16[24,1792]{1,0:T(8,128)(2,1)S(1)} %add_convert_fusion.2.own), channel_id=1, source_target_pairs={{0,64},{1,193},{2,66},{3,195},{4,68},{5,197},{6,70},{7,199},{8,72}... | collective-permute-start | bytes 258056 | tf_op jit(solution)/shard_map/ppermute | solution.py:30
  33.2 10.1 %collective-permute-start.3 = (bf16[24,1792]{1,0:T(8,128)(2,1)S(1)}, bf16[24,1792]{1,0:T(8,128)(2,1)S(1)}, u32[]{:S(2)}, u32[]{:S(2)}) collective-permute-start(bf16[24,1792]{1,0:T(8,128)(2,1)S(1)} %add_convert_fusion.3.own), channel_id=1, source_target_pairs={{0,64},{1,193},{2,66},{3,195},{4,68},{5,197},{6,70},{7,199},{8,72}... | collective-permute-start | bytes 258056 | tf_op jit(solution)/shard_map/ppermute | solution.py:30
  38.8 6.5 %collective-permute-start.7 = (bf16[24,3584]{1,0:T(8,128)(2,1)S(1)}, bf16[24,3584]{1,0:T(8,128)(2,1)S(1)}, u32[]{:S(2)}, u32[]{:S(2)}) collective-permute-start(bf16[24,3584]{1,0:T(8,128)(2,1)S(1)} %add_convert_fusion.own), channel_id=1, source_target_pairs={{0,64},{1,193},{2,66},{3,195},{4,68},{5,197},{6,70},{7,199},{8,72}... | collective-permute-start | bytes 516104 | tf_op jit(solution)/shard_map/ppermute | solution.py:30
  38.9 7.8 %collective-permute-start.12 = (bf16[2,24,1792]{2,1,0:T(8,128)(2,1)S(1)}, bf16[2,24,1792]{2,1,0:T(8,128)(2,1)S(1)}, u32[]{:S(2)}, u32[]{:S(2)}) collective-permute-start(bf16[2,24,1792]{2,1,0:T(8,128)(2,1)S(1)} %pad_maximum_fusion.1), channel_id=1, source_target_pairs={{0,1},{1,0},{2,3},{3,2},{4,5},{5,4},{6,7},{7,6},{8,9},{9,8},{10,11... | collective-permute-start | bytes 516104 | tf_op jit(solution)/shard_map/ppermute | solution.py:34
  43.4 9.1 %collective-permute-start.4 = (bf16[2,24,1792]{2,1,0:T(8,128)(2,1)S(1)}, bf16[2,24,1792]{2,1,0:T(8,128)(2,1)S(1)}, u32[]{:S(2)}, u32[]{:S(2)}) collective-permute-start(bf16[2,24,1792]{2,1,0:T(8,128)(2,1)S(1)} %pad_maximum_fusion), channel_id=1, source_target_pairs={{0,63},{1,2},{2,1},{3,4},{4,3},{5,6},{6,5},{7,8},{8,7},{9,10},{10,... | collective-permute-start | bytes 516104 | tf_op jit(solution)/shard_map/ppermute | solution.py:40

commit v4 on v3

--- a/solution.py
+++ b/solution.py
@@ -36,8 +36,13 @@
 
 def outer_swap(value):
     count = lax.axis_size("fsdp")
-    pairs = [(j, (j + 1) % count if j & 1 else (j - 1) % count) for j in range(count)]
-    return lax.ppermute(value, "fsdp", pairs)
+    pairs = []
+    for i in range(4):
+        for j in range(count):
+            near = j + 1 if j & 1 else j - 1
+            inside = 0 <= near < count
+            pairs.append((i * count + j, i * count + near if inside else PAIRINGS[0][i] * count + j))
+    return jnp.where(at_end(), value, lax.ppermute(value, AXES, pairs))
 
 
 def place():
@@ -65,22 +70,32 @@
     )(*arrays)
 
 
-def fill(payload, rows_scales, first, start, count, target, at=0):
+def at_end():
+    shard = lax.axis_index("fsdp")
+    return (shard == 0) | (shard == lax.axis_size("fsdp") - 1)
+
+
+def turned(block):
+    swapped = jnp.concatenate([block[HALF:], block[:HALF]])
+    return jnp.where(at_end(), swapped, block)
+
+
+def fill(payload, rows_scales, first, start, count, target, turn=lambda block: block):
     rows = pl.ds(first, BAND)
     local = pltpu.roll(rows_scales[rows, :], lax.rem(QB - start, QB), 1)
     for k in range(count):
         cols = pl.ds(pl.multiple_of((start + k) * QB, QB), QB)
         block = payload[rows, cols].astype(F32) * local[:, k : k + 1]
-        target[:, (at + k) * QB : (at + k + 1) * QB] = block.astype(target.dtype)
+        target[:, k * QB : (k + 1) * QB] = turn(block).astype(target.dtype)
 
 
 def side_rows(odd):
     return pl.multiple_of((1 - odd) * (2 * BAND), 16), pl.multiple_of(odd * (2 * BAND), 16)
 
 
-def edge_terms_body(payload_in, scales_in, bounds_in, out_send, in_send, payload, rows_scales, live,
-                    scales, bounds, sems):
-    _, b, c = place()
+def outer_terms_body(payload_in, scales_in, bounds_in, out_send, payload, rows_scales, live, scales,
+                     bounds, sems):
+    a, b, c = place()
     slots, width = payload.shape
     blocks = width // QB
     half, fourth = blocks // 2, blocks // 4
@@ -101,19 +116,21 @@
     rows_scales[...] = jnp.zeros(rows_scales.shape, F32)
     copies[1].wait()
     rows_scales[:, :blocks] = jnp.transpose(scales[...]) * live[:, :blocks]
-    inner, outer = side_rows(c)
-    for copy, first, start, target in (
-        (copies[2], outer, c * half, out_send),
-        (copies[3], inner, (1 - c) * half, in_send),
-    ):
-        copy.wait()
-        for u in range(2):
-            fill(payload, rows_scales, first, start + (b ^ 1 ^ u) * fourth, fourth, target.at[u])
-
-
-def mid_terms_body(payload, rows_scales, send, keep):
-    a = place()[0]
-    half = payload.shape[1] // QB // 2
+    outer = side_rows(c)[1]
+    copies[2].wait()
+    for u in range(2):
+        part = (jnp.where(at_end(), a, b) ^ 1 ^ u) * fourth
+        fill(payload, rows_scales, outer, c * half + part, fourth, out_send.at[u], turned)
+    copies[3].wait()
+
+
+def mid_terms_body(payload, rows_scales, in_send, send, keep):
+    a, b, c = place()
+    blocks = payload.shape[1] // QB
+    half, fourth = blocks // 2, blocks // 4
+    for u in range(2):
+        start = (1 - c) * half + (b ^ 1 ^ u) * fourth
+        fill(payload, rows_scales, side_rows(c)[0], start, fourth, in_send.at[u])
     fill(payload, rows_scales, BAND, (1 - a) * half, half, send)
     fill(payload, rows_scales, BAND, a * half, half, keep)
 
@@ -132,9 +149,8 @@
     return (total.astype(F32) + part.astype(F32)).astype(total.dtype)
 
 
-def reduce_band(send, keep):
-    total = add_to(island_swap(send, 0), keep)
-    return add_to(total, island_swap(total, 1))
+def after(value, *others):
+    return lax.optimization_barrier((value, others))[0]
 
 
 def step_band(first, source, live, params, momentum, params_out, momentum_out, coded_out,
@@ -148,7 +164,7 @@
     copies = []
     for g in range(blocks):
         cols = slice(g * QB, (g + 1) * QB)
-        summed = source(g).astype(F32)
+        summed = source(g)
         block_scale = jnp.max(jnp.abs(summed), axis=1, keepdims=True) + block_eps
         coded = (summed * (1.0 / block_scale)).astype(BF16).astype(F32) * alive
         block_live = block_scale * alive
@@ -172,16 +188,16 @@
     return copies
 
 
-def side_source(blocks, mine_half, own, recv, other):
-    a, b, _ = place()
+def side_source(blocks, mine_half, near_part, own, recv, near, far, turn=lambda block: block):
+    a = place()[0]
     half, fourth = blocks // 2, blocks // 4
 
     def source(g):
         part, k = g % half // fourth, g % fourth
         cols = slice(k * QB, (k + 1) * QB)
-        mine = jnp.where(a == part, own[:, cols], recv[:, cols])
-        theirs = other[part ^ b, :, cols]
-        return jnp.where(mine_half == g // half, mine, theirs)
+        mine = jnp.where(a == part, own[:, cols], recv[:, cols]).astype(F32)
+        theirs = jnp.where(near_part == part, near[:, cols], far[:, cols]).astype(F32)
+        return jnp.where(mine_half == g // half, mine, turn(theirs))
 
     return source
 
@@ -194,7 +210,7 @@
 
     def source(g):
         cols = slice(g % half * QB, (g % half + 1) * QB)
-        return jnp.where(a == g // half, own[:, cols], recv[:, cols])
+        return jnp.where(a == g // half, own[:, cols], recv[:, cols]).astype(F32)
 
     for copy in step_band(BAND, source, live, params, momentum, params_out, momentum_out, coded,
                           scale, *scratch):
@@ -203,9 +219,9 @@
 
 def inner_step_body(own, recv, other, live, params, momentum, _p, _m, params_out, momentum_out,
                     coded, scale, *scratch):
-    c = place()[2]
+    _, b, c = place()
     blocks = params.shape[1] // QB
-    source = side_source(blocks, c, own, recv, other)
+    source = side_source(blocks, c, b, own, recv, other.at[0], other.at[1])
     for copy in step_band(side_rows(c)[0], source, live, params, momentum, params_out,
                           momentum_out, coded, scale, *scratch):
         copy.wait()
@@ -214,14 +230,15 @@
 def outer_step_body(own, recv, other, coded_mid, scale_mid, coded_in, scale_in, live, params,
                     momentum, _p, _m, params_out, momentum_out, payload_out, scales_out, payload,
                     rows_scales, scales, *scratch):
-    c = place()[2]
+    a, b, c = place()
     blocks = params.shape[1] // QB
     inner, outer = side_rows(c)
     payload[pl.ds(BAND, BAND), :] = coded_mid[...]
     payload[pl.ds(inner, BAND), :] = coded_in[...]
     rows_scales[pl.ds(BAND, BAND), :] = scale_mid[...]
     rows_scales[pl.ds(inner, BAND), :] = scale_in[...]
-    source = side_source(blocks, 1 - c, own, recv, other)
+    source = side_source(blocks, 1 - c, jnp.where(at_end(), a, b), own, recv, other.at[0], other.at[1],
+                         turned)
     copies = step_band(outer, source, live, params, momentum, params_out, momentum_out,
                        payload.at[pl.ds(outer, BAND)], rows_scales.at[pl.ds(outer, BAND)], *scratch)
     sems = scratch[-1]
@@ -237,10 +254,9 @@
 def shards(params, momentum, payload, scales, bounds):
     slots, width = payload.shape
     half, fourth, blocks = width // 2, width // 4, width // QB
-    out_send, in_send, payload_near, rows_scales, live = local_call(
-        edge_terms_body,
+    out_send, payload_near, rows_scales, live = local_call(
+        outer_terms_body,
         [
-            ((2, BAND, fourth), BF16, VMEM),
             ((2, BAND, fourth), BF16, VMEM),
             ((slots, width), BF16, VMEM),
             ((slots, QB), F32, VMEM),
@@ -255,24 +271,38 @@
         ],
     )
     out_recv = outer_swap(out_send)
+    near = (payload_near, rows_scales)
+    in_send, mid_send, mid_keep = local_call(
+        mid_terms_body,
+        [
+            ((2, BAND, fourth), BF16, VMEM),
+            ((BAND, half), BF16, VMEM),
+            ((BAND, half), F32, VMEM),
+        ],
+        [VMEM] * 2,
+        *near,
+    )
     in_recv = inner_swap(in_send)
-    near = (payload_near, rows_scales)
-    mid_send, mid_keep = local_call(
-        mid_terms_body, [((BAND, half), BF16, VMEM), ((BAND, half), F32, VMEM)], [VMEM] * 2, *near
-    )
     in_first, in_keep, out_first, out_keep = local_call(
         side_terms_body,
         [((BAND, fourth), BF16, VMEM), ((BAND, fourth), F32, VMEM)] * 2,
         [VMEM] * 2,
         *near,
     )
-    own_mid = reduce_band(mid_send, mid_keep)
-    own_in = reduce_band(add_to(in_first, in_recv[0]), add_to(in_keep, in_recv[1]))
-    own_out = reduce_band(add_to(out_first, out_recv[0]), add_to(out_keep, out_recv[1]))
+    mid = add_to(island_swap(mid_send, 0), mid_keep)
+    out_send, out_keep = add_to(out_first, out_recv[0]), add_to(out_keep, out_recv[1])
+    out = add_to(island_swap(out_send, 0), out_keep)
+    in_send, in_keep = add_to(in_first, in_recv[0]), add_to(in_keep, in_recv[1])
+    inn = add_to(island_swap(in_send, 0), in_keep)
+    mid = after(mid, in_send)
+    own_mid = add_to(mid, island_swap(mid, 1))
+    own_out = add_to(out, island_swap(out, 1))
+    own_in = add_to(inn, island_swap(inn, 1))
     recv_mid = island_swap(own_mid, 0)
+    own_in = after(own_in, own_mid)
     recv_out = island_swap(own_out, 0)
+    out_other = outer_swap(jnp.stack([own_out, recv_out]))
     recv_in = island_swap(own_in, 0)
-    out_other = outer_swap(jnp.stack([own_out, recv_out]))
     in_other = inner_swap(jnp.stack([own_in, recv_in]))
 
     whole = ((slots, width), F32, HBM)

time: 54.4 us -> 51.5 us (0.947)
  the two profiles are of different devices: /device:TPU:0 before, /device:TPU:8 now
where the time goes in v4:
time: 51.5 us; the launch traced here: 51.4 us
  starting transfers between devices  36 us (70%)
  Pallas kernels  7.29 us (14%)
  waiting for transfers between devices  6.93 us (13%)
  between operations  0.8 us (2%)
    ppermute x9, starting transfers between devices, island_swap(): return lax.ppermute(value, AXES, pairs)  31.4 us
    pallas_call x6, Pallas kernels, local_call(): pl.pallas_call(body, out_shape=[jax.ShapeDtypeStruct(s, d) for s, d, _ in...  7.29 us
    ppermute x2, waiting for transfers between devices, outer_swap(): return jnp.where(at_end(), value, lax.ppermute(value, AXES, pairs))  3.84 us
    ppermute x2, starting transfers between devices, outer_swap(): return jnp.where(at_end(), value, lax.ppermute(value, AXES, pairs))  3.62 us
    ppermute x9, waiting for transfers between devices, island_swap(): return lax.ppermute(value, AXES, pairs)  3.08 us
  transfers between devices with their start and end apart: 13, of which 3 were waited for; matrix products, arithmetic and copies ran while one was open for 1% of the time, Pallas kernels for 5%

profile of v4, /device:TPU:8, one launch (start us, length us, event | category | flops | bytes accessed | tf_op | source)
XLA Modules:
  0.0 51.4 jit_solution(10469640959562700752)
XLA Ops:
  0.6 1.4 %shard_map.84 = (bf16[2,24,1792]{2,1,0:T(8,128)(2,1)S(1)}, bf16[72,7168]{1,0:T(8,128)(2,1)S(1)}, f32[72,128]{1,0:T(8,128)S(1)}, f32[72,128]{1,0:T(8,128)S(1)}) custom-call(bf16[72,7168]{1,0:T(8,128)(2,1)} %payload_in.1, f32[56,72]{1,0:T(8,128)} %bitcast.32, s32[4,65]{1,0:T(4,128)} %bounds_in.1), custom_call_target="tpu_custom_call" | custom-call | flops 1048576 | bytes 1048576 | tf_op jit(solution)/shard_map/pallas_call | solution.py:59
  2.0 3.5 %collective-permute-start = (bf16[2,24,1792]{2,1,0:T(8,128)(2,1)S(1)}, bf16[2,24,1792]{2,1,0:T(8,128)(2,1)S(1)}, u32[]{:S(2)}, u32[]{:S(2)}) collective-permute-start(bf16[2,24,1792]{2,1,0:T(8,128)(2,1)S(1)} %get-tuple-element.32), channel_id=1, source_target_pairs={{0,64},{1,2},{2,1},{3,4},{4,3},{5,6},{6,5},{7,8},{8,7},{9,10},{10,... | collective-permute-start | bytes 516104 | tf_op jit(solution)/shard_map/ppermute | solution.py:45
  5.5 0.7 %shard_map.86 = (bf16[2,24,1792]{2,1,0:T(8,128)(2,1)S(1)}, bf16[24,3584]{1,0:T(8,128)(2,1)S(1)}, f32[24,3584]{1,0:T(8,128)S(1)}) custom-call(bf16[72,7168]{1,0:T(8,128)(2,1)S(1)} %get-tuple-element.29.payload, f32[72,128]{1,0:T(8,128)S(1)} %get-tuple-element.30.rows_scales), custom_call_target="tpu_custom_call" | custom-call | flops 1048576 | bytes 1048576 | tf_op jit(solution)/shard_map/pallas_call | solution.py:59
  6.2 3.4 %collective-permute-start.5 = (bf16[24,3584]{1,0:T(8,128)(2,1)S(1)}, bf16[24,3584]{1,0:T(8,128)(2,1)S(1)}, u32[]{:S(2)}, u32[]{:S(2)}) collective-permute-start(bf16[24,3584]{1,0:T(8,128)(2,1)S(1)} %get-tuple-element.34), channel_id=1, source_target_pairs={{0,64},{1,193},{2,66},{3,195},{4,68},{5,197},{6,70},{7,199},{8,72}... | collective-permute-start | bytes 516104 | tf_op jit(solution)/shard_map/ppermute | solution.py:30
  9.5 0.9 %collective-permute-start.6 = (bf16[2,24,1792]{2,1,0:T(8,128)(2,1)S(1)}, bf16[2,24,1792]{2,1,0:T(8,128)(2,1)S(1)}, u32[]{:S(2)}, u32[]{:S(2)}) collective-permute-start(bf16[2,24,1792]{2,1,0:T(8,128)(2,1)S(1)} %get-tuple-element.37), channel_id=1, source_target_pairs={{0,1},{1,0},{2,3},{3,2},{4,5},{5,4},{6,7},{7,6},{8,9},{9,8},{10,11... | collective-permute-start | bytes 516104 | tf_op jit(solution)/shard_map/ppermute | solution.py:34
  10.5 0.5 %shard_map.85 = (bf16[24,1792]{1,0:T(8,128)(2,1)S(1)}, f32[24,1792]{1,0:T(8,128)S(1)}, bf16[24,1792]{1,0:T(8,128)(2,1)S(1)}, f32[24,1792]{1,0:T(8,128)S(1)}) custom-call(bf16[72,7168]{1,0:T(8,128)(2,1)S(1)} %get-tuple-element.29.payload, f32[72,128]{1,0:T(8,128)S(1)} %get-tuple-element.30.rows_scales), custom_call_target="tpu_custom_call" | custom-call | flops 1048576 | bytes 1048576 | tf_op jit(solution)/shard_map/pallas_call | solution.py:59
  11.0 0.0 copy-start
  11.0 0.0 copy-start.1
  11.0 0.0 collective-permute-done
  11.1 3.6 %collective-permute-start.1 = (bf16[24,1792]{1,0:T(8,128)(2,1)S(1)}, bf16[24,1792]{1,0:T(8,128)(2,1)S(1)}, u32[]{:S(2)}, u32[]{:S(2)}) collective-permute-start(bf16[24,1792]{1,0:T(8,128)(2,1)S(1)} %fusion.5), channel_id=1, source_target_pairs={{0,64},{1,193},{2,66},{3,195},{4,68},{5,197},{6,70},{7,199},{8,72}... | collective-permute-start | bytes 258056 | tf_op jit(solution)/shard_map/ppermute | solution.py:30
  14.7 0.0 collective-permute-done.6
  14.7 0.1 collective-permute-start.9
  14.8 0.0 collective-permute-done.5
  14.9 5.4 %collective-permute-start.7 = (bf16[24,3584]{1,0:T(8,128)(2,1)S(1)}, bf16[24,3584]{1,0:T(8,128)(2,1)S(1)}, u32[]{:S(2)}, u32[]{:S(2)}) collective-permute-start(bf16[24,3584]{1,0:T(8,128)(2,1)S(1)} %add_convert_fusion.1), channel_id=1, source_target_pairs={{0,192},{1,65},{2,194},{3,67},{4,196},{5,69},{6,198},{7,71},{8,200... | collective-permute-start | bytes 516104 | tf_op jit(solution)/shard_map/ppermute | solution.py:30
  20.3 0.0 collective-permute-done.1
  20.3 3.1 %collective-permute-start.2 = (bf16[24,1792]{1,0:T(8,128)(2,1)S(1)}, bf16[24,1792]{1,0:T(8,128)(2,1)S(1)}, u32[]{:S(2)}, u32[]{:S(2)}) collective-permute-start(bf16[24,1792]{1,0:T(8,128)(2,1)S(1)} %fusion.4), channel_id=1, source_target_pairs={{0,192},{1,65},{2,194},{3,67},{4,196},{5,69},{6,198},{7,71},{8,200... | collective-permute-start | bytes 258056 | tf_op jit(solution)/shard_map/ppermute | solution.py:30
  23.5 0.6 %collective-permute-done.9 = bf16[24,1792]{1,0:T(8,128)(2,1)S(1)} collective-permute-done((bf16[24,1792]{1,0:T(8,128)(2,1)S(1)}, bf16[24,1792]{1,0:T(8,128)(2,1)S(1)}, u32[]{:S(2)}, u32[]{:S(2)}) %collective-permute-start.9) | collective-permute-done | bytes 86048 | tf_op jit(solution)/shard_map/ppermute | solution.py:30
  24.1 4.0 %collective-permute-start.10 = (bf16[24,1792]{1,0:T(8,128)(2,1)S(1)}, bf16[24,1792]{1,0:T(8,128)(2,1)S(1)}, u32[]{:S(2)}, u32[]{:S(2)}) collective-permute-start(bf16[24,1792]{1,0:T(8,128)(2,1)S(1)} %fusion.1), channel_id=1, source_target_pairs={{0,192},{1,65},{2,194},{3,67},{4,196},{5,69},{6,198},{7,71},{8,200... | collective-permute-start | bytes 258056 | tf_op jit(solution)/shard_map/ppermute | solution.py:30
  28.1 0.0 collective-permute-done.2
  28.2 4.4 %collective-permute-start.3 = (bf16[24,1792]{1,0:T(8,128)(2,1)S(1)}, bf16[24,1792]{1,0:T(8,128)(2,1)S(1)}, u32[]{:S(2)}, u32[]{:S(2)}) collective-permute-start(bf16[24,1792]{1,0:T(8,128)(2,1)S(1)} %add_convert_fusion.3.own), channel_id=1, source_target_pairs={{0,64},{1,193},{2,66},{3,195},{4,68},{5,197},{6,70},{7,199},{8,72}... | collective-permute-start | bytes 258056 | tf_op jit(solution)/shard_map/ppermute | solution.py:30
  32.6 0.0 collective-permute-done.7
  32.6 0.1 collective-permute-start.8
  32.7 0.0 collective-permute-done.10
  32.8 7.3 %collective-permute-start.11 = (bf16[24,1792]{1,0:T(8,128)(2,1)S(1)}, bf16[24,1792]{1,0:T(8,128)(2,1)S(1)}, u32[]{:S(2)}, u32[]{:S(2)}) collective-permute-start(bf16[24,1792]{1,0:T(8,128)(2,1)S(1)} %add_convert_fusion.2.own), channel_id=1, source_target_pairs={{0,64},{1,193},{2,66},{3,195},{4,68},{5,197},{6,70},{7,199},{8,72}... | collective-permute-start | bytes 258056 | tf_op jit(solution)/shard_map/ppermute | solution.py:30
  40.0 0.0 collective-permute-done.3.recv
  40.0 0.1 collective-permute-start.4
  40.1 2.4 %collective-permute-done.11.recv = bf16[24,1792]{1,0:T(8,128)(2,1)S(1)} collective-permute-done((bf16[24,1792]{1,0:T(8,128)(2,1)S(1)}, bf16[24,1792]{1,0:T(8,128)(2,1)S(1)}, u32[]{:S(2)}, u32[]{:S(2)}) %collective-permute-start.11) | collective-permute-done | bytes 86048 | tf_op jit(solution)/shard_map/ppermute | solution.py:30
  42.6 0.1 collective-permute-start.12
  42.7 0.0 collective-permute-done.8.recv
  42.7 0.0 copy-done
  42.7 0.0 copy-done.1
  42.7 1.4 %shard_map.87 = (f32[72,7168]{1,0:T(8,128)}, f32[72,7168]{1,0:T(8,128)}, bf16[24,7168]{1,0:T(8,128)(2,1)S(1)}, f32[24,128]{1,0:T(8,128)S(1)}) custom-call(bf16[24,3584]{1,0:T(8,128)(2,1)S(1)} %add_convert_fusion.own, bf16[24,3584]{1,0:T(8,128)(2,1)S(1)} %collective-permute-done.8.recv, f32[72,128]{1,0:T(8,128)S(1)} %get-tuple-element.39.live, ...), custom_call_target="tpu_custom_call" | custom-call | flops 25165824 | bytes 25165824 | tf_op jit(solution)/shard_map/pallas_call | solution.py:59
  44.1 3.8 %collective-permute-done.4 = bf16[2,24,1792]{2,1,0:T(8,128)(2,1)S(1)} collective-permute-done((bf16[2,24,1792]{2,1,0:T(8,128)(2,1)S(1)}, bf16[2,24,1792]{2,1,0:T(8,128)(2,1)S(1)}, u32[]{:S(2)}, u32[]{:S(2)}) %collective-permute-start.4) | collective-permute-done | bytes 172064 | tf_op jit(solution)/shard_map/ppermute | solution.py:45
  48.0 0.0 collective-permute-done.12.other
  48.0 1.5 %shard_map.88 = (f32[72,7168]{1,0:T(8,128)}, f32[72,7168]{1,0:T(8,128)}, bf16[24,7168]{1,0:T(8,128)(2,1)S(1)}, f32[24,128]{1,0:T(8,128)S(1)}) custom-call(bf16[24,1792]{1,0:T(8,128)(2,1)S(1)} %add_convert_fusion.2.own, bf16[24,1792]{1,0:T(8,128)(2,1)S(1)} %collective-permute-done.11.recv, ...), custom_call_target="tpu_custom_call", output_to_operand_aliasing={{0}: (6, {}), {1}: (7, {})} | custom-call | flops 4194304 | bytes 4194304 | tf_op jit(solution)/shard_map/pallas_call | solution.py:59
  49.5 1.9 %shard_map.89 = (f32[72,7168]{1,0:T(8,128)}, f32[72,7168]{1,0:T(8,128)}, bf16[72,7168]{1,0:T(8,128)(2,1)}, f32[56,72]{1,0:T(8,128)}) custom-call(bf16[24,1792]{1,0:T(8,128)(2,1)S(1)} %add_convert_fusion.3.own, bf16[24,1792]{1,0:T(8,128)(2,1)S(1)} %collective-permute-done.3.recv, ...), custom_call_target="tpu_custom_call", output_to_operand_aliasing={{0}: (10, {}), {1}: (11, {})} | custom-call | flops 4194304 | bytes 4194304 | tf_op jit(solution)/shard_map/pallas_call | solution.py:59
  (12 shorter events, 0.3 us)
Async XLA Ops:
  2.0 9.0 %collective-permute-start = (bf16[2,24,1792]{2,1,0:T(8,128)(2,1)S(1)}, bf16[2,24,1792]{2,1,0:T(8,128)(2,1)S(1)}, u32[]{:S(2)}, u32[]{:S(2)}) collective-permute-start(bf16[2,24,1792]{2,1,0:T(8,128)(2,1)S(1)} %get-tuple-element.32), channel_id=1, source_target_pairs={{0,64},{1,2},{2,1},{3,4},{4,3},{5,6},{6,5},{7,8},{8,7},{9,10},{10,... | collective-permute-start | bytes 516104 | tf_op jit(solution)/shard_map/ppermute | solution.py:45
  6.2 8.7 %collective-permute-start.5 = (bf16[24,3584]{1,0:T(8,128)(2,1)S(1)}, bf16[24,3584]{1,0:T(8,128)(2,1)S(1)}, u32[]{:S(2)}, u32[]{:S(2)}) collective-permute-start(bf16[24,3584]{1,0:T(8,128)(2,1)S(1)} %get-tuple-element.34), channel_id=1, source_target_pairs={{0,64},{1,193},{2,66},{3,195},{4,68},{5,197},{6,70},{7,199},{8,72}... | collective-permute-start | bytes 516104 | tf_op jit(solution)/shard_map/ppermute | solution.py:30
  9.5 5.2 %collective-permute-start.6 = (bf16[2,24,1792]{2,1,0:T(8,128)(2,1)S(1)}, bf16[2,24,1792]{2,1,0:T(8,128)(2,1)S(1)}, u32[]{:S(2)}, u32[]{:S(2)}) collective-permute-start(bf16[2,24,1792]{2,1,0:T(8,128)(2,1)S(1)} %get-tuple-element.37), channel_id=1, source_target_pairs={{0,1},{1,0},{2,3},{3,2},{4,5},{5,4},{6,7},{7,6},{8,9},{9,8},{10,11... | collective-permute-start | bytes 516104 | tf_op jit(solution)/shard_map/ppermute | solution.py:34
  11.0 31.7 %copy-start = (f32[72,7168]{1,0:T(8,128)S(1)}, f32[72,7168]{1,0:T(8,128)}, u32[]{:S(2)}) copy-start(f32[72,7168]{1,0:T(8,128)} %params.5) | copy-start | bytes 6193156
  11.0 31.7 %copy-start.1 = (f32[72,7168]{1,0:T(8,128)S(1)}, f32[72,7168]{1,0:T(8,128)}, u32[]{:S(2)}) copy-start(f32[72,7168]{1,0:T(8,128)} %momentum.5) | copy-start | bytes 6193156
  11.1 9.2 %collective-permute-start.1 = (bf16[24,1792]{1,0:T(8,128)(2,1)S(1)}, bf16[24,1792]{1,0:T(8,128)(2,1)S(1)}, u32[]{:S(2)}, u32[]{:S(2)}) collective-permute-start(bf16[24,1792]{1,0:T(8,128)(2,1)S(1)} %fusion.5), channel_id=1, source_target_pairs={{0,64},{1,193},{2,66},{3,195},{4,68},{5,197},{6,70},{7,199},{8,72}... | collective-permute-start | bytes 258056 | tf_op jit(solution)/shard_map/ppermute | solution.py:30
  14.7 9.4 %collective-permute-start.9 = (bf16[24,1792]{1,0:T(8,128)(2,1)S(1)}, bf16[24,1792]{1,0:T(8,128)(2,1)S(1)}, u32[]{:S(2)}, u32[]{:S(2)}) collective-permute-start(bf16[24,1792]{1,0:T(8,128)(2,1)S(1)} %fusion.2), channel_id=1, source_target_pairs={{0,64},{1,193},{2,66},{3,195},{4,68},{5,197},{6,70},{7,199},{8,72}... | collective-permute-start | bytes 258056 | tf_op jit(solution)/shard_map/ppermute | solution.py:30
  14.9 17.7 %collective-permute-start.7 = (bf16[24,3584]{1,0:T(8,128)(2,1)S(1)}, bf16[24,3584]{1,0:T(8,128)(2,1)S(1)}, u32[]{:S(2)}, u32[]{:S(2)}) collective-permute-start(bf16[24,3584]{1,0:T(8,128)(2,1)S(1)} %add_convert_fusion.1), channel_id=1, source_target_pairs={{0,192},{1,65},{2,194},{3,67},{4,196},{5,69},{6,198},{7,71},{8,200... | collective-permute-start | bytes 516104 | tf_op jit(solution)/shard_map/ppermute | solution.py:30
  20.3 7.8 %collective-permute-start.2 = (bf16[24,1792]{1,0:T(8,128)(2,1)S(1)}, bf16[24,1792]{1,0:T(8,128)(2,1)S(1)}, u32[]{:S(2)}, u32[]{:S(2)}) collective-permute-start(bf16[24,1792]{1,0:T(8,128)(2,1)S(1)} %fusion.4), channel_id=1, source_target_pairs={{0,192},{1,65},{2,194},{3,67},{4,196},{5,69},{6,198},{7,71},{8,200... | collective-permute-start | bytes 258056 | tf_op jit(solution)/shard_map/ppermute | solution.py:30
  24.1 8.6 %collective-permute-start.10 = (bf16[24,1792]{1,0:T(8,128)(2,1)S(1)}, bf16[24,1792]{1,0:T(8,128)(2,1)S(1)}, u32[]{:S(2)}, u32[]{:S(2)}) collective-permute-start(bf16[24,1792]{1,0:T(8,128)(2,1)S(1)} %fusion.1), channel_id=1, source_target_pairs={{0,192},{1,65},{2,194},{3,67},{4,196},{5,69},{6,198},{7,71},{8,200... | collective-permute-start | bytes 258056 | tf_op jit(solution)/shard_map/ppermute | solution.py:30
  28.2 11.8 %collective-permute-start.3 = (bf16[24,1792]{1,0:T(8,128)(2,1)S(1)}, bf16[24,1792]{1,0:T(8,128)(2,1)S(1)}, u32[]{:S(2)}, u32[]{:S(2)}) collective-permute-start(bf16[24,1792]{1,0:T(8,128)(2,1)S(1)} %add_convert_fusion.3.own), channel_id=1, source_target_pairs={{0,64},{1,193},{2,66},{3,195},{4,68},{5,197},{6,70},{7,199},{8,72}... | collective-permute-start | bytes 258056 | tf_op jit(solution)/shard_map/ppermute | solution.py:30
  32.6 10.1 %collective-permute-start.8 = (bf16[24,3584]{1,0:T(8,128)(2,1)S(1)}, bf16[24,3584]{1,0:T(8,128)(2,1)S(1)}, u32[]{:S(2)}, u32[]{:S(2)}) collective-permute-start(bf16[24,3584]{1,0:T(8,128)(2,1)S(1)} %add_convert_fusion.own), channel_id=1, source_target_pairs={{0,64},{1,193},{2,66},{3,195},{4,68},{5,197},{6,70},{7,199},{8,72}... | collective-permute-start | bytes 516104 | tf_op jit(solution)/shard_map/ppermute | solution.py:30
  32.8 9.8 %collective-permute-start.11 = (bf16[24,1792]{1,0:T(8,128)(2,1)S(1)}, bf16[24,1792]{1,0:T(8,128)(2,1)S(1)}, u32[]{:S(2)}, u32[]{:S(2)}) collective-permute-start(bf16[24,1792]{1,0:T(8,128)(2,1)S(1)} %add_convert_fusion.2.own), channel_id=1, source_target_pairs={{0,64},{1,193},{2,66},{3,195},{4,68},{5,197},{6,70},{7,199},{8,72}... | collective-permute-start | bytes 258056 | tf_op jit(solution)/shard_map/ppermute | solution.py:30
  40.0 7.9 %collective-permute-start.4 = (bf16[2,24,1792]{2,1,0:T(8,128)(2,1)S(1)}, bf16[2,24,1792]{2,1,0:T(8,128)(2,1)S(1)}, u32[]{:S(2)}, u32[]{:S(2)}) collective-permute-start(bf16[2,24,1792]{2,1,0:T(8,128)(2,1)S(1)} %pad_maximum_fusion), channel_id=1, source_target_pairs={{0,64},{1,2},{2,1},{3,4},{4,3},{5,6},{6,5},{7,8},{8,7},{9,10},{10,... | collective-permute-start | bytes 516104 | tf_op jit(solution)/shard_map/ppermute | solution.py:45
  42.6 5.4 %collective-permute-start.12 = (bf16[2,24,1792]{2,1,0:T(8,128)(2,1)S(1)}, bf16[2,24,1792]{2,1,0:T(8,128)(2,1)S(1)}, u32[]{:S(2)}, u32[]{:S(2)}) collective-permute-start(bf16[2,24,1792]{2,1,0:T(8,128)(2,1)S(1)} %pad_maximum_fusion.1), channel_id=1, source_target_pairs={{0,1},{1,0},{2,3},{3,2},{4,5},{5,4},{6,7},{7,6},{8,9},{9,8},{10,11... | collective-permute-start | bytes 516104 | tf_op jit(solution)/shard_map/ppermute | solution.py:34

commit v5 on v4

--- a/solution.py
+++ b/solution.py
@@ -217,30 +217,29 @@
         copy.wait()
 
 
-def inner_step_body(own, recv, other, live, params, momentum, _p, _m, params_out, momentum_out,
+def outer_step_body(own, recv, other, live, params, momentum, _p, _m, params_out, momentum_out,
                     coded, scale, *scratch):
-    _, b, c = place()
-    blocks = params.shape[1] // QB
-    source = side_source(blocks, c, b, own, recv, other.at[0], other.at[1])
-    for copy in step_band(side_rows(c)[0], source, live, params, momentum, params_out,
+    a, b, c = place()
+    source = side_source(params.shape[1] // QB, 1 - c, jnp.where(at_end(), a, b), own, recv,
+                         other.at[0], other.at[1], turned)
+    for copy in step_band(side_rows(c)[1], source, live, params, momentum, params_out,
                           momentum_out, coded, scale, *scratch):
         copy.wait()
 
 
-def outer_step_body(own, recv, other, coded_mid, scale_mid, coded_in, scale_in, live, params,
+def inner_step_body(own, recv, other, coded_mid, scale_mid, coded_out, scale_out, live, params,
                     momentum, _p, _m, params_out, momentum_out, payload_out, scales_out, payload,
                     rows_scales, scales, *scratch):
-    a, b, c = place()
+    _, b, c = place()
     blocks = params.shape[1] // QB
     inner, outer = side_rows(c)
     payload[pl.ds(BAND, BAND), :] = coded_mid[...]
-    payload[pl.ds(inner, BAND), :] = coded_in[...]
+    payload[pl.ds(outer, BAND), :] = coded_out[...]
     rows_scales[pl.ds(BAND, BAND), :] = scale_mid[...]
-    rows_scales[pl.ds(inner, BAND), :] = scale_in[...]
-    source = side_source(blocks, 1 - c, jnp.where(at_end(), a, b), own, recv, other.at[0], other.at[1],
-                         turned)
-    copies = step_band(outer, source, live, params, momentum, params_out, momentum_out,
-                       payload.at[pl.ds(outer, BAND)], rows_scales.at[pl.ds(outer, BAND)], *scratch)
+    rows_scales[pl.ds(outer, BAND), :] = scale_out[...]
+    source = side_source(blocks, c, b, own, recv, other.at[0], other.at[1])
+    copies = step_band(inner, source, live, params, momentum, params_out, momentum_out,
+                       payload.at[pl.ds(inner, BAND)], rows_scales.at[pl.ds(inner, BAND)], *scratch)
     sems = scratch[-1]
     copies.append(pltpu.make_async_copy(payload, payload_out, sems.at[2, 0]))
     copies[-1].start()
@@ -317,16 +316,16 @@
         mid_step_body, [whole, whole] + band, [VMEM] * 5, own_mid, recv_mid, *state,
         grant=4, scratch=scratch, cost=24,
     )
-    params_out, momentum_out, coded_in, scale_in = local_call(
-        inner_step_body, [whole, whole] + band, [VMEM] * 6 + [HBM] * 2, own_in, recv_in, in_other,
+    params_out, momentum_out, coded_out, scale_out = local_call(
+        outer_step_body, [whole, whole] + band, [VMEM] * 6 + [HBM] * 2, own_out, recv_out, out_other,
         *state, params_out, momentum_out,
         grant=4, scratch=scratch, cost=4, aliases={6: 0, 7: 1},
     )
     params_out, momentum_out, payload_out, scales_out = local_call(
-        outer_step_body,
+        inner_step_body,
         [whole, whole, ((slots, width), BF16, HBM), ((blocks, slots), F32, HBM)],
         [VMEM] * 10 + [HBM] * 2,
-        own_out, recv_out, out_other, coded_mid, scale_mid, coded_in, scale_in,
+        own_in, recv_in, in_other, coded_mid, scale_mid, coded_out, scale_out,
         *state, params_out, momentum_out,
         grant=6, cost=4, aliases={10: 0, 11: 1},
         scratch=[

time: 51.5 us -> 49.6 us (0.963)
  the two profiles are of different devices: /device:TPU:8 before, /device:TPU:32 now
where the time goes in v5:
time: 49.6 us; the launch traced here: 49.5 us
  starting transfers between devices  29.3 us (59%)
  waiting for transfers between devices  11.8 us (24%)
  Pallas kernels  7.27 us (15%)
  between operations  0.79 us (2%)
    ppermute x9, starting transfers between devices, island_swap(): return lax.ppermute(value, AXES, pairs)  27.2 us
    ppermute x9, waiting for transfers between devices, island_swap(): return lax.ppermute(value, AXES, pairs)  7.52 us
    pallas_call x6, Pallas kernels, local_call(): pl.pallas_call(body, out_shape=[jax.ShapeDtypeStruct(s, d) for s, d, _ in...  7.27 us
    ppermute x2, waiting for transfers between devices, outer_swap(): return jnp.where(at_end(), value, lax.ppermute(value, AXES, pairs))  4.31 us
    ppermute x2, starting transfers between devices, outer_swap(): return jnp.where(at_end(), value, lax.ppermute(value, AXES, pairs))  1.92 us
  transfers between devices with their start and end apart: 13, of which 6 were waited for; matrix products, arithmetic and copies ran while one was open for 1% of the time, Pallas kernels for 8%

profile of v5, /device:TPU:32, one launch (start us, length us, event | category | flops | bytes accessed | tf_op | source)
XLA Modules:
  0.0 49.5 jit_solution(8775063324343346476)
XLA Ops:
  0.6 1.4 %shard_map.84 = (bf16[2,24,1792]{2,1,0:T(8,128)(2,1)S(1)}, bf16[72,7168]{1,0:T(8,128)(2,1)S(1)}, f32[72,128]{1,0:T(8,128)S(1)}, f32[72,128]{1,0:T(8,128)S(1)}) custom-call(bf16[72,7168]{1,0:T(8,128)(2,1)} %payload_in.1, f32[56,72]{1,0:T(8,128)} %bitcast.32, s32[4,65]{1,0:T(4,128)} %bounds_in.1), custom_call_target="tpu_custom_call" | custom-call | flops 1048576 | bytes 1048576 | tf_op jit(solution)/shard_map/pallas_call | solution.py:59
  2.0 1.8 %collective-permute-start.8 = (bf16[2,24,1792]{2,1,0:T(8,128)(2,1)S(1)}, bf16[2,24,1792]{2,1,0:T(8,128)(2,1)S(1)}, u32[]{:S(2)}, u32[]{:S(2)}) collective-permute-start(bf16[2,24,1792]{2,1,0:T(8,128)(2,1)S(1)} %get-tuple-element.42), channel_id=1, source_target_pairs={{0,64},{1,2},{2,1},{3,4},{4,3},{5,6},{6,5},{7,8},{8,7},{9,10},{10,... | collective-permute-start | bytes 516104 | tf_op jit(solution)/shard_map/ppermute | solution.py:45
  3.8 0.7 %shard_map.86 = (bf16[2,24,1792]{2,1,0:T(8,128)(2,1)S(1)}, bf16[24,3584]{1,0:T(8,128)(2,1)S(1)}, f32[24,3584]{1,0:T(8,128)S(1)}) custom-call(bf16[72,7168]{1,0:T(8,128)(2,1)S(1)} %get-tuple-element.29.payload, f32[72,128]{1,0:T(8,128)S(1)} %get-tuple-element.30.rows_scales), custom_call_target="tpu_custom_call" | custom-call | flops 1048576 | bytes 1048576 | tf_op jit(solution)/shard_map/pallas_call | solution.py:59
  4.5 0.1 collective-permute-start
  4.6 3.4 %collective-permute-start.3 = (bf16[24,3584]{1,0:T(8,128)(2,1)S(1)}, bf16[24,3584]{1,0:T(8,128)(2,1)S(1)}, u32[]{:S(2)}, u32[]{:S(2)}) collective-permute-start(bf16[24,3584]{1,0:T(8,128)(2,1)S(1)} %get-tuple-element.34), channel_id=1, source_target_pairs={{0,64},{1,193},{2,66},{3,195},{4,68},{5,197},{6,70},{7,199},{8,72}... | collective-permute-start | bytes 516104 | tf_op jit(solution)/shard_map/ppermute | solution.py:30
  8.0 0.5 %shard_map.85 = (bf16[24,1792]{1,0:T(8,128)(2,1)S(1)}, f32[24,1792]{1,0:T(8,128)S(1)}, bf16[24,1792]{1,0:T(8,128)(2,1)S(1)}, f32[24,1792]{1,0:T(8,128)S(1)}) custom-call(bf16[72,7168]{1,0:T(8,128)(2,1)S(1)} %get-tuple-element.29.payload, f32[72,128]{1,0:T(8,128)S(1)} %get-tuple-element.30.rows_scales), custom_call_target="tpu_custom_call" | custom-call | flops 1048576 | bytes 1048576 | tf_op jit(solution)/shard_map/pallas_call | solution.py:59
  8.5 0.0 copy-start
  8.5 0.0 copy-start.1
  8.5 1.4 %collective-permute-done.8 = bf16[2,24,1792]{2,1,0:T(8,128)(2,1)S(1)} collective-permute-done((bf16[2,24,1792]{2,1,0:T(8,128)(2,1)S(1)}, bf16[2,24,1792]{2,1,0:T(8,128)(2,1)S(1)}, u32[]{:S(2)}, u32[]{:S(2)}) %collective-permute-start.8) | collective-permute-done | bytes 172064 | tf_op jit(solution)/shard_map/ppermute | solution.py:45
  10.0 2.5 %collective-permute-start.9 = (bf16[24,1792]{1,0:T(8,128)(2,1)S(1)}, bf16[24,1792]{1,0:T(8,128)(2,1)S(1)}, u32[]{:S(2)}, u32[]{:S(2)}) collective-permute-start(bf16[24,1792]{1,0:T(8,128)(2,1)S(1)} %fusion.2), channel_id=1, source_target_pairs={{0,64},{1,193},{2,66},{3,195},{4,68},{5,197},{6,70},{7,199},{8,72}... | collective-permute-start | bytes 258056 | tf_op jit(solution)/shard_map/ppermute | solution.py:30
  12.4 0.0 collective-permute-done
  12.5 0.6 %collective-permute-start.1 = (bf16[24,1792]{1,0:T(8,128)(2,1)S(1)}, bf16[24,1792]{1,0:T(8,128)(2,1)S(1)}, u32[]{:S(2)}, u32[]{:S(2)}) collective-permute-start(bf16[24,1792]{1,0:T(8,128)(2,1)S(1)} %fusion.5), channel_id=1, source_target_pairs={{0,64},{1,193},{2,66},{3,195},{4,68},{5,197},{6,70},{7,199},{8,72}... | collective-permute-start | bytes 258056 | tf_op jit(solution)/shard_map/ppermute | solution.py:30
  13.1 1.2 %collective-permute-done.3 = bf16[24,3584]{1,0:T(8,128)(2,1)S(1)} collective-permute-done((bf16[24,3584]{1,0:T(8,128)(2,1)S(1)}, bf16[24,3584]{1,0:T(8,128)(2,1)S(1)}, u32[]{:S(2)}, u32[]{:S(2)}) %collective-permute-start.3) | collective-permute-done | bytes 172064 | tf_op jit(solution)/shard_map/ppermute | solution.py:30
  14.3 5.2 %collective-permute-start.4 = (bf16[24,3584]{1,0:T(8,128)(2,1)S(1)}, bf16[24,3584]{1,0:T(8,128)(2,1)S(1)}, u32[]{:S(2)}, u32[]{:S(2)}) collective-permute-start(bf16[24,3584]{1,0:T(8,128)(2,1)S(1)} %add_convert_fusion.1), channel_id=1, source_target_pairs={{0,192},{1,65},{2,194},{3,67},{4,196},{5,69},{6,198},{7,71},{8,200... | collective-permute-start | bytes 516104 | tf_op jit(solution)/shard_map/ppermute | solution.py:30
  19.6 0.0 collective-permute-done.9
  19.6 7.6 %collective-permute-start.10 = (bf16[24,1792]{1,0:T(8,128)(2,1)S(1)}, bf16[24,1792]{1,0:T(8,128)(2,1)S(1)}, u32[]{:S(2)}, u32[]{:S(2)}) collective-permute-start(bf16[24,1792]{1,0:T(8,128)(2,1)S(1)} %fusion.1), channel_id=1, source_target_pairs={{0,192},{1,65},{2,194},{3,67},{4,196},{5,69},{6,198},{7,71},{8,200... | collective-permute-start | bytes 258056 | tf_op jit(solution)/shard_map/ppermute | solution.py:30
  27.3 0.0 collective-permute-done.1
  27.3 1.9 %collective-permute-start.2 = (bf16[24,1792]{1,0:T(8,128)(2,1)S(1)}, bf16[24,1792]{1,0:T(8,128)(2,1)S(1)}, u32[]{:S(2)}, u32[]{:S(2)}) collective-permute-start(bf16[24,1792]{1,0:T(8,128)(2,1)S(1)} %fusion.4), channel_id=1, source_target_pairs={{0,192},{1,65},{2,194},{3,67},{4,196},{5,69},{6,198},{7,71},{8,200... | collective-permute-start | bytes 258056 | tf_op jit(solution)/shard_map/ppermute | solution.py:30
  29.2 0.7 %collective-permute-done.10 = bf16[24,1792]{1,0:T(8,128)(2,1)S(1)} collective-permute-done((bf16[24,1792]{1,0:T(8,128)(2,1)S(1)}, bf16[24,1792]{1,0:T(8,128)(2,1)S(1)}, u32[]{:S(2)}, u32[]{:S(2)}) %collective-permute-start.10) | collective-permute-done | bytes 86048 | tf_op jit(solution)/shard_map/ppermute | solution.py:30
  29.9 1.2 %collective-permute-start.11 = (bf16[24,1792]{1,0:T(8,128)(2,1)S(1)}, bf16[24,1792]{1,0:T(8,128)(2,1)S(1)}, u32[]{:S(2)}, u32[]{:S(2)}) collective-permute-start(bf16[24,1792]{1,0:T(8,128)(2,1)S(1)} %add_convert_fusion.2.own), channel_id=1, source_target_pairs={{0,64},{1,193},{2,66},{3,195},{4,68},{5,197},{6,70},{7,199},{8,72}... | collective-permute-start | bytes 258056 | tf_op jit(solution)/shard_map/ppermute | solution.py:30
  31.0 0.0 collective-permute-done.4
  31.1 1.9 %collective-permute-start.7 = (bf16[24,3584]{1,0:T(8,128)(2,1)S(1)}, bf16[24,3584]{1,0:T(8,128)(2,1)S(1)}, u32[]{:S(2)}, u32[]{:S(2)}) collective-permute-start(bf16[24,3584]{1,0:T(8,128)(2,1)S(1)} %add_convert_fusion.own), channel_id=1, source_target_pairs={{0,64},{1,193},{2,66},{3,195},{4,68},{5,197},{6,70},{7,199},{8,72}... | collective-permute-start | bytes 516104 | tf_op jit(solution)/shard_map/ppermute | solution.py:30
  33.0 3.2 %collective-permute-done.2 = bf16[24,1792]{1,0:T(8,128)(2,1)S(1)} collective-permute-done((bf16[24,1792]{1,0:T(8,128)(2,1)S(1)}, bf16[24,1792]{1,0:T(8,128)(2,1)S(1)}, u32[]{:S(2)}, u32[]{:S(2)}) %collective-permute-start.2) | collective-permute-done | bytes 86048 | tf_op jit(solution)/shard_map/ppermute | solution.py:30
  36.2 2.9 %collective-permute-start.5 = (bf16[24,1792]{1,0:T(8,128)(2,1)S(1)}, bf16[24,1792]{1,0:T(8,128)(2,1)S(1)}, u32[]{:S(2)}, u32[]{:S(2)}) collective-permute-start(bf16[24,1792]{1,0:T(8,128)(2,1)S(1)} %add_convert_fusion.3.own), channel_id=1, source_target_pairs={{0,64},{1,193},{2,66},{3,195},{4,68},{5,197},{6,70},{7,199},{8,72}... | collective-permute-start | bytes 258056 | tf_op jit(solution)/shard_map/ppermute | solution.py:30
  39.1 0.0 collective-permute-done.11.recv
  39.1 0.1 collective-permute-start.12
  39.2 2.5 %collective-permute-done.5.recv = bf16[24,1792]{1,0:T(8,128)(2,1)S(1)} collective-permute-done((bf16[24,1792]{1,0:T(8,128)(2,1)S(1)}, bf16[24,1792]{1,0:T(8,128)(2,1)S(1)}, u32[]{:S(2)}, u32[]{:S(2)}) %collective-permute-start.5) | collective-permute-done | bytes 86048 | tf_op jit(solution)/shard_map/ppermute | solution.py:30
  41.7 0.1 collective-permute-start.6
  41.8 0.0 collective-permute-done.7.recv
  41.8 0.0 copy-done
  41.8 0.0 copy-done.1
  41.8 1.4 %shard_map.87 = (f32[72,7168]{1,0:T(8,128)}, f32[72,7168]{1,0:T(8,128)}, bf16[24,7168]{1,0:T(8,128)(2,1)S(1)}, f32[24,128]{1,0:T(8,128)S(1)}) custom-call(bf16[24,3584]{1,0:T(8,128)(2,1)S(1)} %add_convert_fusion.own, bf16[24,3584]{1,0:T(8,128)(2,1)S(1)} %collective-permute-done.7.recv, f32[72,128]{1,0:T(8,128)S(1)} %get-tuple-element.38.live, ...), custom_call_target="tpu_custom_call" | custom-call | flops 25165824 | bytes 25165824 | tf_op jit(solution)/shard_map/pallas_call | solution.py:59
  43.2 2.9 %collective-permute-done.12 = bf16[2,24,1792]{2,1,0:T(8,128)(2,1)S(1)} collective-permute-done((bf16[2,24,1792]{2,1,0:T(8,128)(2,1)S(1)}, bf16[2,24,1792]{2,1,0:T(8,128)(2,1)S(1)}, u32[]{:S(2)}, u32[]{:S(2)}) %collective-permute-start.12) | collective-permute-done | bytes 172064 | tf_op jit(solution)/shard_map/ppermute | solution.py:45
  46.2 1.5 %shard_map.88 = (f32[72,7168]{1,0:T(8,128)}, f32[72,7168]{1,0:T(8,128)}, bf16[24,7168]{1,0:T(8,128)(2,1)S(1)}, f32[24,128]{1,0:T(8,128)S(1)}) custom-call(bf16[24,1792]{1,0:T(8,128)(2,1)S(1)} %add_convert_fusion.2.own, bf16[24,1792]{1,0:T(8,128)(2,1)S(1)} %collective-permute-done.11.recv, ...), custom_call_target="tpu_custom_call", output_to_operand_aliasing={{0}: (6, {}), {1}: (7, {})} | custom-call | flops 4194304 | bytes 4194304 | tf_op jit(solution)/shard_map/pallas_call | solution.py:59
  47.7 0.0 collective-permute-done.6.other
  47.7 1.8 %shard_map.89 = (f32[72,7168]{1,0:T(8,128)}, f32[72,7168]{1,0:T(8,128)}, bf16[72,7168]{1,0:T(8,128)(2,1)}, f32[56,72]{1,0:T(8,128)}) custom-call(bf16[24,1792]{1,0:T(8,128)(2,1)S(1)} %add_convert_fusion.3.own, bf16[24,1792]{1,0:T(8,128)(2,1)S(1)} %collective-permute-done.5.recv, ...), custom_call_target="tpu_custom_call", output_to_operand_aliasing={{0}: (10, {}), {1}: (11, {})} | custom-call | flops 4194304 | bytes 4194304 | tf_op jit(solution)/shard_map/pallas_call | solution.py:59
  (12 shorter events, 0.3 us)
Async XLA Ops:
  2.0 7.9 %collective-permute-start.8 = (bf16[2,24,1792]{2,1,0:T(8,128)(2,1)S(1)}, bf16[2,24,1792]{2,1,0:T(8,128)(2,1)S(1)}, u32[]{:S(2)}, u32[]{:S(2)}) collective-permute-start(bf16[2,24,1792]{2,1,0:T(8,128)(2,1)S(1)} %get-tuple-element.42), channel_id=1, source_target_pairs={{0,64},{1,2},{2,1},{3,4},{4,3},{5,6},{6,5},{7,8},{8,7},{9,10},{10,... | collective-permute-start | bytes 516104 | tf_op jit(solution)/shard_map/ppermute | solution.py:45
  4.5 8.0 %collective-permute-start = (bf16[2,24,1792]{2,1,0:T(8,128)(2,1)S(1)}, bf16[2,24,1792]{2,1,0:T(8,128)(2,1)S(1)}, u32[]{:S(2)}, u32[]{:S(2)}) collective-permute-start(bf16[2,24,1792]{2,1,0:T(8,128)(2,1)S(1)} %get-tuple-element.32), channel_id=1, source_target_pairs={{0,1},{1,0},{2,3},{3,2},{4,5},{5,4},{6,7},{7,6},{8,9},{9,8},{10,11... | collective-permute-start | bytes 516104 | tf_op jit(solution)/shard_map/ppermute | solution.py:34
  4.6 9.7 %collective-permute-start.3 = (bf16[24,3584]{1,0:T(8,128)(2,1)S(1)}, bf16[24,3584]{1,0:T(8,128)(2,1)S(1)}, u32[]{:S(2)}, u32[]{:S(2)}) collective-permute-start(bf16[24,3584]{1,0:T(8,128)(2,1)S(1)} %get-tuple-element.34), channel_id=1, source_target_pairs={{0,64},{1,193},{2,66},{3,195},{4,68},{5,197},{6,70},{7,199},{8,72}... | collective-permute-start | bytes 516104 | tf_op jit(solution)/shard_map/ppermute | solution.py:30
  8.5 33.3 %copy-start = (f32[72,7168]{1,0:T(8,128)S(1)}, f32[72,7168]{1,0:T(8,128)}, u32[]{:S(2)}) copy-start(f32[72,7168]{1,0:T(8,128)} %params.5) | copy-start | bytes 6193156
  8.5 33.3 %copy-start.1 = (f32[72,7168]{1,0:T(8,128)S(1)}, f32[72,7168]{1,0:T(8,128)}, u32[]{:S(2)}) copy-start(f32[72,7168]{1,0:T(8,128)} %momentum.5) | copy-start | bytes 6193156
  10.0 9.6 %collective-permute-start.9 = (bf16[24,1792]{1,0:T(8,128)(2,1)S(1)}, bf16[24,1792]{1,0:T(8,128)(2,1)S(1)}, u32[]{:S(2)}, u32[]{:S(2)}) collective-permute-start(bf16[24,1792]{1,0:T(8,128)(2,1)S(1)} %fusion.2), channel_id=1, source_target_pairs={{0,64},{1,193},{2,66},{3,195},{4,68},{5,197},{6,70},{7,199},{8,72}... | collective-permute-start | bytes 258056 | tf_op jit(solution)/shard_map/ppermute | solution.py:30
  12.5 14.8 %collective-permute-start.1 = (bf16[24,1792]{1,0:T(8,128)(2,1)S(1)}, bf16[24,1792]{1,0:T(8,128)(2,1)S(1)}, u32[]{:S(2)}, u32[]{:S(2)}) collective-permute-start(bf16[24,1792]{1,0:T(8,128)(2,1)S(1)} %fusion.5), channel_id=1, source_target_pairs={{0,64},{1,193},{2,66},{3,195},{4,68},{5,197},{6,70},{7,199},{8,72}... | collective-permute-start | bytes 258056 | tf_op jit(solution)/shard_map/ppermute | solution.py:30
  14.3 16.7 %collective-permute-start.4 = (bf16[24,3584]{1,0:T(8,128)(2,1)S(1)}, bf16[24,3584]{1,0:T(8,128)(2,1)S(1)}, u32[]{:S(2)}, u32[]{:S(2)}) collective-permute-start(bf16[24,3584]{1,0:T(8,128)(2,1)S(1)} %add_convert_fusion.1), channel_id=1, source_target_pairs={{0,192},{1,65},{2,194},{3,67},{4,196},{5,69},{6,198},{7,71},{8,200... | collective-permute-start | bytes 516104 | tf_op jit(solution)/shard_map/ppermute | solution.py:30
  19.6 10.2 %collective-permute-start.10 = (bf16[24,1792]{1,0:T(8,128)(2,1)S(1)}, bf16[24,1792]{1,0:T(8,128)(2,1)S(1)}, u32[]{:S(2)}, u32[]{:S(2)}) collective-permute-start(bf16[24,1792]{1,0:T(8,128)(2,1)S(1)} %fusion.1), channel_id=1, source_target_pairs={{0,192},{1,65},{2,194},{3,67},{4,196},{5,69},{6,198},{7,71},{8,200... | collective-permute-start | bytes 258056 | tf_op jit(solution)/shard_map/ppermute | solution.py:30
  27.3 8.9 %collective-permute-start.2 = (bf16[24,1792]{1,0:T(8,128)(2,1)S(1)}, bf16[24,1792]{1,0:T(8,128)(2,1)S(1)}, u32[]{:S(2)}, u32[]{:S(2)}) collective-permute-start(bf16[24,1792]{1,0:T(8,128)(2,1)S(1)} %fusion.4), channel_id=1, source_target_pairs={{0,192},{1,65},{2,194},{3,67},{4,196},{5,69},{6,198},{7,71},{8,200... | collective-permute-start | bytes 258056 | tf_op jit(solution)/shard_map/ppermute | solution.py:30
  29.9 9.2 %collective-permute-start.11 = (bf16[24,1792]{1,0:T(8,128)(2,1)S(1)}, bf16[24,1792]{1,0:T(8,128)(2,1)S(1)}, u32[]{:S(2)}, u32[]{:S(2)}) collective-permute-start(bf16[24,1792]{1,0:T(8,128)(2,1)S(1)} %add_convert_fusion.2.own), channel_id=1, source_target_pairs={{0,64},{1,193},{2,66},{3,195},{4,68},{5,197},{6,70},{7,199},{8,72}... | collective-permute-start | bytes 258056 | tf_op jit(solution)/shard_map/ppermute | solution.py:30
  31.1 10.7 %collective-permute-start.7 = (bf16[24,3584]{1,0:T(8,128)(2,1)S(1)}, bf16[24,3584]{1,0:T(8,128)(2,1)S(1)}, u32[]{:S(2)}, u32[]{:S(2)}) collective-permute-start(bf16[24,3584]{1,0:T(8,128)(2,1)S(1)} %add_convert_fusion.own), channel_id=1, source_target_pairs={{0,64},{1,193},{2,66},{3,195},{4,68},{5,197},{6,70},{7,199},{8,72}... | collective-permute-start | bytes 516104 | tf_op jit(solution)/shard_map/ppermute | solution.py:30
  36.2 5.5 %collective-permute-start.5 = (bf16[24,1792]{1,0:T(8,128)(2,1)S(1)}, bf16[24,1792]{1,0:T(8,128)(2,1)S(1)}, u32[]{:S(2)}, u32[]{:S(2)}) collective-permute-start(bf16[24,1792]{1,0:T(8,128)(2,1)S(1)} %add_convert_fusion.3.own), channel_id=1, source_target_pairs={{0,64},{1,193},{2,66},{3,195},{4,68},{5,197},{6,70},{7,199},{8,72}... | collective-permute-start | bytes 258056 | tf_op jit(solution)/shard_map/ppermute | solution.py:30
  39.1 7.0 %collective-permute-start.12 = (bf16[2,24,1792]{2,1,0:T(8,128)(2,1)S(1)}, bf16[2,24,1792]{2,1,0:T(8,128)(2,1)S(1)}, u32[]{:S(2)}, u32[]{:S(2)}) collective-permute-start(bf16[2,24,1792]{2,1,0:T(8,128)(2,1)S(1)} %pad_maximum_fusion.1), channel_id=1, source_target_pairs={{0,64},{1,2},{2,1},{3,4},{4,3},{5,6},{6,5},{7,8},{8,7},{9,10},{10,... | collective-permute-start | bytes 516104 | tf_op jit(solution)/shard_map/ppermute | solution.py:45
  41.7 6.0 %collective-permute-start.6 = (bf16[2,24,1792]{2,1,0:T(8,128)(2,1)S(1)}, bf16[2,24,1792]{2,1,0:T(8,128)(2,1)S(1)}, u32[]{:S(2)}, u32[]{:S(2)}) collective-permute-start(bf16[2,24,1792]{2,1,0:T(8,128)(2,1)S(1)} %pad_maximum_fusion), channel_id=1, source_target_pairs={{0,1},{1,0},{2,3},{3,2},{4,5},{5,4},{6,7},{7,6},{8,9},{9,8},{10,11... | collective-permute-start | bytes 516104 | tf_op jit(solution)/shard_map/ppermute | solution.py:34

commit v6 on v5

--- a/solution.py
+++ b/solution.py
@@ -154,7 +154,7 @@
 
 
 def step_band(first, source, live, params, momentum, params_out, momentum_out, coded_out,
-              scale_out, params_new, momentum_new, sems):
+              scale_out, params_new, momentum_new, sems, all_rows=()):
     rows = pl.ds(first, BAND)
     blocks = params.shape[1] // QB
     fourth = blocks // 4
@@ -184,6 +184,12 @@
                 )
                 copy.start()
                 copies.append(copy)
+            for new, out in all_rows:
+                copy = pltpu.make_async_copy(
+                    new.at[:, part], out.at[:, part], sems.at[2, g // fourth]
+                )
+                copy.start()
+                copies.append(copy)
     scale_out[...] = scale_row
     return copies
 
@@ -239,12 +245,11 @@
     rows_scales[pl.ds(outer, BAND), :] = scale_out[...]
     source = side_source(blocks, c, b, own, recv, other.at[0], other.at[1])
     copies = step_band(inner, source, live, params, momentum, params_out, momentum_out,
-                       payload.at[pl.ds(inner, BAND)], rows_scales.at[pl.ds(inner, BAND)], *scratch)
+                       payload.at[pl.ds(inner, BAND)], rows_scales.at[pl.ds(inner, BAND)], *scratch,
+                       all_rows=[(payload, payload_out)])
     sems = scratch[-1]
-    copies.append(pltpu.make_async_copy(payload, payload_out, sems.at[2, 0]))
-    copies[-1].start()
     scales[...] = jnp.transpose(rows_scales[...])[:blocks, :]
-    copies.append(pltpu.make_async_copy(scales, scales_out, sems.at[2, 1]))
+    copies.append(pltpu.make_async_copy(scales, scales_out, sems.at[3, 0]))
     copies[-1].start()
     for copy in copies:
         copy.wait()
@@ -309,7 +314,7 @@
     scratch = [
         pltpu.VMEM((BAND, width), F32),
         pltpu.VMEM((BAND, width), F32),
-        pltpu.SemaphoreType.DMA((3, 4)),
+        pltpu.SemaphoreType.DMA((4, 4)),
     ]
     state = (live, params, momentum)
     params_out, momentum_out, coded_mid, scale_mid = local_call(

time: 49.6 us -> 49.7 us (level)
  no operation moved by 1% of the time
where the time goes in v6:
time: 49.7 us; the launch traced here: 49.6 us
  starting transfers between devices  29.3 us (59%)
  waiting for transfers between devices  11.8 us (24%)
  Pallas kernels  7.35 us (15%)
  between operations  0.79 us (2%)
    ppermute x9, starting transfers between devices, island_swap(): return lax.ppermute(value, AXES, pairs)  27.2 us
    ppermute x9, waiting for transfers between devices, island_swap(): return lax.ppermute(value, AXES, pairs)  7.52 us
    pallas_call x6, Pallas kernels, local_call(): pl.pallas_call(body, out_shape=[jax.ShapeDtypeStruct(s, d) for s, d, _ in...  7.35 us
    ppermute x2, waiting for transfers between devices, outer_swap(): return jnp.where(at_end(), value, lax.ppermute(value, AXES, pairs))  4.27 us
    ppermute x2, starting transfers between devices, outer_swap(): return jnp.where(at_end(), value, lax.ppermute(value, AXES, pairs))  1.92 us
  transfers between devices with their start and end apart: 13, of which 6 were waited for; matrix products, arithmetic and copies ran while one was open for 1% of the time, Pallas kernels for 8%

profile of v6, /device:TPU:32, one launch (start us, length us, event | category | flops | bytes accessed | tf_op | source)
XLA Modules:
  0.0 49.6 jit_solution(9785533391186983662)
XLA Ops:
  0.6 1.4 %shard_map.84 = (bf16[2,24,1792]{2,1,0:T(8,128)(2,1)S(1)}, bf16[72,7168]{1,0:T(8,128)(2,1)S(1)}, f32[72,128]{1,0:T(8,128)S(1)}, f32[72,128]{1,0:T(8,128)S(1)}) custom-call(bf16[72,7168]{1,0:T(8,128)(2,1)} %payload_in.1, f32[56,72]{1,0:T(8,128)} %bitcast.32, s32[4,65]{1,0:T(4,128)} %bounds_in.1), custom_call_target="tpu_custom_call" | custom-call | flops 1048576 | bytes 1048576 | tf_op jit(solution)/shard_map/pallas_call | solution.py:59
  2.0 1.8 %collective-permute-start.8 = (bf16[2,24,1792]{2,1,0:T(8,128)(2,1)S(1)}, bf16[2,24,1792]{2,1,0:T(8,128)(2,1)S(1)}, u32[]{:S(2)}, u32[]{:S(2)}) collective-permute-start(bf16[2,24,1792]{2,1,0:T(8,128)(2,1)S(1)} %get-tuple-element.42), channel_id=1, source_target_pairs={{0,64},{1,2},{2,1},{3,4},{4,3},{5,6},{6,5},{7,8},{8,7},{9,10},{10,... | collective-permute-start | bytes 516104 | tf_op jit(solution)/shard_map/ppermute | solution.py:45
  3.8 0.7 %shard_map.86 = (bf16[2,24,1792]{2,1,0:T(8,128)(2,1)S(1)}, bf16[24,3584]{1,0:T(8,128)(2,1)S(1)}, f32[24,3584]{1,0:T(8,128)S(1)}) custom-call(bf16[72,7168]{1,0:T(8,128)(2,1)S(1)} %get-tuple-element.29.payload, f32[72,128]{1,0:T(8,128)S(1)} %get-tuple-element.30.rows_scales), custom_call_target="tpu_custom_call" | custom-call | flops 1048576 | bytes 1048576 | tf_op jit(solution)/shard_map/pallas_call | solution.py:59
  4.5 0.1 collective-permute-start
  4.6 3.4 %collective-permute-start.3 = (bf16[24,3584]{1,0:T(8,128)(2,1)S(1)}, bf16[24,3584]{1,0:T(8,128)(2,1)S(1)}, u32[]{:S(2)}, u32[]{:S(2)}) collective-permute-start(bf16[24,3584]{1,0:T(8,128)(2,1)S(1)} %get-tuple-element.34), channel_id=1, source_target_pairs={{0,64},{1,193},{2,66},{3,195},{4,68},{5,197},{6,70},{7,199},{8,72}... | collective-permute-start | bytes 516104 | tf_op jit(solution)/shard_map/ppermute | solution.py:30
  8.0 0.5 %shard_map.85 = (bf16[24,1792]{1,0:T(8,128)(2,1)S(1)}, f32[24,1792]{1,0:T(8,128)S(1)}, bf16[24,1792]{1,0:T(8,128)(2,1)S(1)}, f32[24,1792]{1,0:T(8,128)S(1)}) custom-call(bf16[72,7168]{1,0:T(8,128)(2,1)S(1)} %get-tuple-element.29.payload, f32[72,128]{1,0:T(8,128)S(1)} %get-tuple-element.30.rows_scales), custom_call_target="tpu_custom_call" | custom-call | flops 1048576 | bytes 1048576 | tf_op jit(solution)/shard_map/pallas_call | solution.py:59
  8.5 0.0 copy-start
  8.5 0.0 copy-start.1
  8.5 1.4 %collective-permute-done.8 = bf16[2,24,1792]{2,1,0:T(8,128)(2,1)S(1)} collective-permute-done((bf16[2,24,1792]{2,1,0:T(8,128)(2,1)S(1)}, bf16[2,24,1792]{2,1,0:T(8,128)(2,1)S(1)}, u32[]{:S(2)}, u32[]{:S(2)}) %collective-permute-start.8) | collective-permute-done | bytes 172064 | tf_op jit(solution)/shard_map/ppermute | solution.py:45
  10.0 2.5 %collective-permute-start.9 = (bf16[24,1792]{1,0:T(8,128)(2,1)S(1)}, bf16[24,1792]{1,0:T(8,128)(2,1)S(1)}, u32[]{:S(2)}, u32[]{:S(2)}) collective-permute-start(bf16[24,1792]{1,0:T(8,128)(2,1)S(1)} %fusion.2), channel_id=1, source_target_pairs={{0,64},{1,193},{2,66},{3,195},{4,68},{5,197},{6,70},{7,199},{8,72}... | collective-permute-start | bytes 258056 | tf_op jit(solution)/shard_map/ppermute | solution.py:30
  12.4 0.0 collective-permute-done
  12.5 0.6 %collective-permute-start.1 = (bf16[24,1792]{1,0:T(8,128)(2,1)S(1)}, bf16[24,1792]{1,0:T(8,128)(2,1)S(1)}, u32[]{:S(2)}, u32[]{:S(2)}) collective-permute-start(bf16[24,1792]{1,0:T(8,128)(2,1)S(1)} %fusion.5), channel_id=1, source_target_pairs={{0,64},{1,193},{2,66},{3,195},{4,68},{5,197},{6,70},{7,199},{8,72}... | collective-permute-start | bytes 258056 | tf_op jit(solution)/shard_map/ppermute | solution.py:30
  13.1 1.2 %collective-permute-done.3 = bf16[24,3584]{1,0:T(8,128)(2,1)S(1)} collective-permute-done((bf16[24,3584]{1,0:T(8,128)(2,1)S(1)}, bf16[24,3584]{1,0:T(8,128)(2,1)S(1)}, u32[]{:S(2)}, u32[]{:S(2)}) %collective-permute-start.3) | collective-permute-done | bytes 172064 | tf_op jit(solution)/shard_map/ppermute | solution.py:30
  14.3 5.2 %collective-permute-start.4 = (bf16[24,3584]{1,0:T(8,128)(2,1)S(1)}, bf16[24,3584]{1,0:T(8,128)(2,1)S(1)}, u32[]{:S(2)}, u32[]{:S(2)}) collective-permute-start(bf16[24,3584]{1,0:T(8,128)(2,1)S(1)} %add_convert_fusion.1), channel_id=1, source_target_pairs={{0,192},{1,65},{2,194},{3,67},{4,196},{5,69},{6,198},{7,71},{8,200... | collective-permute-start | bytes 516104 | tf_op jit(solution)/shard_map/ppermute | solution.py:30
  19.6 0.0 collective-permute-done.9
  19.6 7.6 %collective-permute-start.10 = (bf16[24,1792]{1,0:T(8,128)(2,1)S(1)}, bf16[24,1792]{1,0:T(8,128)(2,1)S(1)}, u32[]{:S(2)}, u32[]{:S(2)}) collective-permute-start(bf16[24,1792]{1,0:T(8,128)(2,1)S(1)} %fusion.1), channel_id=1, source_target_pairs={{0,192},{1,65},{2,194},{3,67},{4,196},{5,69},{6,198},{7,71},{8,200... | collective-permute-start | bytes 258056 | tf_op jit(solution)/shard_map/ppermute | solution.py:30
  27.3 0.0 collective-permute-done.1
  27.3 1.9 %collective-permute-start.2 = (bf16[24,1792]{1,0:T(8,128)(2,1)S(1)}, bf16[24,1792]{1,0:T(8,128)(2,1)S(1)}, u32[]{:S(2)}, u32[]{:S(2)}) collective-permute-start(bf16[24,1792]{1,0:T(8,128)(2,1)S(1)} %fusion.4), channel_id=1, source_target_pairs={{0,192},{1,65},{2,194},{3,67},{4,196},{5,69},{6,198},{7,71},{8,200... | collective-permute-start | bytes 258056 | tf_op jit(solution)/shard_map/ppermute | solution.py:30
  29.2 0.7 %collective-permute-done.10 = bf16[24,1792]{1,0:T(8,128)(2,1)S(1)} collective-permute-done((bf16[24,1792]{1,0:T(8,128)(2,1)S(1)}, bf16[24,1792]{1,0:T(8,128)(2,1)S(1)}, u32[]{:S(2)}, u32[]{:S(2)}) %collective-permute-start.10) | collective-permute-done | bytes 86048 | tf_op jit(solution)/shard_map/ppermute | solution.py:30
  29.9 1.2 %collective-permute-start.11 = (bf16[24,1792]{1,0:T(8,128)(2,1)S(1)}, bf16[24,1792]{1,0:T(8,128)(2,1)S(1)}, u32[]{:S(2)}, u32[]{:S(2)}) collective-permute-start(bf16[24,1792]{1,0:T(8,128)(2,1)S(1)} %add_convert_fusion.2.own), channel_id=1, source_target_pairs={{0,64},{1,193},{2,66},{3,195},{4,68},{5,197},{6,70},{7,199},{8,72}... | collective-permute-start | bytes 258056 | tf_op jit(solution)/shard_map/ppermute | solution.py:30
  31.0 0.0 collective-permute-done.4
  31.1 1.9 %collective-permute-start.7 = (bf16[24,3584]{1,0:T(8,128)(2,1)S(1)}, bf16[24,3584]{1,0:T(8,128)(2,1)S(1)}, u32[]{:S(2)}, u32[]{:S(2)}) collective-permute-start(bf16[24,3584]{1,0:T(8,128)(2,1)S(1)} %add_convert_fusion.own), channel_id=1, source_target_pairs={{0,64},{1,193},{2,66},{3,195},{4,68},{5,197},{6,70},{7,199},{8,72}... | collective-permute-start | bytes 516104 | tf_op jit(solution)/shard_map/ppermute | solution.py:30
  33.0 3.2 %collective-permute-done.2 = bf16[24,1792]{1,0:T(8,128)(2,1)S(1)} collective-permute-done((bf16[24,1792]{1,0:T(8,128)(2,1)S(1)}, bf16[24,1792]{1,0:T(8,128)(2,1)S(1)}, u32[]{:S(2)}, u32[]{:S(2)}) %collective-permute-start.2) | collective-permute-done | bytes 86048 | tf_op jit(solution)/shard_map/ppermute | solution.py:30
  36.2 2.9 %collective-permute-start.5 = (bf16[24,1792]{1,0:T(8,128)(2,1)S(1)}, bf16[24,1792]{1,0:T(8,128)(2,1)S(1)}, u32[]{:S(2)}, u32[]{:S(2)}) collective-permute-start(bf16[24,1792]{1,0:T(8,128)(2,1)S(1)} %add_convert_fusion.3.own), channel_id=1, source_target_pairs={{0,64},{1,193},{2,66},{3,195},{4,68},{5,197},{6,70},{7,199},{8,72}... | collective-permute-start | bytes 258056 | tf_op jit(solution)/shard_map/ppermute | solution.py:30
  39.1 0.0 collective-permute-done.11.recv
  39.1 0.1 collective-permute-start.12
  39.2 2.5 %collective-permute-done.5.recv = bf16[24,1792]{1,0:T(8,128)(2,1)S(1)} collective-permute-done((bf16[24,1792]{1,0:T(8,128)(2,1)S(1)}, bf16[24,1792]{1,0:T(8,128)(2,1)S(1)}, u32[]{:S(2)}, u32[]{:S(2)}) %collective-permute-start.5) | collective-permute-done | bytes 86048 | tf_op jit(solution)/shard_map/ppermute | solution.py:30
  41.7 0.1 collective-permute-start.6
  41.8 0.0 collective-permute-done.7.recv
  41.8 0.0 copy-done
  41.8 0.0 copy-done.1
  41.8 1.4 %shard_map.87 = (f32[72,7168]{1,0:T(8,128)}, f32[72,7168]{1,0:T(8,128)}, bf16[24,7168]{1,0:T(8,128)(2,1)S(1)}, f32[24,128]{1,0:T(8,128)S(1)}) custom-call(bf16[24,3584]{1,0:T(8,128)(2,1)S(1)} %add_convert_fusion.own, bf16[24,3584]{1,0:T(8,128)(2,1)S(1)} %collective-permute-done.7.recv, f32[72,128]{1,0:T(8,128)S(1)} %get-tuple-element.38.live, ...), custom_call_target="tpu_custom_call" | custom-call | flops 25165824 | bytes 25165824 | tf_op jit(solution)/shard_map/pallas_call | solution.py:59
  43.3 2.9 %collective-permute-done.12 = bf16[2,24,1792]{2,1,0:T(8,128)(2,1)S(1)} collective-permute-done((bf16[2,24,1792]{2,1,0:T(8,128)(2,1)S(1)}, bf16[2,24,1792]{2,1,0:T(8,128)(2,1)S(1)}, u32[]{:S(2)}, u32[]{:S(2)}) %collective-permute-start.12) | collective-permute-done | bytes 172064 | tf_op jit(solution)/shard_map/ppermute | solution.py:45
  46.2 1.5 %shard_map.88 = (f32[72,7168]{1,0:T(8,128)}, f32[72,7168]{1,0:T(8,128)}, bf16[24,7168]{1,0:T(8,128)(2,1)S(1)}, f32[24,128]{1,0:T(8,128)S(1)}) custom-call(bf16[24,1792]{1,0:T(8,128)(2,1)S(1)} %add_convert_fusion.2.own, bf16[24,1792]{1,0:T(8,128)(2,1)S(1)} %collective-permute-done.11.recv, ...), custom_call_target="tpu_custom_call", output_to_operand_aliasing={{0}: (6, {}), {1}: (7, {})} | custom-call | flops 4194304 | bytes 4194304 | tf_op jit(solution)/shard_map/pallas_call | solution.py:59
  47.7 0.0 collective-permute-done.6.other
  47.7 1.8 %shard_map.89 = (f32[72,7168]{1,0:T(8,128)}, f32[72,7168]{1,0:T(8,128)}, bf16[72,7168]{1,0:T(8,128)(2,1)}, f32[56,72]{1,0:T(8,128)}) custom-call(bf16[24,1792]{1,0:T(8,128)(2,1)S(1)} %add_convert_fusion.3.own, bf16[24,1792]{1,0:T(8,128)(2,1)S(1)} %collective-permute-done.5.recv, ...), custom_call_target="tpu_custom_call", output_to_operand_aliasing={{0}: (10, {}), {1}: (11, {})} | custom-call | flops 4194304 | bytes 4194304 | tf_op jit(solution)/shard_map/pallas_call | solution.py:59
  (12 shorter events, 0.3 us)
Async XLA Ops:
  2.0 7.9 %collective-permute-start.8 = (bf16[2,24,1792]{2,1,0:T(8,128)(2,1)S(1)}, bf16[2,24,1792]{2,1,0:T(8,128)(2,1)S(1)}, u32[]{:S(2)}, u32[]{:S(2)}) collective-permute-start(bf16[2,24,1792]{2,1,0:T(8,128)(2,1)S(1)} %get-tuple-element.42), channel_id=1, source_target_pairs={{0,64},{1,2},{2,1},{3,4},{4,3},{5,6},{6,5},{7,8},{8,7},{9,10},{10,... | collective-permute-start | bytes 516104 | tf_op jit(solution)/shard_map/ppermute | solution.py:45
  4.5 8.0 %collective-permute-start = (bf16[2,24,1792]{2,1,0:T(8,128)(2,1)S(1)}, bf16[2,24,1792]{2,1,0:T(8,128)(2,1)S(1)}, u32[]{:S(2)}, u32[]{:S(2)}) collective-permute-start(bf16[2,24,1792]{2,1,0:T(8,128)(2,1)S(1)} %get-tuple-element.32), channel_id=1, source_target_pairs={{0,1},{1,0},{2,3},{3,2},{4,5},{5,4},{6,7},{7,6},{8,9},{9,8},{10,11... | collective-permute-start | bytes 516104 | tf_op jit(solution)/shard_map/ppermute | solution.py:34
  4.6 9.7 %collective-permute-start.3 = (bf16[24,3584]{1,0:T(8,128)(2,1)S(1)}, bf16[24,3584]{1,0:T(8,128)(2,1)S(1)}, u32[]{:S(2)}, u32[]{:S(2)}) collective-permute-start(bf16[24,3584]{1,0:T(8,128)(2,1)S(1)} %get-tuple-element.34), channel_id=1, source_target_pairs={{0,64},{1,193},{2,66},{3,195},{4,68},{5,197},{6,70},{7,199},{8,72}... | collective-permute-start | bytes 516104 | tf_op jit(solution)/shard_map/ppermute | solution.py:30
  8.5 33.3 %copy-start = (f32[72,7168]{1,0:T(8,128)S(1)}, f32[72,7168]{1,0:T(8,128)}, u32[]{:S(2)}) copy-start(f32[72,7168]{1,0:T(8,128)} %params.5) | copy-start | bytes 6193156
  8.5 33.3 %copy-start.1 = (f32[72,7168]{1,0:T(8,128)S(1)}, f32[72,7168]{1,0:T(8,128)}, u32[]{:S(2)}) copy-start(f32[72,7168]{1,0:T(8,128)} %momentum.5) | copy-start | bytes 6193156
  10.0 9.6 %collective-permute-start.9 = (bf16[24,1792]{1,0:T(8,128)(2,1)S(1)}, bf16[24,1792]{1,0:T(8,128)(2,1)S(1)}, u32[]{:S(2)}, u32[]{:S(2)}) collective-permute-start(bf16[24,1792]{1,0:T(8,128)(2,1)S(1)} %fusion.2), channel_id=1, source_target_pairs={{0,64},{1,193},{2,66},{3,195},{4,68},{5,197},{6,70},{7,199},{8,72}... | collective-permute-start | bytes 258056 | tf_op jit(solution)/shard_map/ppermute | solution.py:30
  12.5 14.8 %collective-permute-start.1 = (bf16[24,1792]{1,0:T(8,128)(2,1)S(1)}, bf16[24,1792]{1,0:T(8,128)(2,1)S(1)}, u32[]{:S(2)}, u32[]{:S(2)}) collective-permute-start(bf16[24,1792]{1,0:T(8,128)(2,1)S(1)} %fusion.5), channel_id=1, source_target_pairs={{0,64},{1,193},{2,66},{3,195},{4,68},{5,197},{6,70},{7,199},{8,72}... | collective-permute-start | bytes 258056 | tf_op jit(solution)/shard_map/ppermute | solution.py:30
  14.3 16.7 %collective-permute-start.4 = (bf16[24,3584]{1,0:T(8,128)(2,1)S(1)}, bf16[24,3584]{1,0:T(8,128)(2,1)S(1)}, u32[]{:S(2)}, u32[]{:S(2)}) collective-permute-start(bf16[24,3584]{1,0:T(8,128)(2,1)S(1)} %add_convert_fusion.1), channel_id=1, source_target_pairs={{0,192},{1,65},{2,194},{3,67},{4,196},{5,69},{6,198},{7,71},{8,200... | collective-permute-start | bytes 516104 | tf_op jit(solution)/shard_map/ppermute | solution.py:30
  19.6 10.2 %collective-permute-start.10 = (bf16[24,1792]{1,0:T(8,128)(2,1)S(1)}, bf16[24,1792]{1,0:T(8,128)(2,1)S(1)}, u32[]{:S(2)}, u32[]{:S(2)}) collective-permute-start(bf16[24,1792]{1,0:T(8,128)(2,1)S(1)} %fusion.1), channel_id=1, source_target_pairs={{0,192},{1,65},{2,194},{3,67},{4,196},{5,69},{6,198},{7,71},{8,200... | collective-permute-start | bytes 258056 | tf_op jit(solution)/shard_map/ppermute | solution.py:30
  27.3 8.9 %collective-permute-start.2 = (bf16[24,1792]{1,0:T(8,128)(2,1)S(1)}, bf16[24,1792]{1,0:T(8,128)(2,1)S(1)}, u32[]{:S(2)}, u32[]{:S(2)}) collective-permute-start(bf16[24,1792]{1,0:T(8,128)(2,1)S(1)} %fusion.4), channel_id=1, source_target_pairs={{0,192},{1,65},{2,194},{3,67},{4,196},{5,69},{6,198},{7,71},{8,200... | collective-permute-start | bytes 258056 | tf_op jit(solution)/shard_map/ppermute | solution.py:30
  29.9 9.2 %collective-permute-start.11 = (bf16[24,1792]{1,0:T(8,128)(2,1)S(1)}, bf16[24,1792]{1,0:T(8,128)(2,1)S(1)}, u32[]{:S(2)}, u32[]{:S(2)}) collective-permute-start(bf16[24,1792]{1,0:T(8,128)(2,1)S(1)} %add_convert_fusion.2.own), channel_id=1, source_target_pairs={{0,64},{1,193},{2,66},{3,195},{4,68},{5,197},{6,70},{7,199},{8,72}... | collective-permute-start | bytes 258056 | tf_op jit(solution)/shard_map/ppermute | solution.py:30
  31.1 10.7 %collective-permute-start.7 = (bf16[24,3584]{1,0:T(8,128)(2,1)S(1)}, bf16[24,3584]{1,0:T(8,128)(2,1)S(1)}, u32[]{:S(2)}, u32[]{:S(2)}) collective-permute-start(bf16[24,3584]{1,0:T(8,128)(2,1)S(1)} %add_convert_fusion.own), channel_id=1, source_target_pairs={{0,64},{1,193},{2,66},{3,195},{4,68},{5,197},{6,70},{7,199},{8,72}... | collective-permute-start | bytes 516104 | tf_op jit(solution)/shard_map/ppermute | solution.py:30
  36.2 5.5 %collective-permute-start.5 = (bf16[24,1792]{1,0:T(8,128)(2,1)S(1)}, bf16[24,1792]{1,0:T(8,128)(2,1)S(1)}, u32[]{:S(2)}, u32[]{:S(2)}) collective-permute-start(bf16[24,1792]{1,0:T(8,128)(2,1)S(1)} %add_convert_fusion.3.own), channel_id=1, source_target_pairs={{0,64},{1,193},{2,66},{3,195},{4,68},{5,197},{6,70},{7,199},{8,72}... | collective-permute-start | bytes 258056 | tf_op jit(solution)/shard_map/ppermute | solution.py:30
  39.1 7.0 %collective-permute-start.12 = (bf16[2,24,1792]{2,1,0:T(8,128)(2,1)S(1)}, bf16[2,24,1792]{2,1,0:T(8,128)(2,1)S(1)}, u32[]{:S(2)}, u32[]{:S(2)}) collective-permute-start(bf16[2,24,1792]{2,1,0:T(8,128)(2,1)S(1)} %pad_maximum_fusion.1), channel_id=1, source_target_pairs={{0,64},{1,2},{2,1},{3,4},{4,3},{5,6},{6,5},{7,8},{8,7},{9,10},{10,... | collective-permute-start | bytes 516104 | tf_op jit(solution)/shard_map/ppermute | solution.py:45
  41.7 6.0 %collective-permute-start.6 = (bf16[2,24,1792]{2,1,0:T(8,128)(2,1)S(1)}, bf16[2,24,1792]{2,1,0:T(8,128)(2,1)S(1)}, u32[]{:S(2)}, u32[]{:S(2)}) collective-permute-start(bf16[2,24,1792]{2,1,0:T(8,128)(2,1)S(1)} %pad_maximum_fusion), channel_id=1, source_target_pairs={{0,1},{1,0},{2,3},{3,2},{4,5},{5,4},{6,7},{7,6},{8,9},{9,8},{10,11... | collective-permute-start | bytes 516104 | tf_op jit(solution)/shard_map/ppermute | solution.py:34
